TPU v7x, 128 devices: a whole 4x4x4 slice. The times are simulated.
128 devices in a mesh: dp: 16 (over z_hi, y, core), seq: 8 (over z_lo, x).
Axes of the slice: x: 4, y: 4, z: 4 (z_hi: 2, z_lo: 2; z = z_hi * 2 + z_lo), core: 2. Of those that a mesh axis runs over, the one named last changes fastest.
Arguments:
- sequence: bfloat16 [16, 2048, 1408], P('dp', 'seq'), may hold values from -6 to 6
- conv_weight: bfloat16 [1408, 5, 1536], P(('dp', 'seq')), may hold values from -0.0625 to 0.0625
- conv_bias: float32 [1536], replicated, may hold values from -3 to 3
- norm_gain: float32 [1536], replicated, may hold values from 0.25 to 1.75
- proj_weight: bfloat16 [1536, 3, 1536], P('dp', None, 'seq'), may hold values from -0.66340347 to 0.66340347
- out_weight: bfloat16 [1536, 1536], P('seq', 'dp'), may hold values from -0.15625 to 0.15625
- cotangent: bfloat16 [16, 1024, 1536], P('dp', 'seq'), may hold values from -6 to 6
Outputs:
- block_out: bfloat16 [16, 1024, 1536], P('dp', 'seq')
- proj_grad: float32 [1536, 3, 1536], P('dp')
- out_grad: float32 [1536, 1536], P('seq')
All inputs are finite; a program needn't handle non-finite values.
Results may differ from a plain program's by a relative error of at most 0.0065.
Values may be sent and summed in bfloat16 or wider, within the bound.
No kernel may reach another device: no remote copies, remote signals or barrier semaphores. Data moves between devices by JAX's collectives and lax.ppermute only.
A program may use at most 192 MiB of HBM per device.

v0:
```python
import jax
import jax.numpy as jnp
from jax import lax
from jax.sharding import PartitionSpec as P

HD = 192


epsilon = 1e-06


def with_halo(block, sides, width):
    for axis, dim in sides:
        count = lax.axis_size(axis)
        forward = [(i, i + 1) for i in range(count - 1)]
        backward = [(target, source) for source, target in forward]
        low = lax.ppermute(
            lax.slice_in_dim(block, block.shape[dim] - width, None, axis=dim), axis, forward
        )
        high = lax.ppermute(lax.slice_in_dim(block, 0, width, axis=dim), axis, backward)
        block = jnp.concatenate([low, block, high], axis=dim)
    return block


def convolve(padded, filters, positions):
    running = jnp.zeros((positions, filters.shape[2]), jnp.float32)
    for offset in range(filters.shape[1]):
        running = running + jnp.dot(
            padded[offset : offset + positions],
            filters[:, offset, :],
            preferred_element_type=jnp.float32,
        )
    return running


def pool_pairs(conv_sum, conv_bias):
    activated = jax.nn.gelu(conv_sum + conv_bias)
    return jnp.max(activated.reshape(-1, 2, activated.shape[1]), axis=1).astype(jnp.bfloat16)


def normalize(features, norm_gain):
    widened = features.astype(jnp.float32)
    square_mean = jnp.mean(widened * widened, axis=-1, keepdims=True)
    return (widened * lax.rsqrt(square_mean + epsilon) * norm_gain).astype(jnp.bfloat16)


def per_device(sequence, conv_weight, conv_bias, norm_gain, proj_weight, out_weight, cotangent):
    positions = sequence.shape[1]
    conv_reach = conv_weight.shape[1] // 2
    padded = with_halo(sequence, (("seq", 1),), conv_reach)[0]
    filters = lax.all_gather(conv_weight, ("dp", "seq"), axis=0, tiled=True)
    conv_sum = convolve(padded, filters, positions)
    features_local = pool_pairs(conv_sum, conv_bias)
    normed = lax.all_gather(normalize(features_local, norm_gain), "seq", axis=0, tiled=True)
    length = normed.shape[0]
    local_cols = proj_weight.shape[2]
    window = normed
    projected = jnp.einsum(
        "sr,rtc->stc",
        window,
        lax.all_gather(proj_weight, "dp", axis=0, tiled=True),
        preferred_element_type=jnp.float32,
    )
    query = projected[:, 0].astype(jnp.bfloat16).reshape(length, -1, HD)
    key_rows = projected[:, 1].astype(jnp.bfloat16).reshape(length, -1, HD)
    values = projected[:, 2].astype(jnp.bfloat16).reshape(length, -1, HD)
    inv_scale = HD ** (-0.5)
    block_rows = 512
    saved_weights = []
    mixed_parts = []
    for block_start in range(0, length, block_rows):
        q_block = query[block_start : block_start + block_rows]
        scores = (
            jnp.einsum("qhd,khd->hqk", q_block, key_rows, preferred_element_type=jnp.float32)
            * inv_scale
        )
        row_top = jnp.max(scores, axis=-1, keepdims=True)
        exponent = jnp.exp(scores - row_top)
        weights = exponent / jnp.sum(exponent, axis=-1, keepdims=True)
        weights_low = weights.astype(jnp.bfloat16)
        saved_weights.append((weights, weights_low))
        mixed_parts.append(
            jnp.einsum(
                "hqk,khd->qhd", weights_low, values, preferred_element_type=jnp.float32
            ).astype(jnp.bfloat16)
        )
    mixed = jnp.concatenate(mixed_parts, axis=0).reshape(length, local_cols)
    out_full = lax.all_gather(out_weight, "dp", axis=1, tiled=True)
    attended = lax.psum_scatter(
        jnp.dot(mixed, out_full, preferred_element_type=jnp.float32),
        "seq",
        scatter_dimension=0,
        tiled=True,
    )
    block_out = (features_local.astype(jnp.float32) + attended).astype(jnp.bfloat16)[None]
    shard_rows = lax.all_gather(cotangent[0], "seq", axis=0, tiled=True)
    window = mixed
    grad_running = lax.dot_general(
        window, shard_rows, (((0,), (0,)), ((), ())), preferred_element_type=jnp.float32
    )
    back_rows = lax.dot_general(
        shard_rows, out_full, (((1,), (1,)), ((), ())), preferred_element_type=jnp.float32
    )
    out_grad = lax.psum(grad_running, "dp")
    d_mixed = back_rows.astype(jnp.bfloat16).reshape(length, -1, HD)
    key_running = jnp.zeros(key_rows.shape, jnp.float32)
    value_running = jnp.zeros(values.shape, jnp.float32)
    query_parts = []
    for block_index, block_start in enumerate(range(0, length, block_rows)):
        weights, weights_low = saved_weights[block_index]
        d_block = d_mixed[block_start : block_start + block_rows]
        q_block = query[block_start : block_start + block_rows]
        value_running = value_running + jnp.einsum(
            "hqk,qhd->khd", weights_low, d_block, preferred_element_type=jnp.float32
        )
        d_weights = jnp.einsum("qhd,khd->hqk", d_block, values, preferred_element_type=jnp.float32)
        centre = jnp.sum(weights * d_weights, axis=-1, keepdims=True)
        d_scores = (weights * (d_weights - centre) * inv_scale).astype(jnp.bfloat16)
        query_parts.append(
            jnp.einsum(
                "hqk,khd->qhd", d_scores, key_rows, preferred_element_type=jnp.float32
            ).astype(jnp.bfloat16)
        )
        key_running = key_running + jnp.einsum(
            "hqk,qhd->khd", d_scores, q_block, preferred_element_type=jnp.float32
        )
    d_query = jnp.concatenate(query_parts, axis=0).reshape(length, local_cols)
    d_key = key_running.astype(jnp.bfloat16).reshape(length, local_cols)
    d_value = value_running.astype(jnp.bfloat16).reshape(length, local_cols)
    d_proj = jnp.stack([d_query, d_key, d_value], axis=1)
    proj_part = jnp.einsum("sr,stc->rtc", normed, d_proj, preferred_element_type=jnp.float32)
    proj_rows_sum = lax.psum_scatter(proj_part, "dp", scatter_dimension=0, tiled=True)
    proj_grad = lax.all_gather(proj_rows_sum, "seq", axis=2, tiled=True)
    return (block_out, proj_grad, out_grad)


def solution(mesh):
    in_specs = (
        P("dp", "seq", None),
        P(("dp", "seq"), None, None),
        P(),
        P(),
        P("dp", None, "seq"),
        P("seq", "dp"),
        P("dp", "seq", None),
    )
    out_specs = (P("dp", "seq", None), P("dp", None, None), P("seq", None))
    return jax.shard_map(
        per_device, mesh=mesh, in_specs=in_specs, out_specs=out_specs, check_vma=False
    )
```

profile of v0, /device:TPU:1, one launch (start us, length us, event | category | flops | bytes accessed | tf_op | source)
XLA Modules:
  0.0 889.9 jit_solution(5812078844590261302)
XLA Ops:
  7.2 1.8 copy.19
  9.1 0.0 all-gather.11.cloned.1.call-start
  9.1 1.7 copy.25
  10.9 0.8 fusion.80
  11.7 3.9 collective-permute-start
  15.6 1.3 collective-permute-start.1
  17.0 0.0 all-gather.9.cloned.1.call-start
  17.0 0.9 constant_dynamic-update-slice_fusion.1
  17.9 2.1 collective-permute-done.1
  20.0 0.6 constant_dynamic-update-slice_fusion
  20.6 343.0 %all-gather.7.cloned.1.call-done = bf16[1408,5,1536]{2,1,0:T(8,128)(2,1)} async-done(((bf16[11,5,1536]{2,1,0:T(8,128)(2,1)}), bf16[1408,5,1536]{2,1,0:T(8,128)(2,1)}) %all-gather.7.cloned.1.call-update) | async-done | bytes 21626896 | tf_op jit(solution)/shard_map/all_gather | solution.py:51
  363.6 90.8 %fusion.79 = (bf16[1408,1,1536]{2,1,0:T(2,128)(2,1)S(1)}, bf16[1408,1,1536]{2,1,0:T(2,128)(2,1)}, bf16[1408,1,1536]{2,1,0:T(2,128)(2,1)}, bf16[1408,1,1536]{2,1,0:T(2,128)(2,1)S(1)}, bf16[1408,1,1536]{2,1,0:T(2,128)(2,1)S(1)}) fusion(bf16[1408,5,1536]{2,1,0:T(8,128)(2,1)} %all-gather.7.cloned.1.call-done), kind=kLoop, calls=%fused_computation.109 | loop fusion | bytes 43253760 | tf_op jit(solution)/shard_map/slice | solution.py:30
  454.4 5.1 fusion.3
  459.5 0.9 copy-done.3
  460.4 1.4 fusion.2
  461.8 2.5 fusion
  464.3 1.4 fusion.15
  465.7 3.0 fusion.26
  468.8 0.3 reshape.158
  469.1 2.1 reduce_max.27
  471.3 0.2 fusion.45
  471.4 0.9 fusion.47
  472.4 0.0 reduce-scatter.5.cloned.1.call-start
  472.5 0.1 copy.27
  472.6 28.3 %all_gather.21 = bf16[192,1536]{0,1:T(8,128)(2,1)S(1)} all-gather(bf16[192,96]{0,1:T(8,128)(2,1)S(1)} %copy.27), channel_id=1, replica_groups=mesh['dp'=16,'seq'=8] {'dp'}, dimensions={1}, use_global_device_ids=true | all-gather | bytes 626688 | tf_op jit(solution)/shard_map/all_gather | solution.py:88
  500.9 4.5 copy.26
  505.4 3.9 fusion.29
  509.3 8.1 all-gather.9.cloned.1.call-done
  517.4 3.9 fusion.81
  521.3 0.2 convert.5
  521.5 0.6 multiply_reduce_fusion.3
  522.1 0.6 multiply_reduce_fusion.2
  522.6 0.5 fusion.17
  523.2 0.8 multiply_reduce_fusion.1
  524.0 0.4 multiply_convert_fusion.1
  524.4 0.5 fusion.43
  524.9 0.4 fusion.67
  525.3 0.4 fusion.58
  525.6 0.5 fusion.19
  526.2 0.8 multiply_reduce_fusion
  527.0 0.3 multiply_convert_fusion
  527.3 0.5 fusion.44
  527.8 0.4 fusion.33
  528.2 0.1 copy-done
  528.3 0.4 fusion.32
  528.7 1.5 copy-done.13
  530.2 4.3 fusion.9
  534.6 0.0 all-gather.13.cloned.1.call-start
  534.6 81.8 %reduce-scatter.5.cloned.1.call-done = f32[96,3,192]{2,0,1:T(8,128)} async-done(((f32[1536,3,192]{2,0,1:T(8,128)}), f32[96,3,192]{2,0,1:T(8,128)}) %reduce-scatter.5.cloned.1.call-update) | async-done | bytes 221200 | tf_op jit(solution)/shard_map/reduce_scatter | solution.py:132
  616.4 1.9 copy.29
  618.3 0.0 reduce-scatter.3.cloned.1.call-start
  618.4 0.5 fusion.41
  618.9 1.1 copy-done.1
  619.9 0.5 fusion.42
  620.5 3.7 fusion.62
  624.2 0.0 all-reduce.2.cloned.1.call-start
  624.2 1.8 copy-done.2
  626.1 2.7 fusion.5
  628.8 31.2 %all-gather.13.cloned.1.call-done = f32[96,3,1536]{0,1,2:T(4,128)} async-done(((f32[96,3,192]{0,1,2:T(4,128)}), f32[96,3,1536]{0,1,2:T(4,128)}) %all-gather.13.cloned.1.call-update) | async-done | bytes 1769488 | tf_op jit(solution)/shard_map/all_gather | solution.py:133
  660.0 4.2 copy.30
  664.2 73.6 %reduce-scatter.3.cloned.1.call-done = f32[128,1536]{1,0:T(8,128)} async-done(((f32[1024,1536]{1,0:T(8,128)}), f32[128,1536]{1,0:T(8,128)}) %reduce-scatter.3.cloned.1.call-update) | async-done | bytes 786448 | tf_op jit(solution)/shard_map/reduce_scatter | solution.py:89
  737.8 1.9 fusion.61
  739.8 140.9 %all-reduce.2.cloned.1.call-done = f32[192,1536]{1,0:T(8,128)} async-done(((f32[192,1536]{1,0:T(8,128)}), f32[192,1536]{1,0:T(8,128)}) %all-reduce.2.cloned.1.call-update) | async-done | bytes 1179664 | tf_op jit(solution)/shard_map/psum | solution.py:104
  880.7 2.4 copy.62
  (39 shorter events, 0.3 us)
Async XLA Ops:
  7.2 9.8 %copy-start.10 = (bf16[1,256,1408]{2,1,0:T(8,128)(2,1)S(1)}, bf16[1,256,1408]{2,1,0:T(8,128)(2,1)}, u32[]{:S(2)}) copy-start(bf16[1,256,1408]{2,1,0:T(8,128)(2,1)} %param.7) | copy-start | bytes 2162692
  7.2 356.4 %all-gather.7.cloned.1.call-start = ((), (), s32[]{:S(2)}) async-start(), calls=%async_computation.2 | async-start | bytes 34873344 | tf_op jit(solution)/shard_map/all_gather | solution.py:51
  9.1 491.8 %all-gather.11.cloned.1.call-start = ((), (), s32[]{:S(2)}) async-start(), calls=%async_computation.4 | async-start | bytes 3342336 | tf_op jit(solution)/shard_map/all_gather | solution.py:61
  10.9 494.6 %all-gather.15.cloned.1.call-start = ((), (), s32[]{:S(2)}) async-start(), calls=%async_computation.9 | async-start | bytes 3538944 | tf_op jit(solution)/shard_map/all_gather | solution.py:96
  11.7 442.7 %collective-permute-start = (bf16[1,2,1408]{2,1,0:T(2,128)(2,1)S(1)}, bf16[1,2,1408]{2,1,0:T(2,128)(2,1)S(1)}, u32[]{:S(2)}, u32[]{:S(2)}) collective-permute-start(bf16[1,2,1408]{2,1,0:T(2,128)(2,1)S(1)} %get-tuple-element.18), channel_id=1, source_target_pairs={{0,1},{1,2},{2,3},{3,4},{4,5},{5,6},{6,7},{8,9},{9,10},{10,11},{11... | collective-permute-start | bytes 16904 | tf_op jit(solution)/shard_map/ppermute | solution.py:17
  15.6 4.4 collective-permute-start.1
  17.0 500.5 %all-gather.9.cloned.1.call-start = ((), (), s32[]{:S(2)}) async-start(), calls=%async_computation.3 | async-start | bytes 3538944 | tf_op jit(solution)/shard_map/all_gather | solution.py:54
  454.4 6.0 copy-start.3
  464.3 1.4 copy-start.14
  468.8 2.7 copy-start.12
  468.8 3.6 copy-start.11
  471.3 1.2 copy-start.6
  472.4 144.0 %reduce-scatter.5.cloned.1.call-start = ((), (), s32[]{:S(2)}) async-start(), calls=%async_computation.6 | async-start | bytes 5013504 | tf_op jit(solution)/shard_map/reduce_scatter | solution.py:132
  500.9 4.5 copy-start.4
  522.1 1.1 copy-start.9
  527.0 1.3 copy-start
  528.3 1.9 copy-start.13
  534.6 125.4 %all-gather.13.cloned.1.call-start = ((), (), s32[]{:S(2)}) async-start(), calls=%async_computation.7 | async-start | bytes 3538944 | tf_op jit(solution)/shard_map/all_gather | solution.py:133
  618.3 119.5 %reduce-scatter.3.cloned.1.call-start = ((), (), s32[]{:S(2)}) async-start(), calls=%async_computation.5 | async-start | bytes 7077888 | tf_op jit(solution)/shard_map/reduce_scatter | solution.py:89
  618.4 1.6 copy-start.1
  618.4 2.1 copy-start.5
  620.5 3.7 copy-start.8
  624.2 1.9 copy-start.2
  624.2 256.5 %all-reduce.2.cloned.1.call-start = ((), (), s32[]{:S(2)}) async-start(), calls=%async_computation.8 | async-start | bytes 2359296 | tf_op jit(solution)/shard_map/psum | solution.py:104
  628.8 109.0 %copy-start.7 = (bf16[128,1536]{1,0:T(8,128)(2,1)S(1)}, bf16[128,1536]{1,0:T(8,128)(2,1)}, u32[]{:S(2)}) copy-start(bf16[128,1536]{1,0:T(8,128)(2,1)} %copy-done.6) | copy-start | bytes 1179652
Sparse Core Ops, SparseCore 0:
  10.3 353.2 all-gather.6
  366.6 53.2 all-gather.10
  421.5 39.7 all-gather.14
  472.5 44.8 all-gather.8
  534.7 81.6 reduce-scatter.4
  618.6 41.3 all-gather.12
  662.5 75.2 reduce-scatter.2
  741.1 139.5 all-reduce.1
where the time goes:
time: 891 us; the launch traced here: 890 us
  waiting for transfers between devices  681 us (76%)
  local copies, waits for them, and re-layouts  115 us (13%)
  matrix products  38.2 us (4%)
  blocking collectives  28.3 us (3%)
  between operations  14.5 us (2%)
    all_gather x1, waiting for transfers between devices, per_device(): filters = lax.all_gather(conv_weight, ('dp', 'seq'), axis=0, tiled=True)  343 us
    psum x1, waiting for transfers between devices, per_device(): out_grad = lax.psum(grad_running, 'dp')  141 us
    slice x1, local copies, waits for them, and re-layouts, convolve(): filters[:, offset, :]  90.8 us
    reduce_scatter x1, waiting for transfers between devices, per_device(): lax.psum_scatter(proj_part, 'dp', scatter_dimension=0, tiled=True)  81.8 us
    reduce_scatter x1, waiting for transfers between devices, per_device(): lax.psum_scatter(jnp.dot(mixed, out_full, preferred_element_type=jnp.floa...  73.6 us
    all_gather x1, waiting for transfers between devices, per_device(): proj_grad = lax.all_gather(proj_rows_sum, 'seq', axis=2, tiled=True)  31.2 us
    all_gather x1, blocking collectives, per_device(): out_full = lax.all_gather(out_weight, 'dp', axis=1, tiled=True)  28.3 us
  transfers between devices with their start and end apart: 10, of which 7 were waited for; matrix products, arithmetic and copies ran while one was open for 15% of the time, Pallas kernels for 0%

commit v1 on v0

v1 whole, which is shorter than its diff:
```python
import jax
import jax.numpy as jnp
import numpy as np
from jax import lax
from jax.experimental import pallas as pl
from jax.experimental.pallas import tpu as pltpu
from jax.sharding import Mesh, PartitionSpec as P

HD = 192
D = 1536
NX = 4
CIN = 1408
GROUP = 44
SLOT = 48
PLANE = 32
KPAD = PLANE * SLOT
OUTC = D // NX
KW = 5
EPS = 1e-06
HALO = 16

bf16 = jnp.bfloat16
f32 = jnp.float32


def ring(n, k):
    return [(i, (i + k) % n) for i in range(n)]


def staged_ring(block, axis, cut):
    low = lax.ppermute(block, axis, ring(4, 1))
    high = lax.ppermute(block, axis, ring(4, -1))
    far_a = lax.ppermute(lax.slice_in_dim(low, 0, cut), axis, ring(4, 1))
    far_b = lax.ppermute(lax.slice_in_dim(high, cut, None), axis, ring(4, -1))
    return low, high, far_a, far_b


def conv_kernel(zl_ref, x_ref, *refs):
    (w0, w1, w2, w3a, w3b, o0, o1, o2, o3a, o3b, bias_ref, out_ref, wcat, xs, *accs) = refs
    row = 0
    for ref in (w0, w1, w2, w3a, w3b, o0, o1, o2, o3a, o3b):
        for piece in range(ref.shape[0]):
            for off in range(KW):
                wcat[row : row + SLOT, off * OUTC : (off + 1) * OUTC] = ref[piece, off]
            row += SLOT
    lower = zl_ref[0] == 0
    zeros = jnp.zeros((HALO, KPAD), bf16)
    xs[0:HALO, :] = jnp.where(lower, zeros, x_ref[3, 256 : 256 + HALO, :])
    for b in range(4):
        xs[HALO + b * 256 : HALO + (b + 1) * 256, :] = x_ref[b, 0:256, :]
    xs[HALO + 1024 : 2 * HALO + 1024, :] = jnp.where(lower, x_ref[0, 256 : 256 + HALO, :], zeros)

    @pl.loop(0, 8)
    def _(r):
        base = pl.multiple_of(r * 128, 128)
        y = jnp.dot(xs[pl.ds(base, 128 + 2 * HALO), :], wcat[...], preferred_element_type=f32)
        total = bias_ref[...] + jnp.zeros((128, OUTC), f32)
        for off in range(KW):
            first = HALO + off - 2
            total = total + y[first : first + 128, off * OUTC : (off + 1) * OUTC]
        activated = jax.nn.gelu(total)
        for n, acc in enumerate(accs):
            acc[...] = activated[:, n * 128 : (n + 1) * 128]
            top = jnp.maximum(acc[pl.ds(0, 64, 2), :], acc[pl.ds(1, 64, 2), :])
            out_ref[pl.ds(pl.multiple_of(r * 64, 64), 64), n * 128 : (n + 1) * 128] = top.astype(bf16)


def conv_pool(zl, xblocks, pieces, bias):
    vmem = pl.BlockSpec(memory_space=pltpu.VMEM)
    return pl.pallas_call(
        conv_kernel,
        out_shape=jax.ShapeDtypeStruct((512, OUTC), bf16),
        in_specs=[pl.BlockSpec(memory_space=pltpu.SMEM)] + [vmem] * (len(pieces) + 2),
        out_specs=vmem,
        scratch_shapes=[
            pltpu.VMEM((KPAD, KW * OUTC), bf16),
            pltpu.VMEM((1024 + 2 * HALO, KPAD), bf16),
            *[pltpu.VMEM((128, 128), f32)] * 3,
        ],
        compiler_params=pltpu.CompilerParams(vmem_limit_bytes=48 * 1024 * 1024),
        cost_estimate=pl.CostEstimate(flops=6_000_000_000, bytes_accessed=9_000_000, transcendentals=400_000),
    )(zl, xblocks, *pieces, bias)


VMEM = pl.BlockSpec(memory_space=pltpu.VMEM)
SMEM = pl.BlockSpec(memory_space=pltpu.SMEM)
SCALE = HD ** (-0.5)
WIDE = 256
TOKENS = 1024
BLOCK = 256
NT = (((1,), (1,)), ((), ()))
TN = (((0,), (0,)), ((), ()))


def dot(a, b, dims=(((1,), (0,)), ((), ()))):
    return lax.dot_general(a, b, dims, preferred_element_type=f32)


def softmax_rows(q_block, keys):
    scores = dot(q_block, keys, NT) * SCALE
    exponent = jnp.exp(scores - jnp.max(scores, axis=-1, keepdims=True))
    return exponent * (1.0 / jnp.sum(exponent, axis=-1, keepdims=True))


def forward_kernel(feats_ref, gain_ref, w_ref, normed_ref, qkv_ref, mixed_ref, partial_ref, wq, wo):
    for t in range(3):
        wq[:, t * WIDE : t * WIDE + HD] = w_ref[:, t * HD : (t + 1) * HD]
        wq[:, t * WIDE + HD : (t + 1) * WIDE] = jnp.zeros((D, WIDE - HD), bf16)
    wo[:, :HD] = w_ref[:, 3 * HD :]
    wo[:, HD:] = jnp.zeros((D, WIDE - HD), bf16)

    @pl.loop(0, TOKENS // BLOCK)
    def _(r):
        half, inner = r // 2, pl.multiple_of((r % 2) * BLOCK, BLOCK)
        rows = pl.ds(pl.multiple_of(r * BLOCK, BLOCK), BLOCK)
        total = jnp.zeros((BLOCK, 1), f32)
        for g in range(NX):
            part = feats_ref[half * NX + g, pl.ds(inner, BLOCK), :].astype(f32)
            total = total + jnp.sum(part * part, axis=-1, keepdims=True)
        factor = lax.rsqrt(total * (1.0 / D) + EPS)
        for g in range(NX):
            part = feats_ref[half * NX + g, pl.ds(inner, BLOCK), :].astype(f32)
            lanes = slice(g * OUTC, (g + 1) * OUTC)
            normed_ref[rows, lanes] = (part * factor * gain_ref[:, lanes]).astype(bf16)
        qkv = dot(normed_ref[rows, :], wq[...]).astype(bf16)
        for t in range(3):
            qkv_ref[t, rows, :] = qkv[:, t * WIDE : (t + 1) * WIDE]

    @pl.loop(0, TOKENS // BLOCK)
    def _(r):
        rows = pl.ds(pl.multiple_of(r * BLOCK, BLOCK), BLOCK)
        weights = softmax_rows(qkv_ref[0, rows, :], qkv_ref[1]).astype(bf16)
        mixed = dot(weights, qkv_ref[2]).astype(bf16)
        mixed_ref[rows, :] = mixed
        partial_ref[rows, :] = dot(mixed, wo[...], NT).astype(bf16)


def forward(feats, gain, wfull):
    return pl.pallas_call(
        forward_kernel,
        out_shape=(
            jax.ShapeDtypeStruct((TOKENS, D), bf16),
            jax.ShapeDtypeStruct((3, TOKENS, WIDE), bf16),
            jax.ShapeDtypeStruct((TOKENS, WIDE), bf16),
            jax.ShapeDtypeStruct((TOKENS, D), bf16),
        ),
        in_specs=[VMEM] * 3,
        out_specs=[VMEM] * 4,
        scratch_shapes=[pltpu.VMEM((D, 3 * WIDE), bf16), pltpu.VMEM((D, WIDE), bf16)],
        compiler_params=pltpu.CompilerParams(vmem_limit_bytes=48 * 1024 * 1024),
        cost_estimate=pl.CostEstimate(flops=4_000_000_000, bytes_accessed=16_000_000, transcendentals=1_100_000),
    )(feats, gain, wfull)


def backward_kernel(
    c_ref, qkv_ref, cot_ref, w_ref, normed_ref, mixed_ref, kept_ref, sent_ref, wo, dm, dcat, dk, dv, grads, outs
):
    wo[:, :HD] = w_ref[:, 3 * HD :]
    wo[:, HD:] = jnp.zeros((D, WIDE - HD), bf16)

    @pl.loop(0, TOKENS // BLOCK)
    def _(r):
        rows = pl.ds(pl.multiple_of(r * BLOCK, BLOCK), BLOCK)
        d_mixed = dot(cot_ref[rows, :], wo[...]).astype(bf16)
        q_block = qkv_ref[0, rows, :]
        weights = softmax_rows(q_block, qkv_ref[1])
        d_weights = dot(d_mixed, qkv_ref[2], NT)
        centre = jnp.sum(weights * d_weights, axis=-1, keepdims=True)
        d_scores = (weights * (d_weights - centre) * SCALE).astype(bf16)
        dcat[rows, 0:HD] = dot(d_scores, qkv_ref[1]).astype(bf16)[:, :HD]
        d_value = dot(d_mixed, weights.astype(bf16), TN)
        d_key = dot(q_block, d_scores, TN)

        @pl.when(r == 0)
        def _():
            dv[...] = d_value
            dk[...] = d_key

        @pl.when(r > 0)
        def _():
            dv[...] += d_value
            dk[...] += d_key

    dcat[:, HD : 2 * HD] = dk[...].T.astype(bf16)[:, :HD]
    dcat[:, 2 * HD : 3 * HD] = dv[...].T.astype(bf16)[:, :HD]

    @pl.loop(0, 4)
    def _(n):
        lanes = pl.ds(pl.multiple_of(n * 384, 384), 384)
        grads[lanes, :] = dot(normed_ref[:, lanes], dcat[...], TN)
        outs[:, lanes] = dot(mixed_ref[...], cot_ref[:, lanes], TN)[:HD]

    c = c_ref[0]
    for ref, core in ((kept_ref, c), (sent_ref, 1 - c)):
        for g in range(8):
            rows = pl.ds(pl.multiple_of((2 * g + core) * 96, 96), 96)
            ref[g, :, : 3 * HD] = grads[rows, :].astype(bf16)
            piece = outs[g * 24 : (g + 1) * 24, pl.ds(pl.multiple_of(core * 768, 768), 768)]
            packed = jnp.concatenate([piece[:, j * HD : (j + 1) * HD] for j in range(4)], axis=0)
            ref[g, :, 3 * HD :] = packed.astype(bf16)


def backward(c, qkv, cot, wfull, normed, mixed):
    return pl.pallas_call(
        backward_kernel,
        out_shape=(jax.ShapeDtypeStruct((8, 96, 768), bf16),) * 2,
        in_specs=[SMEM] + [VMEM] * 5,
        out_specs=[VMEM] * 2,
        scratch_shapes=[
            pltpu.VMEM((D, WIDE), bf16),
            pltpu.VMEM((TOKENS, WIDE), bf16),
            pltpu.VMEM((TOKENS, 3 * HD), bf16),
            pltpu.VMEM((WIDE, TOKENS), f32),
            pltpu.VMEM((WIDE, TOKENS), f32),
            pltpu.VMEM((D, 3 * HD), f32),
            pltpu.VMEM((HD, D), f32),
        ],
        compiler_params=pltpu.CompilerParams(vmem_limit_bytes=56 * 1024 * 1024),
        cost_estimate=pl.CostEstimate(flops=6_000_000_000, bytes_accessed=18_000_000, transcendentals=1_100_000),
    )(c, qkv, cot, wfull, normed, mixed)


def total_kernel(parts_ref, proj_ref, out_ref):
    total = parts_ref[0].astype(f32)
    for g in range(1, 8):
        total = total + parts_ref[g].astype(f32)
    proj_ref[...] = total[:, : 3 * HD].astype(bf16)
    packed = total[:, 3 * HD :]
    out_ref[...] = jnp.concatenate([packed[j * 24 : (j + 1) * 24] for j in range(4)], axis=1).astype(bf16)


def total_parts(parts):
    return pl.pallas_call(
        total_kernel,
        out_shape=(jax.ShapeDtypeStruct((96, 3 * HD), bf16), jax.ShapeDtypeStruct((24, 768), bf16)),
        in_specs=[VMEM],
        out_specs=[VMEM] * 2,
    )(parts)


def proj_kernel(heads_ref, out_ref):
    for h in range(8):
        for t in range(3):
            out_ref[t, :, h * HD : (h + 1) * HD] = heads_ref[h, :, t * HD : (t + 1) * HD].astype(f32)


def place_proj(heads):
    return pl.pallas_call(
        proj_kernel,
        out_shape=jax.ShapeDtypeStruct((3, 96, D), f32),
        in_specs=[VMEM],
        out_specs=VMEM,
    )(heads)


def out_kernel(c_ref, own_ref, other_ref, out_ref):
    c = c_ref[0]
    for ref, core in ((own_ref, c), (other_ref, 1 - c)):
        lanes = pl.ds(pl.multiple_of(core * 768, 768), 768)
        for g in range(8):
            out_ref[g * 24 : (g + 1) * 24, lanes] = ref[g].astype(f32)


def place_out(c, own, other):
    return pl.pallas_call(
        out_kernel,
        out_shape=jax.ShapeDtypeStruct((HD, D), f32),
        in_specs=[SMEM, VMEM, VMEM],
        out_specs=VMEM,
    )(c, own, other)


def lane_sources(zh, y, c, zl):
    lane = lax.iota(jnp.int32, KPAD)
    slot, j = lane // SLOT, lane % SLOT
    core = jnp.where(slot < 16, c, 1 - c)
    within = slot % 16
    zstep = within // 4
    ystep = within % 4
    z = zh * 2 + zl
    src_z = (z + jnp.where(zstep == 1, 3, jnp.where(zstep == 2, 1, jnp.where(zstep == 3, 2, 0)))) % 4
    src_y = (y + 4 - ystep) % 4
    plane = (((src_z // 2) * 4 + src_y) * 2 + core) * 2 + src_z % 2
    return jnp.where(j < GROUP, plane * GROUP + j, -1)


def per_device(sequence, conv_weight, conv_bias, norm_gain, proj_weight, out_weight, cotangent):
    zh, y, c, zl, x = (lax.axis_index(a) for a in ("zh", "y", "c", "zl", "x"))
    zring = ("zh", "zl")

    split = conv_weight.reshape(11, KW, NX, OUTC).transpose(2, 1, 0, 3)
    mine = jnp.zeros((NX, KW, 11, OUTC), bf16)
    for k in range(NX):
        piece = lax.dynamic_index_in_dim(split, (x + k) % NX, 0, keepdims=False)
        if k:
            piece = lax.ppermute(piece, "x", ring(NX, k))
        mine = lax.dynamic_update_index_in_dim(mine, piece, (x + NX - k) % NX, 0)
    mine = mine.transpose(1, 0, 2, 3).reshape(KW, GROUP, OUTC)
    mine = jnp.pad(mine, ((0, 0), (0, SLOT - GROUP), (0, 0)))

    sources = lane_sources(zh, y, c, zl)
    select = (lax.broadcasted_iota(jnp.int32, (CIN, KPAD), 0) == sources[None, :]).astype(bf16)
    edge = jnp.where(zl == 0, sequence[0, -HALO:], sequence[0, :HALO])
    edge = lax.ppermute(edge, "zl", ring(2, 1))
    block = jnp.concatenate([sequence[0], edge], axis=0)
    block = jnp.dot(block, select, preferred_element_type=f32).astype(bf16)
    low, high, far_a, far_b = staged_ring(block, "x", 128)
    far = jnp.concatenate([far_a, far_b], axis=0)
    xblocks = jnp.zeros((NX,) + block.shape, bf16)
    for step, part in ((0, block), (3, low), (1, high), (2, far)):
        xblocks = lax.dynamic_update_index_in_dim(xblocks, part, (x + step) % NX, 0)

    ypieces = jnp.stack([mine] + [lax.ppermute(mine, "y", ring(4, k)) for k in (1, 2, 3)])
    zpieces = staged_ring(ypieces, zring, 2)
    pieces = [ypieces, *zpieces]
    pieces = pieces + [lax.ppermute(p, "c", ring(2, 1)) for p in pieces]
    bias = lax.dynamic_slice_in_dim(conv_bias, x * OUTC, OUTC)[None]
    feat = conv_pool(zl.reshape(1), xblocks, pieces, bias)

    wcat = jnp.concatenate([proj_weight.reshape(96, 576), out_weight.T], axis=1)
    wfull = lax.all_gather(wcat, ("zh", "y", "c"), axis=0, tiled=True)
    cot = lax.all_gather(cotangent[0], ("zl", "x"), axis=0, tiled=True)

    feat, cot = lax.optimization_barrier((feat, cot))
    feats = lax.all_to_all(jnp.broadcast_to(feat[None], (8, 512, OUTC)), ("zl", "x"), 0, 0)
    own = feats.reshape(2, NX, 4, 128, OUTC)
    own = lax.dynamic_index_in_dim(own, zl, 0, keepdims=False)
    own = lax.dynamic_index_in_dim(own, x, 1, keepdims=False)
    own = own.transpose(1, 0, 2).reshape(128, D)

    normed, qkv, mixed, partial = forward(feats, norm_gain[None], wfull)
    attended = lax.psum_scatter(partial, ("zl", "x"), scatter_dimension=0, tiled=True)
    block_out = (own.astype(f32) + attended.astype(f32)).astype(bf16)[None]

    core = c.reshape(1)
    kept, sent = backward(core, qkv, cot, wfull, normed, mixed)
    both = (kept.astype(f32) + lax.ppermute(sent, "c", ring(2, 1)).astype(f32)).astype(bf16)
    proj, outs = total_parts(lax.all_to_all(both, ("zh", "y"), 0, 0))

    heads = lax.all_to_all(jnp.broadcast_to(proj[None], (8, 96, 576)), ("zl", "x"), 0, 0)
    rows = lax.all_to_all(jnp.broadcast_to(outs[None], (8, 24, 768)), ("zh", "y"), 0, 0)
    proj_grad = place_proj(heads).transpose(1, 0, 2)
    out_grad = place_out(core, rows, lax.ppermute(rows, "c", ring(2, 1)))
    return (block_out, proj_grad, out_grad)


def solution(mesh):
    fine = Mesh(mesh.devices.reshape(2, 4, 2, 2, 4), ("zh", "y", "c", "zl", "x"))
    dp, seq = ("zh", "y", "c"), ("zl", "x")
    in_specs = (
        P(dp, seq, None),
        P(dp + seq, None, None),
        P(),
        P(),
        P(dp, None, seq),
        P(seq, dp),
        P(dp, seq, None),
    )
    out_specs = (P(dp, seq, None), P(dp, None, None), P(seq, None))
    return jax.shard_map(per_device, mesh=fine, in_specs=in_specs, out_specs=out_specs, check_vma=False)
```

time: 891 us -> 282 us (0.32)
  waiting for transfers between devices: 681 us -> 101 us
  local copies, waits for them, and re-layouts: 115 us -> 19.5 us
  Pallas kernels: 0 us -> 52.2 us
  matrix products: 38.2 us -> 2.71 us
  starting transfers between devices: 5.57 us -> 39.9 us
  blocking collectives: 28.3 us -> 44 us
    all_gather x5 -> x2, waiting for transfers between devices: 382 us -> 51.9 us  [the longest x1 51.8 us: per_device(): wfull = lax.all_gather(wcat, ('zh', 'y', 'c'), axis=0, tiled=True)]
    reduce_scatter x2 -> x1, waiting for transfers between devices: 155 us -> 0.01 us  [per_device(): lax.psum_scatter(partial, ('zl', 'x'), scatter_dimension=0, tiled=True)]
    psum x1 -> x0, waiting for transfers between devices: 141 us -> none  [per_device(): out_grad = lax.psum(grad_running, 'dp')]
    slice x2 -> x4, local copies, waits for them, and re-layouts: 91.5 us -> 1.13 us  [the longest x2 1.06 us: staged_ring(): far_a = lax.ppermute(lax.slice_in_dim(low, 0, cut), axis, ring(4, 1))]
    pallas_call x0 -> x6, Pallas kernels: none -> 52.2 us  [the longest x1 18.6 us: backward(): pl.pallas_call(backward_kernel, out_shape=(jax.ShapeDtypeStruct((8, 96, 7...]
    all_to_all x0 -> x2, blocking collectives: none -> 44 us  [the longest x1 31.9 us: per_device(): proj, outs = total_parts(lax.all_to_all(both, ('zh', 'y'), 0, 0))]
    ppermute x2 -> x22, waiting for transfers between devices: 2.07 us -> 39.8 us  [the longest x2 27.5 us: staged_ring(): high = lax.ppermute(block, axis, ring(4, -1))]
    dot_general x21 -> x1, matrix products: 34.3 us -> 2.71 us  [per_device(): block = jnp.dot(block, select, preferred_element_type=f32).astype(bf16)]
  transfers between devices with their start and end apart: 10 -> 27, of which waited for: 7 -> 11; matrix products, arithmetic and copies ran while one was open for 15% -> 7% of each run, Pallas kernels for 0% -> 14%
where the time goes in v1:
time: 282 us; the launch traced here: 281 us
  waiting for transfers between devices  101 us (36%)
  Pallas kernels  52.2 us (19%)
  blocking collectives  44 us (16%)
  starting transfers between devices  39.9 us (14%)
  local copies, waits for them, and re-layouts  19.5 us (7%)
  between operations  14.1 us (5%)
  other arithmetic  7.13 us (3%)
    all_gather x1, waiting for transfers between devices, per_device(): wfull = lax.all_gather(wcat, ('zh', 'y', 'c'), axis=0, tiled=True)  51.8 us
    all_to_all x1, blocking collectives, per_device(): proj, outs = total_parts(lax.all_to_all(both, ('zh', 'y'), 0, 0))  31.9 us
    ppermute x2, waiting for transfers between devices, staged_ring(): high = lax.ppermute(block, axis, ring(4, -1))  27.5 us
    pallas_call x1, Pallas kernels, backward(): pl.pallas_call(backward_kernel, out_shape=(jax.ShapeDtypeStruct((8, 96, 7...  18.6 us
    pallas_call x1, Pallas kernels, forward(): pl.pallas_call(forward_kernel, out_shape=(jax.ShapeDtypeStruct((TOKENS, D...  13.4 us
    pallas_call x1, Pallas kernels, conv_pool(): pl.pallas_call(conv_kernel, out_shape=jax.ShapeDtypeStruct((512, OUTC), b...  13.3 us
    all_to_all x1, blocking collectives, per_device(): lax.all_to_all(jnp.broadcast_to(outs[None], (8, 24, 768)), ('zh', 'y'), 0...  12.1 us
    all_to_all x1, waiting for transfers between devices, per_device(): lax.all_to_all(jnp.broadcast_to(proj[None], (8, 96, 576)), ('zl', 'x'), 0...  8.88 us
  transfers between devices with their start and end apart: 27, of which 11 were waited for; matrix products, arithmetic and copies ran while one was open for 7% of the time, Pallas kernels for 14%

profile of v1, /device:TPU:1, one launch (start us, length us, event | category | flops | bytes accessed | tf_op | source)
XLA Modules:
  0.0 280.8 jit_solution(384756123952442080)
XLA Ops:
  7.2 0.7 all-gather.6.cloned.1.call-update
  8.0 0.8 select_bitcast_fusion
  8.8 2.5 collective-permute-start
  11.3 1.1 reshape.159
  12.4 0.4 constant_dynamic-slice_fusion
  12.8 1.3 collective-permute-start.5
  14.1 2.5 collective-permute-start.6
  16.7 1.2 collective-permute-start.7
  18.0 0.9 collective-permute-done.6
  18.9 1.6 collective-permute-done.7
  20.6 2.8 collective-permute-start.10
  23.4 0.3 collective-permute-start.9
  23.8 0.7 collective-permute-start.8
  24.5 0.3 broadcast_in_dim.75
  24.8 2.7 bitcast_dynamic-update-slice_fusion.2
  27.5 2.7 collective-permute-start.2
  30.2 4.5 %collective-permute-done.8 = bf16[5,48,384]{2,1,0:T(8,128)(2,1)S(1)} collective-permute-done((bf16[5,48,384]{2,1,0:T(8,128)(2,1)S(1)}, bf16[5,48,384]{2,1,0:T(8,128)(2,1)S(1)}, u32[]{:S(2)}, u32[]{:S(2)}) %collective-permute-start.8) | collective-permute-done | bytes 184352 | tf_op jit(solution)/shard_map/ppermute | solution.py:313
  34.6 0.1 pad_maximum_fusion.refs_0_
  34.8 2.7 collective-permute-start.12
  37.6 0.2 copy.22
  37.8 0.2 copy.24
  37.9 0.8 pad_maximum_fusion.1
  38.7 0.8 dynamic_slice.26
  39.5 1.9 collective-permute-start.15
  41.4 24.0 %collective-permute-done.2 = bf16[272,1536]{1,0:T(8,128)(2,1)S(1)} collective-permute-done((bf16[272,1536]{1,0:T(8,128)(2,1)}, bf16[272,1536]{1,0:T(8,128)(2,1)S(1)}, u32[]{:S(2)}, u32[]{:S(2)}) %collective-permute-start.2) | collective-permute-done | bytes 835616 | tf_op jit(solution)/shard_map/ppermute | solution.py:32
  65.4 3.5 %collective-permute-start.4 = (bf16[144,1536]{1,0:T(8,128)(2,1)S(1)}, bf16[144,1536]{1,0:T(8,128)(2,1)S(1)}, u32[]{:S(2)}, u32[]{:S(2)}) collective-permute-start(bf16[144,1536]{1,0:T(8,128)(2,1)S(1)} %slice.25), channel_id=1, source_target_pairs={{0,3},{1,0},{2,1},{3,2},{4,7},{5,4},{6,5},{7,6},{8,11},{9,8},{10,9... | collective-permute-start | bytes 1327112 | tf_op jit(solution)/shard_map/ppermute | solution.py:34
  68.9 1.0 slice.24
  70.1 3.5 %collective-permute-done.12.refs_2_ = bf16[4,5,48,384]{3,2,1,0:T(8,128)(2,1)S(1)} collective-permute-done((bf16[4,5,48,384]{3,2,1,0:T(8,128)(2,1)S(1)}, bf16[4,5,48,384]{3,2,1,0:T(8,128)(2,1)S(1)}, u32[]{:S(2)}, u32[]{:S(2)}) %collective-permute-start.12) | collective-permute-done | bytes 737312 | tf_op jit(solution)/shard_map/ppermute | solution.py:32
  73.7 2.1 bitcast_dynamic-update-slice_fusion.1
  75.9 2.0 collective-permute-done.3
  77.8 5.4 %collective-permute-start.16 = (bf16[4,5,48,384]{3,2,1,0:T(8,128)(2,1)S(1)}, bf16[4,5,48,384]{3,2,1,0:T(8,128)(2,1)S(1)}, u32[]{:S(2)}, u32[]{:S(2)}) collective-permute-start(bf16[4,5,48,384]{3,2,1,0:T(8,128)(2,1)S(1)} %collective-permute-done.11.refs_1_), channel_id=1, source_target_pairs={{0,8},{8,0},{1,9},{9,1},{2,10},{10,2},{3,11},{11,3},{4,12},{12,4},... | collective-permute-start | bytes 2211848 | tf_op jit(solution)/shard_map/ppermute | solution.py:316
  83.3 0.5 collective-permute-start.18
  83.8 1.0 collective-permute-start.19
  84.7 1.0 bitcast_dynamic-update-slice_fusion
  85.7 0.9 fusion.3.x_ref
  86.7 0.5 collective-permute-done.19.refs_9_
  87.2 0.3 copy-done.12
  87.5 13.3 %shard_map.94 = bf16[512,384]{1,0:T(8,128)(2,1)S(1)} custom-call(s32[1]{0:T(128)} %bitcast.zl_ref, bf16[4,272,1536]{2,1,0:T(8,128)(2,1)} %fusion.3.x_ref, bf16[4,5,48,384]{3,2,1,0:T(8,128)(2,1)S(1)} %pad_maximum_fusion.refs_0_, bf16[4,5,48,384]{3,2,1,0:T(8,128)(2,1)S(1)} %collective-permute-done.11.refs_1_, ...), custom_call_target="tpu_custom_call" | custom-call | flops 6000000000 | bytes 9000000 | tf_op jit(solution)/shard_map/pallas_call | solution.py:70
  100.8 1.9 broadcast_in_dim.87
  102.8 4.6 %all-to-all-start = ((bf16[8,512,384]{2,1,0:T(8,128)(2,1)}), bf16[8,512,384]{2,1,0:T(8,128)(2,1)S(1)}, u32[]{:S(2)}, u32[]{:S(2)}) async-start(bf16[8,512,384]{2,1,0:T(8,128)(2,1)} %broadcast_in_dim.87), calls=%async_computation | async-start | bytes 6291456 | tf_op jit(solution)/shard_map/all_to_all | solution.py:325
  107.4 51.8 %all-gather.4.cloned.1.call-done.w_ref = bf16[1536,768]{1,0:T(8,128)(2,1)} async-done(((bf16[96,768]{1,0:T(8,128)(2,1)}), bf16[1536,768]{1,0:T(8,128)(2,1)}) %all-gather.4.cloned.1.call-update) | async-done | bytes 2359312 | tf_op jit(solution)/shard_map/all_gather | solution.py:321
  159.3 1.7 copy-done.3
  161.0 1.7 copy-done
  162.6 13.4 %shard_map.95 = (bf16[1024,1536]{1,0:T(8,128)(2,1)}, bf16[3,1024,256]{2,1,0:T(8,128)(2,1)S(1)}, bf16[1024,256]{1,0:T(8,128)(2,1)S(1)}, bf16[1024,1536]{1,0:T(8,128)(2,1)}) custom-call(bf16[8,512,384]{2,1,0:T(8,128)(2,1)} %copy-done.3, f32[1,1536]{1,0:T(1,128)S(1)} %broadcast_in_dim.88.gain_ref, bf16[1536,768]{1,0:T(8,128)(2,1)S(1)} %copy-done), custom_call_target="tpu_custom_call" | custom-call | flops 4000000000 | bytes 16000000 | tf_op jit(solution)/shard_map/pallas_call | solution.py:139
  176.1 1.1 copy-done.1
  177.2 0.8 copy-done.2
  178.0 18.6 %shard_map.96 = (bf16[8,96,768]{2,1,0:T(8,128)(2,1)}, bf16[8,96,768]{2,1,0:T(8,128)(2,1)}) custom-call(s32[1]{0:T(128)} %bitcast.29.c_ref, bf16[3,1024,256]{2,1,0:T(8,128)(2,1)} %copy-done.1, bf16[1024,1536]{1,0:T(8,128)(2,1)} %bitcast.75, bf16[1536,768]{1,0:T(8,128)(2,1)} %all-gather.4.cloned.1.call-done.w_ref, ...), custom_call_target="tpu_custom_call" | custom-call | flops 6000000000 | bytes 18000000 | tf_op jit(solution)/shard_map/pallas_call | solution.py:204
  196.6 0.3 collective-permute-start.20
  196.9 2.8 collective-permute-done.20
  199.7 1.6 add_convert_fusion
  201.2 31.9 %all_to_all.20.parts_ref = bf16[8,96,768]{2,1,0:T(8,128)(2,1)} all-to-all(bf16[8,96,768]{2,1,0:T(8,128)(2,1)S(1)} %add_convert_fusion), channel_id=1, replica_groups=mesh['zh'=2,'y'=4,'c'=2,'zl'=2,'x'=4] {'zh','y'}, dimensions={0} | all-to-all | bytes 2359296 | tf_op jit(solution)/shard_map/all_to_all | solution.py:338
  233.2 2.1 shard_map.97
  235.3 0.8 broadcast_in_dim.91
  236.1 12.1 %all_to_all.21.own_ref = bf16[8,24,768]{2,1,0:T(8,128)(2,1)S(1)} all-to-all(bf16[8,24,768]{2,1,0:T(8,128)(2,1)S(1)} %broadcast_in_dim.91), channel_id=1, replica_groups=mesh['zh'=2,'y'=4,'c'=2,'zl'=2,'x'=4] {'zh','y'}, dimensions={0} | all-to-all | bytes 589824 | tf_op jit(solution)/shard_map/all_to_all | solution.py:341
  248.2 2.0 broadcast_in_dim.90
  250.2 3.6 %all-to-all-start.2 = ((bf16[8,96,576]{2,1,0:T(8,128)(2,1)}), bf16[8,96,576]{2,1,0:T(8,128)(2,1)S(1)}, u32[]{:S(2)}, u32[]{:S(2)}) async-start(bf16[8,96,576]{2,1,0:T(8,128)(2,1)} %broadcast_in_dim.90), calls=%async_computation.3 | async-start | bytes 1966080 | tf_op jit(solution)/shard_map/all_to_all | solution.py:340
  253.8 2.1 collective-permute-start.21
  255.9 1.0 convert_bitcast_fusion
  257.1 0.7 copy-done.7
  257.8 2.1 shard_map.99
  260.0 8.9 %all-to-all-done.2.heads_ref = bf16[8,96,576]{2,1,0:T(8,128)(2,1)S(1)} async-done(((bf16[8,96,576]{2,1,0:T(8,128)(2,1)}), bf16[8,96,576]{2,1,0:T(8,128)(2,1)S(1)}, u32[]{:S(2)}, u32[]{:S(2)}) %all-to-all-start.2) | async-done | bytes 884768 | tf_op jit(solution)/shard_map/all_to_all | solution.py:340
  268.8 1.0 copy-done.4
  269.8 2.6 shard_map.98
  272.4 1.8 fusion.7
  (65 shorter events, 1.2 us)
Async XLA Ops:
  7.2 93.7 %all-gather.6.cloned.1.call-start = ((), (), s32[]{:S(2)}) async-start(), calls=%async_computation.7 | async-start | bytes 3538944 | tf_op jit(solution)/shard_map/all_gather | solution.py:322
  7.9 151.4 %all-gather.4.cloned.1.call-start = ((), (), s32[]{:S(2)}) async-start(), calls=%async_computation.5 | async-start | bytes 2506752 | tf_op jit(solution)/shard_map/all_gather | solution.py:321
  8.8 15.7 %collective-permute-start = (bf16[16,1408]{1,0:T(8,128)(2,1)S(1)}, bf16[16,1408]{1,0:T(8,128)(2,1)S(1)}, u32[]{:S(2)}, u32[]{:S(2)}) collective-permute-start(bf16[16,1408]{1,0:T(8,128)(2,1)S(1)} %select_bitcast_fusion), channel_id=1, source_target_pairs={{0,4},{4,0},{1,5},{5,1},{2,6},{6,2},{3,7},{7,3},{8,12},{12,8},{9,1... | collective-permute-start | bytes 135176 | tf_op jit(solution)/shard_map/ppermute | solution.py:304
  12.8 5.2 %collective-permute-start.5 = (bf16[5,11,384]{2,1,0:T(8,128)(2,1)S(1)}, bf16[5,11,384]{2,1,0:T(8,128)(2,1)S(1)}, u32[]{:S(2)}, u32[]{:S(2)}) collective-permute-start(bf16[5,11,384]{2,1,0:T(8,128)(2,1)S(1)} %bitcast.73), channel_id=1, source_target_pairs={{0,1},{1,2},{2,3},{3,0},{4,5},{5,6},{6,7},{7,4},{8,9},{9,10},{10,1... | collective-permute-start | bytes 126728 | tf_op jit(solution)/shard_map/ppermute | solution.py:296
  14.1 4.8 %collective-permute-start.6 = (bf16[5,11,384]{2,1,0:T(8,128)(2,1)S(1)}, bf16[5,11,384]{2,1,0:T(8,128)(2,1)S(1)}, u32[]{:S(2)}, u32[]{:S(2)}) collective-permute-start(bf16[5,11,384]{2,1,0:T(8,128)(2,1)S(1)} %bitcast.72), channel_id=1, source_target_pairs={{0,2},{1,3},{2,0},{3,1},{4,6},{5,7},{6,4},{7,5},{8,10},{9,11},{10,... | collective-permute-start | bytes 126728 | tf_op jit(solution)/shard_map/ppermute | solution.py:296
  16.7 3.8 %collective-permute-start.7 = (bf16[5,11,384]{2,1,0:T(8,128)(2,1)S(1)}, bf16[5,11,384]{2,1,0:T(8,128)(2,1)S(1)}, u32[]{:S(2)}, u32[]{:S(2)}) collective-permute-start(bf16[5,11,384]{2,1,0:T(8,128)(2,1)S(1)} %bitcast.71), channel_id=1, source_target_pairs={{0,3},{1,0},{2,1},{3,2},{4,7},{5,4},{6,5},{7,6},{8,11},{9,8},{10,9... | collective-permute-start | bytes 126728 | tf_op jit(solution)/shard_map/ppermute | solution.py:296
  17.9 6.8 %copy-start.10 = (bf16[1,256,1408]{2,1,0:T(8,128)(2,1)S(1)}, bf16[1,256,1408]{2,1,0:T(8,128)(2,1)}, u32[]{:S(2)}) copy-start(bf16[1,256,1408]{2,1,0:T(8,128)(2,1)} %param.7) | copy-start | bytes 2162692
  20.6 9.5 %collective-permute-start.10 = (bf16[5,48,384]{2,1,0:T(8,128)(2,1)S(1)}, bf16[5,48,384]{2,1,0:T(8,128)(2,1)S(1)}, u32[]{:S(2)}, u32[]{:S(2)}) collective-permute-start(bf16[5,48,384]{2,1,0:T(8,128)(2,1)S(1)} %get-tuple-element.24), channel_id=1, source_target_pairs={{0,48},{16,0},{32,16},{48,32},{1,49},{17,1},{33,17},{49,33},{2,50}... | collective-permute-start | bytes 552968 | tf_op jit(solution)/shard_map/ppermute | solution.py:313
  23.4 6.7 %collective-permute-start.9 = (bf16[5,48,384]{2,1,0:T(8,128)(2,1)S(1)}, bf16[5,48,384]{2,1,0:T(8,128)(2,1)S(1)}, u32[]{:S(2)}, u32[]{:S(2)}) collective-permute-start(bf16[5,48,384]{2,1,0:T(8,128)(2,1)S(1)} %get-tuple-element.24), channel_id=1, source_target_pairs={{0,32},{16,48},{32,0},{48,16},{1,33},{17,49},{33,1},{49,17},{2,34}... | collective-permute-start | bytes 552968 | tf_op jit(solution)/shard_map/ppermute | solution.py:313
  23.8 10.9 %collective-permute-start.8 = (bf16[5,48,384]{2,1,0:T(8,128)(2,1)S(1)}, bf16[5,48,384]{2,1,0:T(8,128)(2,1)S(1)}, u32[]{:S(2)}, u32[]{:S(2)}) collective-permute-start(bf16[5,48,384]{2,1,0:T(8,128)(2,1)S(1)} %get-tuple-element.24), channel_id=1, source_target_pairs={{0,16},{16,32},{32,48},{48,0},{1,17},{17,33},{33,49},{49,1},{2,18}... | collective-permute-start | bytes 552968 | tf_op jit(solution)/shard_map/ppermute | solution.py:313
  24.7 12.8 %copy-start.9 = (bf16[192,96]{1,0:T(8,128)(2,1)S(1)}, bf16[192,96]{1,0:T(8,128)(2,1)}, u32[]{:S(2)}) copy-start(bf16[192,96]{1,0:T(8,128)(2,1)} %param.12) | copy-start | bytes 110596
  24.7 12.9 %copy-start.8 = (bf16[96,3,192]{2,0,1:T(8,128)(2,1)S(1)}, bf16[96,3,192]{2,0,1:T(8,128)(2,1)}, u32[]{:S(2)}) copy-start(bf16[96,3,192]{2,0,1:T(8,128)(2,1)} %param.11) | copy-start | bytes 331780
  27.5 7.3 %copy-start.5 = (bf16[4,272,1536]{2,1,0:T(8,128)(2,1)}, bf16[4,272,1536]{2,1,0:T(8,128)(2,1)S(1)}, u32[]{:S(2)}) copy-start(bf16[4,272,1536]{2,1,0:T(8,128)(2,1)S(1)} %get-tuple-element.29) | copy-start | bytes 10027012
  27.5 41.4 %collective-permute-start.1 = (bf16[272,1536]{1,0:T(8,128)(2,1)}, bf16[272,1536]{1,0:T(8,128)(2,1)}, u32[]{:S(2)}, u32[]{:S(2)}) collective-permute-start(bf16[272,1536]{1,0:T(8,128)(2,1)} %get-tuple-element.30), channel_id=1, source_target_pairs={{0,1},{1,2},{2,3},{3,0},{4,5},{5,6},{6,7},{7,4},{8,9},{9,10},{10,1... | collective-permute-start | bytes 2506760 | tf_op jit(solution)/shard_map/ppermute | solution.py:31
  27.5 37.9 %collective-permute-start.2 = (bf16[272,1536]{1,0:T(8,128)(2,1)}, bf16[272,1536]{1,0:T(8,128)(2,1)S(1)}, u32[]{:S(2)}, u32[]{:S(2)}) collective-permute-start(bf16[272,1536]{1,0:T(8,128)(2,1)} %get-tuple-element.30), channel_id=1, source_target_pairs={{0,3},{1,0},{2,1},{3,2},{4,7},{5,4},{6,5},{7,6},{8,11},{9,8},{10,9... | collective-permute-start | bytes 2506760 | tf_op jit(solution)/shard_map/ppermute | solution.py:32
  34.8 35.2 %collective-permute-start.11 = (bf16[4,5,48,384]{3,2,1,0:T(8,128)(2,1)S(1)}, bf16[4,5,48,384]{3,2,1,0:T(8,128)(2,1)S(1)}, u32[]{:S(2)}, u32[]{:S(2)}) collective-permute-start(bf16[4,5,48,384]{3,2,1,0:T(8,128)(2,1)S(1)} %pad_maximum_fusion.refs_0_), channel_id=1, source_target_pairs={{0,4},{4,64},{64,68},{68,0},{1,5},{5,65},{65,69},{69,1},{2,6},{6,6... | collective-permute-start | bytes 2211848 | tf_op jit(solution)/shard_map/ppermute | solution.py:31
  34.8 38.8 %collective-permute-start.12 = (bf16[4,5,48,384]{3,2,1,0:T(8,128)(2,1)S(1)}, bf16[4,5,48,384]{3,2,1,0:T(8,128)(2,1)S(1)}, u32[]{:S(2)}, u32[]{:S(2)}) collective-permute-start(bf16[4,5,48,384]{3,2,1,0:T(8,128)(2,1)S(1)} %pad_maximum_fusion.refs_0_), channel_id=1, source_target_pairs={{0,68},{4,0},{64,4},{68,64},{1,69},{5,1},{65,5},{69,65},{2,70},{6,... | collective-permute-start | bytes 2211848 | tf_op jit(solution)/shard_map/ppermute | solution.py:32
  39.5 47.1 %collective-permute-start.15 = (bf16[4,5,48,384]{3,2,1,0:T(8,128)(2,1)S(1)}, bf16[4,5,48,384]{3,2,1,0:T(8,128)(2,1)S(1)}, u32[]{:S(2)}, u32[]{:S(2)}) collective-permute-start(bf16[4,5,48,384]{3,2,1,0:T(8,128)(2,1)S(1)} %pad_maximum_fusion.refs_0_), channel_id=1, source_target_pairs={{0,8},{8,0},{1,9},{9,1},{2,10},{10,2},{3,11},{11,3},{4,12},{12,4},... | collective-permute-start | bytes 2211848 | tf_op jit(solution)/shard_map/ppermute | solution.py:316
  65.4 17.8 %collective-permute-start.4 = (bf16[144,1536]{1,0:T(8,128)(2,1)S(1)}, bf16[144,1536]{1,0:T(8,128)(2,1)S(1)}, u32[]{:S(2)}, u32[]{:S(2)}) collective-permute-start(bf16[144,1536]{1,0:T(8,128)(2,1)S(1)} %slice.25), channel_id=1, source_target_pairs={{0,3},{1,0},{2,1},{3,2},{4,7},{5,4},{6,5},{7,6},{8,11},{9,8},{10,9... | collective-permute-start | bytes 1327112 | tf_op jit(solution)/shard_map/ppermute | solution.py:34
  69.9 7.9 %collective-permute-start.3 = (bf16[128,1536]{1,0:T(8,128)(2,1)S(1)}, bf16[128,1536]{1,0:T(8,128)(2,1)S(1)}, u32[]{:S(2)}, u32[]{:S(2)}) collective-permute-start(bf16[128,1536]{1,0:T(8,128)(2,1)S(1)} %slice.24), channel_id=1, source_target_pairs={{0,1},{1,2},{2,3},{3,0},{4,5},{5,6},{6,7},{7,4},{8,9},{9,10},{10,1... | collective-permute-start | bytes 1179656 | tf_op jit(solution)/shard_map/ppermute | solution.py:33
  70.0 13.2 %collective-permute-start.13 = (bf16[2,5,48,384]{3,2,1,0:T(8,128)(2,1)S(1)}, bf16[2,5,48,384]{3,2,1,0:T(8,128)(2,1)S(1)}, u32[]{:S(2)}, u32[]{:S(2)}) collective-permute-start(bf16[2,5,48,384]{3,2,1,0:T(8,128)(2,1)S(1)} %slice.26), channel_id=1, source_target_pairs={{0,4},{4,64},{64,68},{68,0},{1,5},{5,65},{65,69},{69,1},{2,6},{6,6... | collective-permute-start | bytes 1105928 | tf_op jit(solution)/shard_map/ppermute | solution.py:33
  73.6 10.1 %collective-permute-start.14 = (bf16[2,5,48,384]{3,2,1,0:T(8,128)(2,1)S(1)}, bf16[2,5,48,384]{3,2,1,0:T(8,128)(2,1)S(1)}, u32[]{:S(2)}, u32[]{:S(2)}) collective-permute-start(bf16[2,5,48,384]{3,2,1,0:T(8,128)(2,1)S(1)} %slice.27), channel_id=1, source_target_pairs={{0,68},{4,0},{64,4},{68,64},{1,69},{5,1},{65,5},{69,65},{2,70},{6,... | collective-permute-start | bytes 1105928 | tf_op jit(solution)/shard_map/ppermute | solution.py:34
  77.8 8.8 %collective-permute-start.16 = (bf16[4,5,48,384]{3,2,1,0:T(8,128)(2,1)S(1)}, bf16[4,5,48,384]{3,2,1,0:T(8,128)(2,1)S(1)}, u32[]{:S(2)}, u32[]{:S(2)}) collective-permute-start(bf16[4,5,48,384]{3,2,1,0:T(8,128)(2,1)S(1)} %collective-permute-done.11.refs_1_), channel_id=1, source_target_pairs={{0,8},{8,0},{1,9},{9,1},{2,10},{10,2},{3,11},{11,3},{4,12},{12,4},... | collective-permute-start | bytes 2211848 | tf_op jit(solution)/shard_map/ppermute | solution.py:316
  83.2 3.4 %collective-permute-start.17 = (bf16[4,5,48,384]{3,2,1,0:T(8,128)(2,1)S(1)}, bf16[4,5,48,384]{3,2,1,0:T(8,128)(2,1)S(1)}, u32[]{:S(2)}, u32[]{:S(2)}) collective-permute-start(bf16[4,5,48,384]{3,2,1,0:T(8,128)(2,1)S(1)} %collective-permute-done.12.refs_2_), channel_id=1, source_target_pairs={{0,8},{8,0},{1,9},{9,1},{2,10},{10,2},{3,11},{11,3},{4,12},{12,4},... | collective-permute-start | bytes 2211848 | tf_op jit(solution)/shard_map/ppermute | solution.py:316
  83.3 3.4 %collective-permute-start.18 = (bf16[2,5,48,384]{3,2,1,0:T(8,128)(2,1)S(1)}, bf16[2,5,48,384]{3,2,1,0:T(8,128)(2,1)S(1)}, u32[]{:S(2)}, u32[]{:S(2)}) collective-permute-start(bf16[2,5,48,384]{3,2,1,0:T(8,128)(2,1)S(1)} %collective-permute-done.13.refs_3_), channel_id=1, source_target_pairs={{0,8},{8,0},{1,9},{9,1},{2,10},{10,2},{3,11},{11,3},{4,12},{12,4},... | collective-permute-start | bytes 1105928 | tf_op jit(solution)/shard_map/ppermute | solution.py:316
  83.8 3.4 %collective-permute-start.19 = (bf16[2,5,48,384]{3,2,1,0:T(8,128)(2,1)S(1)}, bf16[2,5,48,384]{3,2,1,0:T(8,128)(2,1)S(1)}, u32[]{:S(2)}, u32[]{:S(2)}) collective-permute-start(bf16[2,5,48,384]{3,2,1,0:T(8,128)(2,1)S(1)} %collective-permute-done.14.refs_4_), channel_id=1, source_target_pairs={{0,8},{8,0},{1,9},{9,1},{2,10},{10,2},{3,11},{11,3},{4,12},{12,4},... | collective-permute-start | bytes 1105928 | tf_op jit(solution)/shard_map/ppermute | solution.py:316
  86.6 0.9 copy-start.12
  102.8 4.6 %copy-start.11 = (f32[1536]{0:T(1024)S(1)}, f32[1536]{0:T(1024)}, u32[]{:S(2)}) copy-start(f32[1536]{0:T(1024)} %param.10) | copy-start | bytes 18436
  102.8 56.5 %all-to-all-start = ((bf16[8,512,384]{2,1,0:T(8,128)(2,1)}), bf16[8,512,384]{2,1,0:T(8,128)(2,1)S(1)}, u32[]{:S(2)}, u32[]{:S(2)}) async-start(bf16[8,512,384]{2,1,0:T(8,128)(2,1)} %broadcast_in_dim.87), calls=%async_computation | async-start | bytes 6291456 | tf_op jit(solution)/shard_map/all_to_all | solution.py:325
  107.4 165.1 %reduce-scatter.2.cloned.1.call-start = ((), (), s32[]{:S(2)}) async-start(), calls=%async_computation.6 | async-start | bytes 3538944 | tf_op jit(solution)/shard_map/reduce_scatter | solution.py:332
  159.3 1.7 copy-start.3
  161.0 1.7 copy-start
  176.1 1.1 copy-start.1
  177.2 0.8 copy-start.2
  196.6 3.1 %collective-permute-start.20 = (bf16[8,96,768]{2,1,0:T(8,128)(2,1)}, bf16[8,96,768]{2,1,0:T(8,128)(2,1)S(1)}, u32[]{:S(2)}, u32[]{:S(2)}) collective-permute-start(bf16[8,96,768]{2,1,0:T(8,128)(2,1)} %get-tuple-element.20), channel_id=1, source_target_pairs={{0,8},{8,0},{1,9},{9,1},{2,10},{10,2},{3,11},{11,3},{4,12},{12,4},... | collective-permute-start | bytes 3538952 | tf_op jit(solution)/shard_map/ppermute | solution.py:337
  248.2 8.8 %copy-start.6 = (bf16[8,24,768]{2,1,0:T(8,128)(2,1)}, bf16[8,24,768]{2,1,0:T(8,128)(2,1)S(1)}, u32[]{:S(2)}) copy-start(bf16[8,24,768]{2,1,0:T(8,128)(2,1)S(1)} %all_to_all.21.own_ref) | copy-start | bytes 884740
  250.2 18.6 %all-to-all-start.2 = ((bf16[8,96,576]{2,1,0:T(8,128)(2,1)}), bf16[8,96,576]{2,1,0:T(8,128)(2,1)S(1)}, u32[]{:S(2)}, u32[]{:S(2)}) async-start(bf16[8,96,576]{2,1,0:T(8,128)(2,1)} %broadcast_in_dim.90), calls=%async_computation.3 | async-start | bytes 1966080 | tf_op jit(solution)/shard_map/all_to_all | solution.py:340
  253.8 3.3 %collective-permute-start.21 = (bf16[8,24,768]{2,1,0:T(8,128)(2,1)S(1)}, bf16[8,24,768]{2,1,0:T(8,128)(2,1)S(1)}, u32[]{:S(2)}, u32[]{:S(2)}) collective-permute-start(bf16[8,24,768]{2,1,0:T(8,128)(2,1)S(1)} %all_to_all.21.own_ref), channel_id=1, source_target_pairs={{0,8},{8,0},{1,9},{9,1},{2,10},{10,2},{3,11},{11,3},{4,12},{12,4},... | collective-permute-start | bytes 884744 | tf_op jit(solution)/shard_map/ppermute | solution.py:343
  257.1 0.7 copy-start.7
  268.8 1.0 copy-start.4
Sparse Core Ops, SparseCore 0:
  9.6 63.9 all-gather.5
  76.6 82.6 all-gather.3
  178.2 49.2 reduce-scatter.1

commit v2 on v1

v2 whole, which is shorter than its diff:
```python
import jax
import jax.numpy as jnp
import numpy as np
from jax import lax
from jax.experimental import pallas as pl
from jax.experimental.pallas import tpu as pltpu
from jax.sharding import Mesh, PartitionSpec as P

HD = 192
D = 1536
NX = 4
CIN = 1408
GROUP = 44
SLOT = 48
PLANE = 32
KPAD = PLANE * SLOT
OUTC = D // NX
KW = 5
EPS = 1e-06
HALO = 16

bf16 = jnp.bfloat16
f32 = jnp.float32


def ring(n, k):
    return [(i, (i + k) % n) for i in range(n)]


def across(low, high, axis, cut):
    far_a = lax.ppermute(lax.slice_in_dim(low, 0, cut), axis, ring(4, 1))
    far_b = lax.ppermute(lax.slice_in_dim(high, cut, None), axis, ring(4, -1))
    return far_a, far_b


def staged_ring(block, axis, cut):
    low = lax.ppermute(block, axis, ring(4, 1))
    high = lax.ppermute(block, axis, ring(4, -1))
    return low, high, *across(low, high, axis, cut)


def conv_kernel(pos_ref, *refs):
    (x0, x1, x2, x3a, x3b, w0, w1, w2, w3a, w3b, o0, o1, o2, o3a, o3b, bias_ref, out_ref, wcat, xs, *accs) = refs
    row = 0
    for ref in (w0, w1, w2, w3a, w3b, o0, o1, o2, o3a, o3b):
        for piece in range(ref.shape[0]):
            for off in range(KW):
                wcat[row : row + SLOT, off * OUTC : (off + 1) * OUTC] = ref[piece, off]
            row += SLOT
    x, half = pos_ref[1], pos_ref[3] % 2
    zeros = jnp.zeros((HALO, KPAD), bf16)
    xs[0:HALO, :] = zeros
    xs[HALO + 1024 : 2 * HALO + 1024, :] = zeros

    def place_halo(b, edge):
        @pl.when(jnp.logical_and(half == 0, b == 0))
        def _():
            xs[HALO + 1024 : 2 * HALO + 1024, :] = edge()

        @pl.when(jnp.logical_and(half == 1, b == 3))
        def _():
            xs[0:HALO, :] = edge()

    for ref, step in ((x0, 0), (x1, 3), (x2, 1)):
        b = (x + step) % NX
        xs[pl.ds(pl.multiple_of(HALO + b * 256, HALO), 256), :] = ref[0:256, :]
        place_halo(b, lambda ref=ref: ref[256 : 256 + HALO, :])
    b = (x + 2) % NX
    xs[pl.ds(pl.multiple_of(HALO + b * 256, HALO), 128), :] = x3a[...]
    xs[pl.ds(pl.multiple_of(HALO + b * 256 + 128, HALO), 128), :] = x3b[0:128, :]
    place_halo(b, lambda: x3b[128 : 128 + HALO, :])

    @pl.loop(0, 4)
    def _(r):
        base = pl.multiple_of(r * 256, 256)
        y = jnp.dot(xs[pl.ds(base, 256 + 2 * HALO), :], wcat[...], preferred_element_type=f32)
        total = bias_ref[...] + jnp.zeros((256, OUTC), f32)
        for off in range(KW):
            first = HALO + off - 2
            total = total + y[first : first + 256, off * OUTC : (off + 1) * OUTC]
        activated = jax.nn.gelu(total)
        for n, acc in enumerate(accs):
            acc[...] = activated[:, n * 128 : (n + 1) * 128]
            top = jnp.maximum(acc[pl.ds(0, 128, 2), :], acc[pl.ds(1, 128, 2), :])
            out_ref[pl.ds(pl.multiple_of(r * 128, 128), 128), n * 128 : (n + 1) * 128] = top.astype(bf16)


VMEM = pl.BlockSpec(memory_space=pltpu.VMEM)
SMEM = pl.BlockSpec(memory_space=pltpu.SMEM)


def conv_pool(pos, xpieces, wpieces, bias):
    return pl.pallas_call(
        conv_kernel,
        out_shape=jax.ShapeDtypeStruct((512, OUTC), bf16),
        in_specs=[SMEM] + [VMEM] * (len(xpieces) + len(wpieces) + 1),
        out_specs=VMEM,
        scratch_shapes=[
            pltpu.VMEM((KPAD, KW * OUTC), bf16),
            pltpu.VMEM((1024 + 2 * HALO, KPAD), bf16),
            *[pltpu.VMEM((256, 128), f32)] * 3,
        ],
        compiler_params=pltpu.CompilerParams(vmem_limit_bytes=48 * 1024 * 1024),
        cost_estimate=pl.CostEstimate(flops=6_000_000_000, bytes_accessed=9_000_000, transcendentals=400_000),
    )(pos, *xpieces, *wpieces, bias)


SCALE = HD ** (-0.5)
WIDE = 256
TOKENS = 1024
BLOCK = 256
NT = (((1,), (1,)), ((), ()))
TN = (((0,), (0,)), ((), ()))


def dot(a, b, dims=(((1,), (0,)), ((), ()))):
    return lax.dot_general(a, b, dims, preferred_element_type=f32)


def softmax_rows(q_block, keys):
    scores = dot(q_block, keys, NT) * SCALE
    exponent = jnp.exp(scores - jnp.max(scores, axis=-1, keepdims=True))
    return exponent * (1.0 / jnp.sum(exponent, axis=-1, keepdims=True))


def forward_kernel(pos_ref, *refs):
    feat_refs, refs = refs[:10], refs[10:]
    (gain_ref, z0, z1, z2, z3a, z3b, cot_ref) = refs[:7]
    (normed_ref, qkv_ref, dm_ref, partial_ref, own_ref, sent_ref, wo, feats, wq, mixed_ref, dv, dval, grads, outs) = refs[7:]
    c, x, y, z = (pos_ref[i] for i in range(4))
    for t in range(3):
        wq[:, t * WIDE + HD : (t + 1) * WIDE] = jnp.zeros((D, WIDE - HD), bf16)
    wo[:, HD:] = jnp.zeros((D, WIDE - HD), bf16)
    for ref, zstep, first in ((z0, 0, 0), (z1, 3, 0), (z2, 1, 0), (z3a, 2, 0), (z3b, 2, 2)):
        for k in range(ref.shape[0]):
            src_z, src_y = (z + zstep) % 4, (y + 4 - (first + k)) % 4
            rows = pl.ds(pl.multiple_of((((src_z // 2) * 4 + src_y) * 2 + src_z % 2) * 96, 96), 96)
            piece = ref[k]
            for t in range(3):
                wq[rows, t * WIDE : t * WIDE + HD] = piece[:, t * HD : (t + 1) * HD]
            wo[rows, :HD] = piece[:, 3 * HD :]

    for side in range(2):
        half = c if side == 0 else 1 - c
        for ref, step, first in zip(feat_refs[side * 5 : side * 5 + 5], (0, 3, 1, 2, 2), (0, 0, 0, 0, 256)):
            size = ref.shape[0]
            rows = pl.ds(pl.multiple_of(half * 512 + first, 256), size)
            lanes = pl.ds(pl.multiple_of(((x + step) % NX) * OUTC, 128), OUTC)
            feats[rows, lanes] = ref[...]
    own_ref[...] = feats[pl.ds(pl.multiple_of((c * NX + x) * 128, 128), 128), :]

    @pl.loop(0, TOKENS // BLOCK)
    def _(r):
        rows = pl.ds(pl.multiple_of(r * BLOCK, BLOCK), BLOCK)
        part = feats[rows, :].astype(f32)
        factor = lax.rsqrt(jnp.sum(part * part, axis=-1, keepdims=True) * (1.0 / D) + EPS)
        normed = (part * factor * gain_ref[...]).astype(bf16)
        normed_ref[rows, :] = normed
        qkv = dot(normed, wq[...]).astype(bf16)
        for t in range(3):
            qkv_ref[t, rows, :] = qkv[:, t * WIDE : (t + 1) * WIDE]

    @pl.loop(0, TOKENS // BLOCK)
    def _(r):
        rows = pl.ds(pl.multiple_of(r * BLOCK, BLOCK), BLOCK)
        weights = softmax_rows(qkv_ref[0, rows, :], qkv_ref[1]).astype(bf16)
        mixed = dot(weights, qkv_ref[2]).astype(bf16)
        mixed_ref[rows, :] = mixed
        partial_ref[rows, :] = dot(mixed, wo[...], NT).astype(bf16)
        d_mixed = dot(cot_ref[rows, :], wo[...]).astype(bf16)
        dm_ref[rows, :] = d_mixed
        d_value = dot(d_mixed, weights, TN)

        @pl.when(r == 0)
        def _():
            dv[...] = d_value

        @pl.when(r > 0)
        def _():
            dv[...] += d_value

    dval[...] = dv[...].T.astype(bf16)

    @pl.loop(0, 4)
    def _(n):
        lanes = pl.ds(pl.multiple_of(n * 384, 384), 384)
        grads[lanes, :] = dot(normed_ref[:, lanes], dval[...], TN)
        outs[:, lanes] = dot(mixed_ref[...], cot_ref[:, lanes], TN)[:HD]

    for d in range(16):
        sent_ref[d, :, :HD] = grads[d * 96 : (d + 1) * 96, :HD].astype(bf16)
        g, lane = d // 2, (d % 2) * 768
        packed = [outs[g * 24 : (g + 1) * 24, lane + j * HD : lane + (j + 1) * HD] for j in range(4)]
        sent_ref[d, :, HD:] = jnp.concatenate(packed, axis=0).astype(bf16)


def forward(pos, feats, gain, wpieces, cot):
    return pl.pallas_call(
        forward_kernel,
        out_shape=(
            jax.ShapeDtypeStruct((TOKENS, D), bf16),
            jax.ShapeDtypeStruct((3, TOKENS, WIDE), bf16),
            jax.ShapeDtypeStruct((TOKENS, WIDE), bf16),
            jax.ShapeDtypeStruct((TOKENS, D), bf16),
            jax.ShapeDtypeStruct((128, D), bf16),
            jax.ShapeDtypeStruct((16, 96, 2 * HD), bf16),
        ),
        in_specs=[SMEM] + [VMEM] * 17,
        out_specs=[VMEM] * 6,
        scratch_shapes=[
            pltpu.VMEM((D, WIDE), bf16),
            pltpu.VMEM((TOKENS, D), bf16),
            pltpu.VMEM((D, 3 * WIDE), bf16),
            pltpu.VMEM((TOKENS, WIDE), bf16),
            pltpu.VMEM((WIDE, TOKENS), f32),
            pltpu.VMEM((TOKENS, WIDE), bf16),
            pltpu.VMEM((D, WIDE), f32),
            pltpu.VMEM((HD, D), f32),
        ],
        compiler_params=pltpu.CompilerParams(vmem_limit_bytes=56 * 1024 * 1024),
        cost_estimate=pl.CostEstimate(flops=8_000_000_000, bytes_accessed=20_000_000, transcendentals=1_100_000),
    )(pos, *feats, gain, *wpieces, cot)


def backward_kernel(qkv_ref, dm_ref, normed_ref, sent_ref, dcat, dk, grads):
    @pl.loop(0, TOKENS // BLOCK)
    def _(r):
        rows = pl.ds(pl.multiple_of(r * BLOCK, BLOCK), BLOCK)
        q_block = qkv_ref[0, rows, :]
        weights = softmax_rows(q_block, qkv_ref[1])
        d_weights = dot(dm_ref[rows, :], qkv_ref[2], NT)
        centre = jnp.sum(weights * d_weights, axis=-1, keepdims=True)
        d_scores = (weights * (d_weights - centre) * SCALE).astype(bf16)
        dcat[rows, 0:HD] = dot(d_scores, qkv_ref[1]).astype(bf16)[:, :HD]
        d_key = dot(q_block, d_scores, TN)

        @pl.when(r == 0)
        def _():
            dk[...] = d_key

        @pl.when(r > 0)
        def _():
            dk[...] += d_key

    dcat[:, HD:] = dk[...].T.astype(bf16)[:, :HD]

    @pl.loop(0, 4)
    def _(n):
        lanes = pl.ds(pl.multiple_of(n * 384, 384), 384)
        grads[lanes, :] = dot(normed_ref[:, lanes], dcat[...], TN)

    for d in range(16):
        sent_ref[d] = grads[d * 96 : (d + 1) * 96, :].astype(bf16)


def backward(qkv, d_mixed, normed):
    return pl.pallas_call(
        backward_kernel,
        out_shape=jax.ShapeDtypeStruct((16, 96, 2 * HD), bf16),
        in_specs=[VMEM] * 3,
        out_specs=VMEM,
        scratch_shapes=[
            pltpu.VMEM((TOKENS, 2 * HD), bf16),
            pltpu.VMEM((WIDE, TOKENS), f32),
            pltpu.VMEM((D, 2 * HD), f32),
        ],
        compiler_params=pltpu.CompilerParams(vmem_limit_bytes=56 * 1024 * 1024),
        cost_estimate=pl.CostEstimate(flops=6_000_000_000, bytes_accessed=8_000_000, transcendentals=1_100_000),
    )(qkv, d_mixed, normed)


def total_kernel(parts_ref, out_ref):
    total = parts_ref[0].astype(f32)
    for g in range(1, 16):
        total = total + parts_ref[g].astype(f32)
    out_ref[...] = total.astype(bf16)


def total_parts(parts):
    return pl.pallas_call(
        total_kernel,
        out_shape=jax.ShapeDtypeStruct((96, 2 * HD), bf16),
        in_specs=[VMEM],
        out_specs=VMEM,
    )(parts)


def proj_kernel(heads_ref, out_ref):
    for h in range(8):
        for t in range(3):
            out_ref[t, :, h * HD : (h + 1) * HD] = heads_ref[h, :, t * HD : (t + 1) * HD].astype(f32)


def place_proj(heads):
    return pl.pallas_call(
        proj_kernel,
        out_shape=jax.ShapeDtypeStruct((3, 96, D), f32),
        in_specs=[VMEM],
        out_specs=VMEM,
    )(heads)


def out_kernel(pos_ref, own_ref, other_ref, out_ref):
    c, y, zh = pos_ref[0], pos_ref[2], pos_ref[3] // 2
    for ref, core in ((own_ref, c), (other_ref, 1 - c)):
        lanes = pl.ds(pl.multiple_of(core * 768, 768), 768)
        for step in range(2):
            for k in range(4):
                g = ((zh + step) % 2) * 4 + (y + 4 - k) % 4
                piece = [ref[step, k, j * 24 : (j + 1) * 24, :] for j in range(4)]
                rows = pl.ds(pl.multiple_of(g * 24, 8), 24)
                out_ref[rows, lanes] = jnp.concatenate(piece, axis=1).astype(f32)


def place_out(c, own, other):
    return pl.pallas_call(
        out_kernel,
        out_shape=jax.ShapeDtypeStruct((HD, D), f32),
        in_specs=[SMEM, VMEM, VMEM],
        out_specs=VMEM,
    )(c, own, other)


def lane_sources(zh, y, c, zl):
    lane = lax.iota(jnp.int32, KPAD)
    slot, j = lane // SLOT, lane % SLOT
    core = jnp.where(slot < 16, c, 1 - c)
    within = slot % 16
    zstep = within // 4
    ystep = within % 4
    z = zh * 2 + zl
    src_z = (z + jnp.where(zstep == 1, 3, jnp.where(zstep == 2, 1, jnp.where(zstep == 3, 2, 0)))) % 4
    src_y = (y + 4 - ystep) % 4
    plane = (((src_z // 2) * 4 + src_y) * 2 + core) * 2 + src_z % 2
    return jnp.where(j < GROUP, plane * GROUP + j, -1)


def lanes_kernel(block_ref, edge_ref, sources_ref, out_ref):
    for n in range(4):
        lanes = slice(n * 384, (n + 1) * 384)
        select = lax.broadcasted_iota(jnp.int32, (CIN, 384), 0) == sources_ref[:, lanes]
        select = jnp.where(select, 1.0, 0.0).astype(bf16)
        out_ref[0:256, lanes] = dot(block_ref[...], select).astype(bf16)
        out_ref[256:, lanes] = dot(edge_ref[...], select).astype(bf16)


def order_lanes(block, edge, sources):
    return pl.pallas_call(
        lanes_kernel,
        out_shape=jax.ShapeDtypeStruct((256 + HALO, KPAD), bf16),
        in_specs=[VMEM] * 3,
        out_specs=VMEM,
        compiler_params=pltpu.CompilerParams(vmem_limit_bytes=32 * 1024 * 1024),
        cost_estimate=pl.CostEstimate(flops=1_200_000_000, bytes_accessed=1_600_000, transcendentals=0),
    )(block, edge, sources)


def swap_axes(value):
    return lax.ppermute(value, ("c", "zl"), [(0, 0), (1, 2), (2, 1), (3, 3)])


def from_other_core(parts):
    return [lax.ppermute(p, "c", ring(2, 1)) for p in parts]


def per_device(sequence, conv_weight, conv_bias, norm_gain, proj_weight, out_weight, cotangent):
    zh, y, c, zl, x = (lax.axis_index(a) for a in ("zh", "y", "c", "zl", "x"))
    zring = ("zh", "zl")
    pos = jnp.stack([c, x, y, zh * 2 + zl])

    edge = jnp.where(zl == 0, sequence[0, -HALO:], sequence[0, :HALO])
    edge = lax.ppermute(edge, "zl", ring(2, 1))
    block = order_lanes(sequence[0], edge, lane_sources(zh, y, c, zl)[None])

    split = conv_weight.reshape(11, KW, NX, OUTC).transpose(2, 1, 0, 3)
    mine = jnp.zeros((NX, KW, 11, OUTC), bf16)
    for k in range(NX):
        piece = lax.dynamic_index_in_dim(split, (x + k) % NX, 0, keepdims=False)
        if k:
            piece = lax.ppermute(piece, "x", ring(NX, k))
        mine = lax.dynamic_update_index_in_dim(mine, piece, (x + NX - k) % NX, 0)
    mine = mine.transpose(1, 0, 2, 3).reshape(KW, GROUP, OUTC)
    mine = jnp.pad(mine, ((0, 0), (0, SLOT - GROUP), (0, 0)))

    later = jnp.concatenate([proj_weight.reshape(96, 3 * HD), out_weight.T], axis=1).reshape(48, D)
    later = swap_axes(jnp.concatenate([cotangent[0], later], axis=0))

    block, mine = lax.optimization_barrier((block, mine))
    ypieces = [mine] + [lax.ppermute(mine, "y", ring(4, k)) for k in (1, 2, 3)]
    *ypieces, block, later = lax.optimization_barrier((*ypieces, block, later))
    ypieces = jnp.stack(ypieces)
    head_w = later[128:].reshape(96, 768)
    xlow, xhigh = (lax.ppermute(block, "x", ring(4, k)) for k in (1, -1))
    zlow, zhigh = (lax.ppermute(ypieces, zring, ring(4, k)) for k in (1, -1))
    head_w = jnp.stack([head_w] + [lax.ppermute(head_w, "y", ring(4, k)) for k in (1, 2, 3)])
    xlow, xhigh, zlow, zhigh, head_w = lax.optimization_barrier((xlow, xhigh, zlow, zhigh, head_w))
    xfar = across(xlow, xhigh, "x", 128)
    zfar = across(zlow, zhigh, zring, 2)
    *xfar, za, zb, head_w, cot = lax.optimization_barrier((*xfar, *zfar, head_w, later[:128]))
    cot = lax.all_gather(cot, ("c", "x"), axis=0, tiled=True)
    xpieces = [block, xlow, xhigh, *xfar]
    wpieces = [ypieces, zlow, zhigh, za, zb]
    head_w = [head_w, *staged_ring(head_w, zring, 2)]
    bias = lax.dynamic_slice_in_dim(conv_bias, x * OUTC, OUTC)[None]

    feat = swap_axes(conv_pool(pos, xpieces, wpieces + from_other_core(wpieces), bias))
    feats = [feat, *staged_ring(feat, "x", 256)]
    feats = feats + from_other_core(feats)

    plane = ("zh", "y", "zl")
    normed, qkv, d_mixed, partial, own, first = forward(pos, feats, norm_gain[None], head_w, cot)
    attended = lax.psum_scatter(partial, ("c", "x"), scatter_dimension=0, tiled=True)
    first = lax.all_to_all(first, plane, 0, 0)
    second = backward(qkv, d_mixed, normed)
    first, second = lax.optimization_barrier((first, second))
    second = lax.all_to_all(second, plane, 0, 0)
    first = swap_axes(total_parts(first))
    rows = jnp.stack([first[:, HD:]] + [lax.ppermute(first[:, HD:], "y", ring(4, k)) for k in (1, 2, 3)])

    block_out = swap_axes((own.astype(f32) + attended.astype(f32)).astype(bf16))
    second, rows, block_out = lax.optimization_barrier((second, rows, block_out))
    second = swap_axes(total_parts(second))
    rows = jnp.stack([rows, lax.ppermute(rows, "zh", ring(2, 1))])
    proj = jnp.concatenate([second, first[:, :HD]], axis=1)
    heads = lax.all_to_all(jnp.broadcast_to(proj[None], (8, 96, 3 * HD)), ("zl", "x"), 0, 0)
    proj_grad = place_proj(heads).transpose(1, 0, 2)
    out_grad = place_out(pos, rows, lax.ppermute(rows, "c", ring(2, 1)))
    return (block_out[None], proj_grad, out_grad)


def solution(mesh):
    fine = Mesh(mesh.devices.reshape(2, 4, 2, 2, 4), ("zh", "y", "c", "zl", "x"))
    dp, seq = ("zh", "y", "c"), ("zl", "x")
    in_specs = (
        P(dp, seq, None),
        P(dp + seq, None, None),
        P(),
        P(),
        P(dp, None, seq),
        P(seq, dp),
        P(dp, seq, None),
    )
    out_specs = (P(dp, seq, None), P(dp, None, None), P(seq, None))
    return jax.shard_map(per_device, mesh=fine, in_specs=in_specs, out_specs=out_specs, check_vma=False)
```

time: 282 us -> 259 us (0.918)
  blocking collectives: 44 us -> 0 us
  starting transfers between devices: 39.9 us -> 77.4 us
  waiting for transfers between devices: 101 us -> 82.7 us
  Pallas kernels: 52.2 us -> 58.5 us
    ppermute x14 -> x38, waiting for transfers between devices: 9.85 us -> 68.9 us  [the longest x1 15.8 us: per_device(): rows = jnp.stack([rows, lax.ppermute(rows, 'zh', ring(2, 1))])]
    all_gather x2 -> x1, waiting for transfers between devices: 51.9 us -> 0.01 us  [per_device(): cot = lax.all_gather(cot, ('c', 'x'), axis=0, tiled=True)]
    all_to_all x2 -> x0, blocking collectives: 44 us -> none  [the longest x1 31.9 us: per_device(): proj, outs = total_parts(lax.all_to_all(both, ('zh', 'y'), 0, 0))]
    ppermute x14 -> x38, starting transfers between devices: 18.6 us -> 53.3 us  [the longest x5 17.1 us: swap_axes(): return lax.ppermute(value, ('c', 'zl'), [(0, 0), (1, 2), (2, 1), (3, 3)])]
    ppermute x2, waiting for transfers between devices: 27.5 us -> 2.22 us  [staged_ring(): high = lax.ppermute(block, axis, ring(4, -1))]
    pallas_call x1, Pallas kernels: 13.4 us -> 23 us  [forward(): pl.pallas_call(forward_kernel, out_shape=(jax.ShapeDtypeStruct((TOKENS, D...]
    slice x4 -> x11, local copies, waits for them, and re-layouts: 1.13 us -> 6.23 us  [the longest x4 2.59 us: across(): far_a = lax.ppermute(lax.slice_in_dim(low, 0, cut), axis, ring(4, 1))]
    all_to_all x2 -> x3, starting transfers between devices: 8.15 us -> 12.1 us  [the longest x1 4.82 us: per_device(): first = lax.all_to_all(first, plane, 0, 0)]
  transfers between devices with their start and end apart: 27 -> 51, of which waited for: 11 -> 22; matrix products, arithmetic and copies ran while one was open for 7% -> 5% of each run, Pallas kernels for 14% -> 12%
where the time goes in v2:
time: 259 us; the launch traced here: 258 us
  waiting for transfers between devices  82.7 us (32%)
  starting transfers between devices  77.4 us (30%)
  Pallas kernels  58.5 us (23%)
  local copies, waits for them, and re-layouts  19.8 us (8%)
  between operations  14.8 us (6%)
  other arithmetic  5.23 us (2%)
    pallas_call x1, Pallas kernels, forward(): pl.pallas_call(forward_kernel, out_shape=(jax.ShapeDtypeStruct((TOKENS, D...  23 us
    ppermute x5, starting transfers between devices, swap_axes(): return lax.ppermute(value, ('c', 'zl'), [(0, 0), (1, 2), (2, 1), (3, 3)])  17.1 us
    ppermute x1, waiting for transfers between devices, per_device(): rows = jnp.stack([rows, lax.ppermute(rows, 'zh', ring(2, 1))])  15.8 us
    ppermute x3, waiting for transfers between devices, per_device(): lax.ppermute(head_w, 'y', ring(4, k))  15.7 us
    pallas_call x1, Pallas kernels, conv_pool(): pl.pallas_call(conv_kernel, out_shape=jax.ShapeDtypeStruct((512, OUTC), b...  12 us
    pallas_call x1, Pallas kernels, backward(): pl.pallas_call(backward_kernel, out_shape=jax.ShapeDtypeStruct((16, 96, 2...  11.7 us
    ppermute x3, waiting for transfers between devices, per_device(): ypieces = [mine] + [lax.ppermute(mine, 'y', ring(4, k)) for k in (1, 2, 3)]  11 us
    ppermute x10, starting transfers between devices, from_other_core(): return [lax.ppermute(p, 'c', ring(2, 1)) for p in parts]  10.7 us
  transfers between devices with their start and end apart: 51, of which 22 were waited for; matrix products, arithmetic and copies ran while one was open for 5% of the time, Pallas kernels for 12%

profile of v2, /device:TPU:1, one launch (start us, length us, event | category | flops | bytes accessed | tf_op | source)
XLA Modules:
  0.0 258.5 jit_solution(10132357201728036703)
XLA Ops:
  7.2 0.8 select_bitcast_fusion
  8.1 2.5 collective-permute-start
  10.6 1.1 reshape.357
  12.1 2.8 %collective-permute-start.2 = (bf16[5,11,384]{2,1,0:T(8,128)(2,1)S(1)}, bf16[5,11,384]{2,1,0:T(8,128)(2,1)S(1)}, u32[]{:S(2)}, u32[]{:S(2)}) collective-permute-start(bf16[5,11,384]{2,1,0:T(8,128)(2,1)S(1)} %bitcast.68), channel_id=1, source_target_pairs={{0,2},{1,3},{2,0},{3,1},{4,6},{5,7},{6,4},{7,5},{8,10},{9,11},{10,... | collective-permute-start | bytes 126728 | tf_op jit(solution)/shard_map/ppermute | solution.py:380
  15.4 2.4 collective-permute-start.3
  18.2 0.8 pad_maximum_fusion.2
  19.1 3.4 %collective-permute-start.7 = (bf16[176,1536]{1,0:T(8,128)(2,1)}, bf16[176,1536]{1,0:T(8,128)(2,1)S(1)}, u32[]{:S(2)}, u32[]{:S(2)}) collective-permute-start(bf16[176,1536]{1,0:T(8,128)(2,1)} %pad_maximum_fusion.2), channel_id=1, source_target_pairs={{0,0},{4,8},{8,4},{12,12},{1,1},{5,9},{9,5},{13,13},{2,2},{6,10},{... | collective-permute-start | bytes 1622024 | tf_op jit(solution)/shard_map/ppermute | solution.py:359
  23.0 2.6 %shard_map.94.refs_0_ = bf16[272,1536]{1,0:T(8,128)(2,1)S(1)} custom-call(bf16[256,1408]{1,0:T(8,128)(2,1)S(1)} %bitcast.54, bf16[16,1408]{1,0:T(8,128)(2,1)S(1)} %collective-permute-done.edge_ref, s32[1,1536]{1,0:T(1,128)S(1)} %compare_select_fusion.10.sources_ref), custom_call_target="tpu_custom_call" | custom-call | flops 1200000000 | bytes 1600000 | tf_op jit(solution)/shard_map/pallas_call | solution.py:348
  25.6 2.8 %collective-permute-start.6 = (bf16[5,48,384]{2,1,0:T(8,128)(2,1)S(1)}, bf16[5,48,384]{2,1,0:T(8,128)(2,1)S(1)}, u32[]{:S(2)}, u32[]{:S(2)}) collective-permute-start(bf16[5,48,384]{2,1,0:T(8,128)(2,1)S(1)} %pad.4), channel_id=1, source_target_pairs={{0,48},{16,0},{32,16},{48,32},{1,49},{17,1},{33,17},{49,33},{2,50}... | collective-permute-start | bytes 552968 | tf_op jit(solution)/shard_map/ppermute | solution.py:389
  29.5 6.8 %collective-permute-done.6 = bf16[5,48,384]{2,1,0:T(8,128)(2,1)S(1)} collective-permute-done((bf16[5,48,384]{2,1,0:T(8,128)(2,1)S(1)}, bf16[5,48,384]{2,1,0:T(8,128)(2,1)S(1)}, u32[]{:S(2)}, u32[]{:S(2)}) %collective-permute-start.6) | collective-permute-done | bytes 184352 | tf_op jit(solution)/shard_map/ppermute | solution.py:389
  36.3 4.2 %collective-permute-done.4 = bf16[5,48,384]{2,1,0:T(8,128)(2,1)S(1)} collective-permute-done((bf16[5,48,384]{2,1,0:T(8,128)(2,1)S(1)}, bf16[5,48,384]{2,1,0:T(8,128)(2,1)S(1)}, u32[]{:S(2)}, u32[]{:S(2)}) %collective-permute-start.4) | collective-permute-done | bytes 184352 | tf_op jit(solution)/shard_map/ppermute | solution.py:389
  40.5 1.5 collective-permute-start.8
  42.1 1.5 collective-permute-start.10
  43.6 0.9 slice.47
  45.2 4.6 %collective-permute-done.14 = bf16[96,768]{1,0:T(8,128)(2,1)S(1)} collective-permute-done((bf16[96,768]{1,0:T(8,128)(2,1)}, bf16[96,768]{1,0:T(8,128)(2,1)S(1)}, u32[]{:S(2)}, u32[]{:S(2)}) %collective-permute-start.14) | collective-permute-done | bytes 147488 | tf_op jit(solution)/shard_map/ppermute | solution.py:395
  50.2 5.4 %collective-permute-done.13 = bf16[96,768]{1,0:T(8,128)(2,1)S(1)} collective-permute-done((bf16[96,768]{1,0:T(8,128)(2,1)}, bf16[96,768]{1,0:T(8,128)(2,1)S(1)}, u32[]{:S(2)}, u32[]{:S(2)}) %collective-permute-start.13) | collective-permute-done | bytes 147488 | tf_op jit(solution)/shard_map/ppermute | solution.py:395
  56.3 5.7 %collective-permute-done.12 = bf16[96,768]{1,0:T(8,128)(2,1)} collective-permute-done((bf16[96,768]{1,0:T(8,128)(2,1)}, bf16[96,768]{1,0:T(8,128)(2,1)}, u32[]{:S(2)}, u32[]{:S(2)}) %collective-permute-start.12) | collective-permute-done | bytes 147488 | tf_op jit(solution)/shard_map/ppermute | solution.py:395
  62.0 1.9 pad_maximum_fusion.1.refs_11_
  63.9 1.0 slice.49
  65.0 1.2 collective-permute-start.16
  66.2 1.8 slice.48
  69.8 2.1 collective-permute-start.18
  72.8 4.1 %collective-permute-done.18.refs_9_ = bf16[2,5,48,384]{3,2,1,0:T(8,128)(2,1)} collective-permute-done((bf16[2,5,48,384]{3,2,1,0:T(8,128)(2,1)}, bf16[2,5,48,384]{3,2,1,0:T(8,128)(2,1)}, u32[]{:S(2)}, u32[]{:S(2)}) %collective-permute-start.18) | collective-permute-done | bytes 368672 | tf_op jit(solution)/shard_map/ppermute | solution.py:32
  76.9 3.2 %collective-permute-done.17.refs_8_ = bf16[2,5,48,384]{3,2,1,0:T(8,128)(2,1)} collective-permute-done((bf16[2,5,48,384]{3,2,1,0:T(8,128)(2,1)}, bf16[2,5,48,384]{3,2,1,0:T(8,128)(2,1)}, u32[]{:S(2)}, u32[]{:S(2)}) %collective-permute-start.17) | collective-permute-done | bytes 368672 | tf_op jit(solution)/shard_map/ppermute | solution.py:31
  80.8 6.2 %collective-permute-start.19 = (bf16[4,5,48,384]{3,2,1,0:T(8,128)(2,1)S(1)}, bf16[4,5,48,384]{3,2,1,0:T(8,128)(2,1)S(1)}, u32[]{:S(2)}, u32[]{:S(2)}) collective-permute-start(bf16[4,5,48,384]{3,2,1,0:T(8,128)(2,1)S(1)} %pad_maximum_fusion.refs_5_), channel_id=1, source_target_pairs={{0,8},{8,0},{1,9},{9,1},{2,10},{10,2},{3,11},{11,3},{4,12},{12,4},... | collective-permute-start | bytes 2211848 | tf_op jit(solution)/shard_map/ppermute | solution.py:363
  88.8 1.0 collective-permute-done.19.refs_10_
  92.3 1.1 copy-done.4
  93.3 12.0 %shard_map.95 = bf16[512,384]{1,0:T(8,128)(2,1)S(1)} custom-call(s32[4]{0:T(128)S(1)} %pad_add_fusion.pos_ref, bf16[272,1536]{1,0:T(8,128)(2,1)} %copy-done.2, bf16[272,1536]{1,0:T(8,128)(2,1)} %collective-permute-done.8.refs_1_, bf16[272,1536]{1,0:T(8,128)(2,1)} %collective-permute-done.9.refs_2_, bf16[128,1536]{1,0:T(8,128)(2,1)S(1)} %copy-done.4, ...), custom_call_target="tpu_custom_call" | custom-call | flops 6000000000 | bytes 9000000 | tf_op jit(solution)/shard_map/pallas_call | solution.py:93
  105.3 1.9 collective-permute-start.24
  107.3 7.5 %collective-permute-done.24.refs_0_ = bf16[512,384]{1,0:T(8,128)(2,1)S(1)} collective-permute-done((bf16[512,384]{1,0:T(8,128)(2,1)S(1)}, bf16[512,384]{1,0:T(8,128)(2,1)S(1)}, u32[]{:S(2)}, u32[]{:S(2)}) %collective-permute-start.24) | collective-permute-done | bytes 393248 | tf_op jit(solution)/shard_map/ppermute | solution.py:359
  114.7 2.9 %collective-permute-start.26 = (bf16[512,384]{1,0:T(8,128)(2,1)S(1)}, bf16[512,384]{1,0:T(8,128)(2,1)S(1)}, u32[]{:S(2)}, u32[]{:S(2)}) collective-permute-start(bf16[512,384]{1,0:T(8,128)(2,1)S(1)} %collective-permute-done.24.refs_0_), channel_id=1, source_target_pairs={{0,3},{1,0},{2,1},{3,2},{4,7},{5,4},{6,5},{7,6},{8,11},{9,8},{10,9... | collective-permute-start | bytes 1179656 | tf_op jit(solution)/shard_map/ppermute | solution.py:38
  117.9 1.5 collective-permute-start.36
  119.4 0.8 collective-permute-start.29
  120.2 2.2 collective-permute-done.26.refs_2_
  122.4 3.2 %collective-permute-start.28 = (bf16[256,384]{1,0:T(8,128)(2,1)S(1)}, bf16[256,384]{1,0:T(8,128)(2,1)S(1)}, u32[]{:S(2)}, u32[]{:S(2)}) collective-permute-start(bf16[256,384]{1,0:T(8,128)(2,1)S(1)} %slice.60), channel_id=1, source_target_pairs={{0,3},{1,0},{2,1},{3,2},{4,7},{5,4},{6,5},{7,6},{8,11},{9,8},{10,9... | collective-permute-start | bytes 589832 | tf_op jit(solution)/shard_map/ppermute | solution.py:32
  126.1 2.5 collective-permute-start.30
  128.7 3.3 %collective-permute-done.27.refs_3_ = bf16[256,384]{1,0:T(8,128)(2,1)S(1)} collective-permute-done((bf16[256,384]{1,0:T(8,128)(2,1)S(1)}, bf16[256,384]{1,0:T(8,128)(2,1)S(1)}, u32[]{:S(2)}, u32[]{:S(2)}) %collective-permute-start.27) | collective-permute-done | bytes 196640 | tf_op jit(solution)/shard_map/ppermute | solution.py:31
  134.9 23.0 %shard_map.96 = (bf16[1024,1536]{1,0:T(8,128)(2,1)}, bf16[3,1024,256]{2,1,0:T(8,128)(2,1)}, bf16[1024,256]{1,0:T(8,128)(2,1)}, bf16[1024,1536]{1,0:T(8,128)(2,1)...) custom-call(s32[4]{0:T(128)} %copy-done.1, bf16[512,384]{1,0:T(8,128)(2,1)} %copy-done.22, ...), custom_call_target="tpu_custom_call" | custom-call | flops 8000000000 | bytes 20000000 | tf_op jit(solution)/shard_map/pallas_call | solution.py:198
  157.9 4.8 %all-to-all-start = ((bf16[16,96,384]{2,1,0:T(8,128)(2,1)}), bf16[16,96,384]{2,1,0:T(8,128)(2,1)S(1)}, u32[]{:S(2)}, u32[]{:S(2)}) async-start(bf16[16,96,384]{2,1,0:T(8,128)(2,1)} %get-tuple-element.52), calls=%async_computation | async-start | bytes 2359296 | tf_op jit(solution)/shard_map/all_to_all | solution.py:413
  162.7 11.7 %shard_map.97 = bf16[16,96,384]{2,1,0:T(8,128)(2,1)} custom-call(bf16[3,1024,256]{2,1,0:T(8,128)(2,1)} %get-tuple-element.53.qkv_ref, bf16[1024,256]{1,0:T(8,128)(2,1)} %get-tuple-element.54.dm_ref, bf16[1024,1536]{1,0:T(8,128)(2,1)} %get-tuple-element.55.normed_ref), custom_call_target="tpu_custom_call" | custom-call | flops 6000000000 | bytes 8000000 | tf_op jit(solution)/shard_map/pallas_call | solution.py:257
  174.4 7.9 %all-to-all-done.parts_ref = bf16[16,96,384]{2,1,0:T(8,128)(2,1)S(1)} async-done(((bf16[16,96,384]{2,1,0:T(8,128)(2,1)}), bf16[16,96,384]{2,1,0:T(8,128)(2,1)S(1)}, u32[]{:S(2)}, u32[]{:S(2)}) %all-to-all-start) | async-done | bytes 1179680 | tf_op jit(solution)/shard_map/all_to_all | solution.py:413
  182.4 1.0 copy-done.6
  183.4 3.7 %all-to-all-start.1 = ((bf16[16,96,384]{2,1,0:T(8,128)(2,1)}), bf16[16,96,384]{2,1,0:T(8,128)(2,1)S(1)}, u32[]{:S(2)}, u32[]{:S(2)}) async-start(bf16[16,96,384]{2,1,0:T(8,128)(2,1)} %shard_map.97), calls=%async_computation.1 | async-start | bytes 2359296 | tf_op jit(solution)/shard_map/all_to_all | solution.py:416
  187.1 2.1 shard_map.98
  189.2 4.4 %collective-permute-start.38 = (bf16[96,384]{1,0:T(8,128)(2,1)}, bf16[96,384]{1,0:T(8,128)(2,1)S(1)}, u32[]{:S(2)}, u32[]{:S(2)}) collective-permute-start(bf16[96,384]{1,0:T(8,128)(2,1)} %shard_map.98), channel_id=1, source_target_pairs={{0,0},{4,8},{8,4},{12,12},{1,1},{5,9},{9,5},{13,13},{2,2},{6,10},{... | collective-permute-start | bytes 221192 | tf_op jit(solution)/shard_map/ppermute | solution.py:359
  193.7 3.4 %reduce-scatter.2.cloned.1.call-done = bf16[128,1536]{1,0:T(8,128)(2,1)} async-done(((bf16[1024,1536]{1,0:T(8,128)(2,1)}), bf16[128,1536]{1,0:T(8,128)(2,1)}) %reduce-scatter.2.cloned.1.call-update) | async-done | bytes 393232 | tf_op jit(solution)/shard_map/reduce_scatter | solution.py:412
  197.1 1.1 add_convert_fusion
  198.2 3.3 %collective-permute-start.42 = (bf16[128,1536]{1,0:T(8,128)(2,1)S(1)}, bf16[128,1536]{1,0:T(8,128)(2,1)S(1)}, u32[]{:S(2)}, u32[]{:S(2)}) collective-permute-start(bf16[128,1536]{1,0:T(8,128)(2,1)S(1)} %add_convert_fusion), channel_id=1, source_target_pairs={{0,0},{4,8},{8,4},{12,12},{1,1},{5,9},{9,5},{13,13},{2,2},{6,10},{... | collective-permute-start | bytes 1179656 | tf_op jit(solution)/shard_map/ppermute | solution.py:359
  201.6 3.7 %collective-permute-start.40 = (bf16[96,192]{1,0:T(8,128)(2,1)S(1)}, bf16[96,192]{1,0:T(8,128)(2,1)S(1)}, u32[]{:S(2)}, u32[]{:S(2)}) collective-permute-start(bf16[96,192]{1,0:T(8,128)(2,1)S(1)} %get-tuple-element.69), channel_id=1, source_target_pairs={{0,32},{16,48},{32,0},{48,16},{1,33},{17,49},{33,1},{49,17},{2,34}... | collective-permute-start | bytes 110600 | tf_op jit(solution)/shard_map/ppermute | solution.py:418
  205.3 1.1 collective-permute-start.39
  206.4 1.6 collective-permute-start.41
  208.0 1.5 collective-permute-done.39
  209.6 1.0 copy-done.5
  210.6 2.1 shard_map.99
  212.6 4.1 %collective-permute-start.43 = (bf16[96,384]{1,0:T(8,128)(2,1)}, bf16[96,384]{1,0:T(8,128)(2,1)S(1)}, u32[]{:S(2)}, u32[]{:S(2)}) collective-permute-start(bf16[96,384]{1,0:T(8,128)(2,1)} %shard_map.99), channel_id=1, source_target_pairs={{0,0},{4,8},{8,4},{12,12},{1,1},{5,9},{9,5},{13,13},{2,2},{6,10},{... | collective-permute-start | bytes 221192 | tf_op jit(solution)/shard_map/ppermute | solution.py:359
  216.7 2.2 collective-permute-done.43
  219.0 1.0 broadcast_in_dim.56
  220.0 3.6 %all-to-all-start.2 = ((bf16[8,96,576]{2,1,0:T(8,128)(2,1)}), bf16[8,96,576]{2,1,0:T(8,128)(2,1)S(1)}, u32[]{:S(2)}, u32[]{:S(2)}) async-start(bf16[8,96,576]{2,1,0:T(8,128)(2,1)} %broadcast_in_dim.56), calls=%async_computation.3 | async-start | bytes 1966080 | tf_op jit(solution)/shard_map/all_to_all | solution.py:425
  223.5 2.6 %collective-permute-start.44 = (bf16[4,96,192]{2,1,0:T(8,128)(2,1)S(1)}, bf16[4,96,192]{2,1,0:T(8,128)(2,1)S(1)}, u32[]{:S(2)}, u32[]{:S(2)}) collective-permute-start(bf16[4,96,192]{2,1,0:T(8,128)(2,1)S(1)} %pad_maximum_fusion.5), channel_id=1, source_target_pairs={{0,64},{64,0},{1,65},{65,1},{2,66},{66,2},{3,67},{67,3},{4,68},{68... | collective-permute-start | bytes 442376 | tf_op jit(solution)/shard_map/ppermute | solution.py:423
  226.1 15.8 %collective-permute-done.44 = bf16[4,96,192]{2,1,0:T(8,128)(2,1)S(1)} collective-permute-done((bf16[4,96,192]{2,1,0:T(8,128)(2,1)S(1)}, bf16[4,96,192]{2,1,0:T(8,128)(2,1)S(1)}, u32[]{:S(2)}, u32[]{:S(2)}) %collective-permute-start.44) | collective-permute-done | bytes 147488 | tf_op jit(solution)/shard_map/ppermute | solution.py:423
  242.8 1.3 collective-permute-done.45.other_ref
  244.9 2.3 shard_map.101
  247.3 0.9 copy-done.7
  248.2 2.6 %shard_map.100 = f32[3,96,1536]{2,1,0:T(8,128)} custom-call(bf16[8,96,576]{2,1,0:T(8,128)(2,1)} %copy-done.7), custom_call_target="tpu_custom_call" | custom-call | tf_op jit(solution)/shard_map/pallas_call | solution.py:295
  (156 shorter events, 18.3 us)
Async XLA Ops:
  7.2 10.6 %copy-start.17 = (bf16[96,3,192]{2,0,1:T(8,128)(2,1)S(1)}, bf16[96,3,192]{2,0,1:T(8,128)(2,1)}, u32[]{:S(2)}) copy-start(bf16[96,3,192]{2,0,1:T(8,128)(2,1)} %param.11) | copy-start | bytes 331780
  7.2 10.8 %copy-start.20 = (bf16[192,96]{1,0:T(8,128)(2,1)S(1)}, bf16[192,96]{1,0:T(8,128)(2,1)}, u32[]{:S(2)}) copy-start(bf16[192,96]{1,0:T(8,128)(2,1)} %param.12) | copy-start | bytes 110596
  7.2 126.9 %all-gather.2.cloned.1.call-start = ((), (), s32[]{:S(2)}) async-start(), calls=%async_computation.4 | async-start | bytes 3538944 | tf_op jit(solution)/shard_map/all_gather | solution.py:400
  8.1 14.9 %collective-permute-start = (bf16[16,1408]{1,0:T(8,128)(2,1)S(1)}, bf16[16,1408]{1,0:T(8,128)(2,1)S(1)}, u32[]{:S(2)}, u32[]{:S(2)}) collective-permute-start(bf16[16,1408]{1,0:T(8,128)(2,1)S(1)} %select_bitcast_fusion), channel_id=1, source_target_pairs={{0,4},{4,0},{1,5},{5,1},{2,6},{6,2},{3,7},{7,3},{8,12},{12,8},{9,1... | collective-permute-start | bytes 135176 | tf_op jit(solution)/shard_map/ppermute | solution.py:372
  12.1 10.7 %collective-permute-start.2 = (bf16[5,11,384]{2,1,0:T(8,128)(2,1)S(1)}, bf16[5,11,384]{2,1,0:T(8,128)(2,1)S(1)}, u32[]{:S(2)}, u32[]{:S(2)}) collective-permute-start(bf16[5,11,384]{2,1,0:T(8,128)(2,1)S(1)} %bitcast.68), channel_id=1, source_target_pairs={{0,2},{1,3},{2,0},{3,1},{4,6},{5,7},{6,4},{7,5},{8,10},{9,11},{10,... | collective-permute-start | bytes 126728 | tf_op jit(solution)/shard_map/ppermute | solution.py:380
  15.0 7.8 %collective-permute-start.1 = (bf16[5,11,384]{2,1,0:T(8,128)(2,1)S(1)}, bf16[5,11,384]{2,1,0:T(8,128)(2,1)S(1)}, u32[]{:S(2)}, u32[]{:S(2)}) collective-permute-start(bf16[5,11,384]{2,1,0:T(8,128)(2,1)S(1)} %bitcast.70), channel_id=1, source_target_pairs={{0,1},{1,2},{2,3},{3,0},{4,5},{5,6},{6,7},{7,4},{8,9},{9,10},{10,1... | collective-permute-start | bytes 126728 | tf_op jit(solution)/shard_map/ppermute | solution.py:380
  15.4 7.5 %collective-permute-start.3 = (bf16[5,11,384]{2,1,0:T(8,128)(2,1)S(1)}, bf16[5,11,384]{2,1,0:T(8,128)(2,1)S(1)}, u32[]{:S(2)}, u32[]{:S(2)}) collective-permute-start(bf16[5,11,384]{2,1,0:T(8,128)(2,1)S(1)} %bitcast.69), channel_id=1, source_target_pairs={{0,3},{1,0},{2,1},{3,2},{4,7},{5,4},{6,5},{7,6},{8,11},{9,8},{10,9... | collective-permute-start | bytes 126728 | tf_op jit(solution)/shard_map/ppermute | solution.py:380
  19.1 21.4 %collective-permute-start.7 = (bf16[176,1536]{1,0:T(8,128)(2,1)}, bf16[176,1536]{1,0:T(8,128)(2,1)S(1)}, u32[]{:S(2)}, u32[]{:S(2)}) collective-permute-start(bf16[176,1536]{1,0:T(8,128)(2,1)} %pad_maximum_fusion.2), channel_id=1, source_target_pairs={{0,0},{4,8},{8,4},{12,12},{1,1},{5,9},{9,5},{13,13},{2,2},{6,10},{... | collective-permute-start | bytes 1622024 | tf_op jit(solution)/shard_map/ppermute | solution.py:359
  25.6 30.6 %copy-start.2 = (bf16[272,1536]{1,0:T(8,128)(2,1)}, bf16[272,1536]{1,0:T(8,128)(2,1)S(1)}, u32[]{:S(2)}) copy-start(bf16[272,1536]{1,0:T(8,128)(2,1)S(1)} %shard_map.94.refs_0_) | copy-start | bytes 2506756
  25.6 10.6 %collective-permute-start.6 = (bf16[5,48,384]{2,1,0:T(8,128)(2,1)S(1)}, bf16[5,48,384]{2,1,0:T(8,128)(2,1)S(1)}, u32[]{:S(2)}, u32[]{:S(2)}) collective-permute-start(bf16[5,48,384]{2,1,0:T(8,128)(2,1)S(1)} %pad.4), channel_id=1, source_target_pairs={{0,48},{16,0},{32,16},{48,32},{1,49},{17,1},{33,17},{49,33},{2,50}... | collective-permute-start | bytes 552968 | tf_op jit(solution)/shard_map/ppermute | solution.py:389
  28.4 7.8 %collective-permute-start.5 = (bf16[5,48,384]{2,1,0:T(8,128)(2,1)S(1)}, bf16[5,48,384]{2,1,0:T(8,128)(2,1)S(1)}, u32[]{:S(2)}, u32[]{:S(2)}) collective-permute-start(bf16[5,48,384]{2,1,0:T(8,128)(2,1)S(1)} %pad.4), channel_id=1, source_target_pairs={{0,32},{16,48},{32,0},{48,16},{1,33},{17,49},{33,1},{49,17},{2,34}... | collective-permute-start | bytes 552968 | tf_op jit(solution)/shard_map/ppermute | solution.py:389
  28.8 11.7 %collective-permute-start.4 = (bf16[5,48,384]{2,1,0:T(8,128)(2,1)S(1)}, bf16[5,48,384]{2,1,0:T(8,128)(2,1)S(1)}, u32[]{:S(2)}, u32[]{:S(2)}) collective-permute-start(bf16[5,48,384]{2,1,0:T(8,128)(2,1)S(1)} %pad.4), channel_id=1, source_target_pairs={{0,16},{16,32},{32,48},{48,0},{1,17},{17,33},{33,49},{49,1},{2,18}... | collective-permute-start | bytes 552968 | tf_op jit(solution)/shard_map/ppermute | solution.py:389
  40.5 23.5 %collective-permute-start.9 = (bf16[272,1536]{1,0:T(8,128)(2,1)S(1)}, bf16[272,1536]{1,0:T(8,128)(2,1)}, u32[]{:S(2)}, u32[]{:S(2)}) collective-permute-start(bf16[272,1536]{1,0:T(8,128)(2,1)S(1)} %shard_map.94.refs_0_), channel_id=1, source_target_pairs={{0,3},{1,0},{2,1},{3,2},{4,7},{5,4},{6,5},{7,6},{8,11},{9,8},{10,9... | collective-permute-start | bytes 2506760 | tf_op jit(solution)/shard_map/ppermute | solution.py:393
  40.5 23.5 %collective-permute-start.8 = (bf16[272,1536]{1,0:T(8,128)(2,1)S(1)}, bf16[272,1536]{1,0:T(8,128)(2,1)}, u32[]{:S(2)}, u32[]{:S(2)}) collective-permute-start(bf16[272,1536]{1,0:T(8,128)(2,1)S(1)} %shard_map.94.refs_0_), channel_id=1, source_target_pairs={{0,1},{1,2},{2,3},{3,0},{4,5},{5,6},{6,7},{7,4},{8,9},{9,10},{10,1... | collective-permute-start | bytes 2506760 | tf_op jit(solution)/shard_map/ppermute | solution.py:393
  42.0 21.9 %collective-permute-start.11 = (bf16[4,5,48,384]{3,2,1,0:T(8,128)(2,1)S(1)}, bf16[4,5,48,384]{3,2,1,0:T(8,128)(2,1)S(1)}, u32[]{:S(2)}, u32[]{:S(2)}) collective-permute-start(bf16[4,5,48,384]{3,2,1,0:T(8,128)(2,1)S(1)} %pad_maximum_fusion.refs_5_), channel_id=1, source_target_pairs={{0,68},{4,0},{64,4},{68,64},{1,69},{5,1},{65,5},{69,65},{2,70},{6,... | collective-permute-start | bytes 2211848 | tf_op jit(solution)/shard_map/ppermute | solution.py:394
  42.1 21.8 %collective-permute-start.10 = (bf16[4,5,48,384]{3,2,1,0:T(8,128)(2,1)S(1)}, bf16[4,5,48,384]{3,2,1,0:T(8,128)(2,1)S(1)}, u32[]{:S(2)}, u32[]{:S(2)}) collective-permute-start(bf16[4,5,48,384]{3,2,1,0:T(8,128)(2,1)S(1)} %pad_maximum_fusion.refs_5_), channel_id=1, source_target_pairs={{0,4},{4,64},{64,68},{68,0},{1,5},{5,65},{65,69},{69,1},{2,6},{6,6... | collective-permute-start | bytes 2211848 | tf_op jit(solution)/shard_map/ppermute | solution.py:394
  45.2 4.6 %collective-permute-start.14 = (bf16[96,768]{1,0:T(8,128)(2,1)}, bf16[96,768]{1,0:T(8,128)(2,1)S(1)}, u32[]{:S(2)}, u32[]{:S(2)}) collective-permute-start(bf16[96,768]{1,0:T(8,128)(2,1)} %reshape.361), channel_id=1, source_target_pairs={{0,48},{16,0},{32,16},{48,32},{1,49},{17,1},{33,17},{49,33},{2,50}... | collective-permute-start | bytes 442376 | tf_op jit(solution)/shard_map/ppermute | solution.py:395
  49.8 5.7 %collective-permute-start.13 = (bf16[96,768]{1,0:T(8,128)(2,1)}, bf16[96,768]{1,0:T(8,128)(2,1)S(1)}, u32[]{:S(2)}, u32[]{:S(2)}) collective-permute-start(bf16[96,768]{1,0:T(8,128)(2,1)} %reshape.361), channel_id=1, source_target_pairs={{0,32},{16,48},{32,0},{48,16},{1,33},{17,49},{33,1},{49,17},{2,34}... | collective-permute-start | bytes 442376 | tf_op jit(solution)/shard_map/ppermute | solution.py:395
  56.2 5.8 %collective-permute-start.12 = (bf16[96,768]{1,0:T(8,128)(2,1)}, bf16[96,768]{1,0:T(8,128)(2,1)}, u32[]{:S(2)}, u32[]{:S(2)}) collective-permute-start(bf16[96,768]{1,0:T(8,128)(2,1)} %reshape.361), channel_id=1, source_target_pairs={{0,16},{16,32},{32,48},{48,0},{1,17},{17,33},{33,49},{49,1},{2,18}... | collective-permute-start | bytes 442376 | tf_op jit(solution)/shard_map/ppermute | solution.py:395
  65.0 15.1 %collective-permute-start.16 = (bf16[144,1536]{1,0:T(8,128)(2,1)S(1)}, bf16[144,1536]{1,0:T(8,128)(2,1)S(1)}, u32[]{:S(2)}, u32[]{:S(2)}) collective-permute-start(bf16[144,1536]{1,0:T(8,128)(2,1)S(1)} %slice.49), channel_id=1, source_target_pairs={{0,3},{1,0},{2,1},{3,2},{4,7},{5,4},{6,5},{7,6},{8,11},{9,8},{10,9... | collective-permute-start | bytes 1327112 | tf_op jit(solution)/shard_map/ppermute | solution.py:32
  68.0 12.1 %collective-permute-start.15 = (bf16[128,1536]{1,0:T(8,128)(2,1)}, bf16[128,1536]{1,0:T(8,128)(2,1)S(1)}, u32[]{:S(2)}, u32[]{:S(2)}) collective-permute-start(bf16[128,1536]{1,0:T(8,128)(2,1)} %slice.48), channel_id=1, source_target_pairs={{0,1},{1,2},{2,3},{3,0},{4,5},{5,6},{6,7},{7,4},{8,9},{9,10},{10,1... | collective-permute-start | bytes 1179656 | tf_op jit(solution)/shard_map/ppermute | solution.py:31
  69.8 7.0 %collective-permute-start.18 = (bf16[2,5,48,384]{3,2,1,0:T(8,128)(2,1)}, bf16[2,5,48,384]{3,2,1,0:T(8,128)(2,1)}, u32[]{:S(2)}, u32[]{:S(2)}) collective-permute-start(bf16[2,5,48,384]{3,2,1,0:T(8,128)(2,1)} %slice.51), channel_id=1, source_target_pairs={{0,68},{4,0},{64,4},{68,64},{1,69},{5,1},{65,5},{69,65},{2,70},{6,... | collective-permute-start | bytes 1105928 | tf_op jit(solution)/shard_map/ppermute | solution.py:32
  72.0 8.1 %collective-permute-start.17 = (bf16[2,5,48,384]{3,2,1,0:T(8,128)(2,1)}, bf16[2,5,48,384]{3,2,1,0:T(8,128)(2,1)}, u32[]{:S(2)}, u32[]{:S(2)}) collective-permute-start(bf16[2,5,48,384]{3,2,1,0:T(8,128)(2,1)} %slice.50), channel_id=1, source_target_pairs={{0,4},{4,64},{64,68},{68,0},{1,5},{5,65},{65,69},{69,1},{2,6},{6,6... | collective-permute-start | bytes 1105928 | tf_op jit(solution)/shard_map/ppermute | solution.py:31
  80.8 116.3 %reduce-scatter.2.cloned.1.call-start = ((), (), s32[]{:S(2)}) async-start(), calls=%async_computation.5 | async-start | bytes 3538944 | tf_op jit(solution)/shard_map/reduce_scatter | solution.py:412
  80.8 9.0 %collective-permute-start.19 = (bf16[4,5,48,384]{3,2,1,0:T(8,128)(2,1)S(1)}, bf16[4,5,48,384]{3,2,1,0:T(8,128)(2,1)S(1)}, u32[]{:S(2)}, u32[]{:S(2)}) collective-permute-start(bf16[4,5,48,384]{3,2,1,0:T(8,128)(2,1)S(1)} %pad_maximum_fusion.refs_5_), channel_id=1, source_target_pairs={{0,8},{8,0},{1,9},{9,1},{2,10},{10,2},{3,11},{11,3},{4,12},{12,4},... | collective-permute-start | bytes 2211848 | tf_op jit(solution)/shard_map/ppermute | solution.py:363
  87.0 3.9 %collective-permute-start.20 = (bf16[4,5,48,384]{3,2,1,0:T(8,128)(2,1)S(1)}, bf16[4,5,48,384]{3,2,1,0:T(8,128)(2,1)}, u32[]{:S(2)}, u32[]{:S(2)}) collective-permute-start(bf16[4,5,48,384]{3,2,1,0:T(8,128)(2,1)S(1)} %collective-permute-done.10.refs_6_), channel_id=1, source_target_pairs={{0,8},{8,0},{1,9},{9,1},{2,10},{10,2},{3,11},{11,3},{4,12},{12,4},... | collective-permute-start | bytes 2211848 | tf_op jit(solution)/shard_map/ppermute | solution.py:363
  87.0 5.1 %collective-permute-start.21 = (bf16[4,5,48,384]{3,2,1,0:T(8,128)(2,1)S(1)}, bf16[4,5,48,384]{3,2,1,0:T(8,128)(2,1)}, u32[]{:S(2)}, u32[]{:S(2)}) collective-permute-start(bf16[4,5,48,384]{3,2,1,0:T(8,128)(2,1)S(1)} %collective-permute-done.11.refs_7_), channel_id=1, source_target_pairs={{0,8},{8,0},{1,9},{9,1},{2,10},{10,2},{3,11},{11,3},{4,12},{12,4},... | collective-permute-start | bytes 2211848 | tf_op jit(solution)/shard_map/ppermute | solution.py:363
  87.5 4.6 %collective-permute-start.22 = (bf16[2,5,48,384]{3,2,1,0:T(8,128)(2,1)}, bf16[2,5,48,384]{3,2,1,0:T(8,128)(2,1)}, u32[]{:S(2)}, u32[]{:S(2)}) collective-permute-start(bf16[2,5,48,384]{3,2,1,0:T(8,128)(2,1)} %collective-permute-done.17.refs_8_), channel_id=1, source_target_pairs={{0,8},{8,0},{1,9},{9,1},{2,10},{10,2},{3,11},{11,3},{4,12},{12,4},... | collective-permute-start | bytes 1105928 | tf_op jit(solution)/shard_map/ppermute | solution.py:363
  87.5 4.8 %collective-permute-start.23 = (bf16[2,5,48,384]{3,2,1,0:T(8,128)(2,1)}, bf16[2,5,48,384]{3,2,1,0:T(8,128)(2,1)}, u32[]{:S(2)}, u32[]{:S(2)}) collective-permute-start(bf16[2,5,48,384]{3,2,1,0:T(8,128)(2,1)} %collective-permute-done.18.refs_9_), channel_id=1, source_target_pairs={{0,8},{8,0},{1,9},{9,1},{2,10},{10,2},{3,11},{11,3},{4,12},{12,4},... | collective-permute-start | bytes 1105928 | tf_op jit(solution)/shard_map/ppermute | solution.py:363
  88.8 16.5 %copy-start.1 = (s32[4]{0:T(128)}, s32[4]{0:T(128)S(1)}, u32[]{:S(2)}) copy-start(s32[4]{0:T(128)S(1)} %pad_add_fusion.pos_ref) | copy-start | bytes 52
  89.8 27.9 %collective-permute-start.35 = (bf16[4,96,768]{2,1,0:T(8,128)(2,1)}, bf16[4,96,768]{2,1,0:T(8,128)(2,1)S(1)}, u32[]{:S(2)}, u32[]{:S(2)}) collective-permute-start(bf16[4,96,768]{2,1,0:T(8,128)(2,1)} %pad_maximum_fusion.1.refs_11_), channel_id=1, source_target_pairs={{0,68},{4,0},{64,4},{68,64},{1,69},{5,1},{65,5},{69,65},{2,70},{6,... | collective-permute-start | bytes 1769480 | tf_op jit(solution)/shard_map/ppermute | solution.py:38
  90.9 26.9 %collective-permute-start.34 = (bf16[4,96,768]{2,1,0:T(8,128)(2,1)}, bf16[4,96,768]{2,1,0:T(8,128)(2,1)S(1)}, u32[]{:S(2)}, u32[]{:S(2)}) collective-permute-start(bf16[4,96,768]{2,1,0:T(8,128)(2,1)} %pad_maximum_fusion.1.refs_11_), channel_id=1, source_target_pairs={{0,4},{4,64},{64,68},{68,0},{1,5},{5,65},{65,69},{69,1},{2,6},{6,6... | collective-permute-start | bytes 1769480 | tf_op jit(solution)/shard_map/ppermute | solution.py:37
  105.3 26.6 %copy-start.21 = (f32[1536]{0:T(1024)S(1)}, f32[1536]{0:T(1024)}, u32[]{:S(2)}) copy-start(f32[1536]{0:T(1024)} %param.10) | copy-start | bytes 18436
  105.3 9.4 %collective-permute-start.24 = (bf16[512,384]{1,0:T(8,128)(2,1)S(1)}, bf16[512,384]{1,0:T(8,128)(2,1)S(1)}, u32[]{:S(2)}, u32[]{:S(2)}) collective-permute-start(bf16[512,384]{1,0:T(8,128)(2,1)S(1)} %shard_map.95), channel_id=1, source_target_pairs={{0,0},{4,8},{8,4},{12,12},{1,1},{5,9},{9,5},{13,13},{2,2},{6,10},{... | collective-permute-start | bytes 1179656 | tf_op jit(solution)/shard_map/ppermute | solution.py:359
  114.7 19.4 %copy-start.22 = (bf16[512,384]{1,0:T(8,128)(2,1)}, bf16[512,384]{1,0:T(8,128)(2,1)S(1)}, u32[]{:S(2)}) copy-start(bf16[512,384]{1,0:T(8,128)(2,1)S(1)} %collective-permute-done.24.refs_0_) | copy-start | bytes 1179652
  114.7 7.7 %collective-permute-start.26 = (bf16[512,384]{1,0:T(8,128)(2,1)S(1)}, bf16[512,384]{1,0:T(8,128)(2,1)S(1)}, u32[]{:S(2)}, u32[]{:S(2)}) collective-permute-start(bf16[512,384]{1,0:T(8,128)(2,1)S(1)} %collective-permute-done.24.refs_0_), channel_id=1, source_target_pairs={{0,3},{1,0},{2,1},{3,2},{4,7},{5,4},{6,5},{7,6},{8,11},{9,8},{10,9... | collective-permute-start | bytes 1179656 | tf_op jit(solution)/shard_map/ppermute | solution.py:38
  117.7 8.1 %collective-permute-start.25 = (bf16[512,384]{1,0:T(8,128)(2,1)S(1)}, bf16[512,384]{1,0:T(8,128)(2,1)S(1)}, u32[]{:S(2)}, u32[]{:S(2)}) collective-permute-start(bf16[512,384]{1,0:T(8,128)(2,1)S(1)} %collective-permute-done.24.refs_0_), channel_id=1, source_target_pairs={{0,1},{1,2},{2,3},{3,0},{4,5},{5,6},{6,7},{7,4},{8,9},{9,10},{10,1... | collective-permute-start | bytes 1179656 | tf_op jit(solution)/shard_map/ppermute | solution.py:37
  117.7 14.3 %copy-start.15 = (bf16[4,96,768]{2,1,0:T(8,128)(2,1)}, bf16[4,96,768]{2,1,0:T(8,128)(2,1)S(1)}, u32[]{:S(2)}) copy-start(bf16[4,96,768]{2,1,0:T(8,128)(2,1)S(1)} %collective-permute-done.35.refs_13_) | copy-start | bytes 1769476
  117.7 8.2 %collective-permute-start.37 = (bf16[2,96,768]{2,1,0:T(8,128)(2,1)S(1)}, bf16[2,96,768]{2,1,0:T(8,128)(2,1)S(1)}, u32[]{:S(2)}, u32[]{:S(2)}) collective-permute-start(bf16[2,96,768]{2,1,0:T(8,128)(2,1)S(1)} %slice.62), channel_id=1, source_target_pairs={{0,68},{4,0},{64,4},{68,64},{1,69},{5,1},{65,5},{69,65},{2,70},{6,... | collective-permute-start | bytes 884744 | tf_op jit(solution)/shard_map/ppermute | solution.py:32
  117.8 14.1 %copy-start.16 = (bf16[4,96,768]{2,1,0:T(8,128)(2,1)}, bf16[4,96,768]{2,1,0:T(8,128)(2,1)S(1)}, u32[]{:S(2)}) copy-start(bf16[4,96,768]{2,1,0:T(8,128)(2,1)S(1)} %collective-permute-done.34.refs_12_) | copy-start | bytes 1769476
  117.9 8.2 %collective-permute-start.36 = (bf16[2,96,768]{2,1,0:T(8,128)(2,1)S(1)}, bf16[2,96,768]{2,1,0:T(8,128)(2,1)S(1)}, u32[]{:S(2)}, u32[]{:S(2)}) collective-permute-start(bf16[2,96,768]{2,1,0:T(8,128)(2,1)S(1)} %slice.61), channel_id=1, source_target_pairs={{0,4},{4,64},{64,68},{68,0},{1,5},{5,65},{65,69},{69,1},{2,6},{6,6... | collective-permute-start | bytes 884744 | tf_op jit(solution)/shard_map/ppermute | solution.py:31
  119.4 13.3 %collective-permute-start.29 = (bf16[512,384]{1,0:T(8,128)(2,1)S(1)}, bf16[512,384]{1,0:T(8,128)(2,1)S(1)}, u32[]{:S(2)}, u32[]{:S(2)}) collective-permute-start(bf16[512,384]{1,0:T(8,128)(2,1)S(1)} %collective-permute-done.24.refs_0_), channel_id=1, source_target_pairs={{0,8},{8,0},{1,9},{9,1},{2,10},{10,2},{3,11},{11,3},{4,12},{12,4},... | collective-permute-start | bytes 1179656 | tf_op jit(solution)/shard_map/ppermute | solution.py:363
  122.4 11.7 %copy-start.18 = (bf16[512,384]{1,0:T(8,128)(2,1)}, bf16[512,384]{1,0:T(8,128)(2,1)S(1)}, u32[]{:S(2)}) copy-start(bf16[512,384]{1,0:T(8,128)(2,1)S(1)} %collective-permute-done.26.refs_2_) | copy-start | bytes 1179652
  122.4 6.1 %collective-permute-start.28 = (bf16[256,384]{1,0:T(8,128)(2,1)S(1)}, bf16[256,384]{1,0:T(8,128)(2,1)S(1)}, u32[]{:S(2)}, u32[]{:S(2)}) collective-permute-start(bf16[256,384]{1,0:T(8,128)(2,1)S(1)} %slice.60), channel_id=1, source_target_pairs={{0,3},{1,0},{2,1},{3,2},{4,7},{5,4},{6,5},{7,6},{8,11},{9,8},{10,9... | collective-permute-start | bytes 589832 | tf_op jit(solution)/shard_map/ppermute | solution.py:32
  125.8 8.3 %copy-start.19 = (bf16[512,384]{1,0:T(8,128)(2,1)}, bf16[512,384]{1,0:T(8,128)(2,1)S(1)}, u32[]{:S(2)}) copy-start(bf16[512,384]{1,0:T(8,128)(2,1)S(1)} %collective-permute-done.25.refs_1_) | copy-start | bytes 1179652
  125.8 6.1 %collective-permute-start.27 = (bf16[256,384]{1,0:T(8,128)(2,1)S(1)}, bf16[256,384]{1,0:T(8,128)(2,1)S(1)}, u32[]{:S(2)}, u32[]{:S(2)}) collective-permute-start(bf16[256,384]{1,0:T(8,128)(2,1)S(1)} %slice.59), channel_id=1, source_target_pairs={{0,1},{1,2},{2,3},{3,0},{4,5},{5,6},{6,7},{7,4},{8,9},{9,10},{10,1... | collective-permute-start | bytes 589832 | tf_op jit(solution)/shard_map/ppermute | solution.py:31
  125.9 8.2 %copy-start.26 = (bf16[2,96,768]{2,1,0:T(8,128)(2,1)}, bf16[2,96,768]{2,1,0:T(8,128)(2,1)S(1)}, u32[]{:S(2)}) copy-start(bf16[2,96,768]{2,1,0:T(8,128)(2,1)S(1)} %collective-permute-done.37.refs_15_) | copy-start | bytes 884740
  125.9 6.7 %collective-permute-start.31 = (bf16[512,384]{1,0:T(8,128)(2,1)S(1)}, bf16[512,384]{1,0:T(8,128)(2,1)S(1)}, u32[]{:S(2)}, u32[]{:S(2)}) collective-permute-start(bf16[512,384]{1,0:T(8,128)(2,1)S(1)} %collective-permute-done.26.refs_2_), channel_id=1, source_target_pairs={{0,8},{8,0},{1,9},{9,1},{2,10},{10,2},{3,11},{11,3},{4,12},{12,4},... | collective-permute-start | bytes 1179656 | tf_op jit(solution)/shard_map/ppermute | solution.py:363
  126.1 8.1 %copy-start.27 = (bf16[2,96,768]{2,1,0:T(8,128)(2,1)}, bf16[2,96,768]{2,1,0:T(8,128)(2,1)S(1)}, u32[]{:S(2)}) copy-start(bf16[2,96,768]{2,1,0:T(8,128)(2,1)S(1)} %collective-permute-done.36.refs_14_) | copy-start | bytes 884740
  126.1 8.0 %collective-permute-start.30 = (bf16[512,384]{1,0:T(8,128)(2,1)S(1)}, bf16[512,384]{1,0:T(8,128)(2,1)S(1)}, u32[]{:S(2)}, u32[]{:S(2)}) collective-permute-start(bf16[512,384]{1,0:T(8,128)(2,1)S(1)} %collective-permute-done.25.refs_1_), channel_id=1, source_target_pairs={{0,8},{8,0},{1,9},{9,1},{2,10},{10,2},{3,11},{11,3},{4,12},{12,4},... | collective-permute-start | bytes 1179656 | tf_op jit(solution)/shard_map/ppermute | solution.py:363
  128.6 4.1 %collective-permute-start.33 = (bf16[256,384]{1,0:T(8,128)(2,1)S(1)}, bf16[256,384]{1,0:T(8,128)(2,1)S(1)}, u32[]{:S(2)}, u32[]{:S(2)}) collective-permute-start(bf16[256,384]{1,0:T(8,128)(2,1)S(1)} %collective-permute-done.28.refs_4_), channel_id=1, source_target_pairs={{0,8},{8,0},{1,9},{9,1},{2,10},{10,2},{3,11},{11,3},{4,12},{12,4},... | collective-permute-start | bytes 589832 | tf_op jit(solution)/shard_map/ppermute | solution.py:363
  131.9 1.4 collective-permute-start.32
  157.9 24.5 %all-to-all-start = ((bf16[16,96,384]{2,1,0:T(8,128)(2,1)}), bf16[16,96,384]{2,1,0:T(8,128)(2,1)S(1)}, u32[]{:S(2)}, u32[]{:S(2)}) async-start(bf16[16,96,384]{2,1,0:T(8,128)(2,1)} %get-tuple-element.52), calls=%async_computation | async-start | bytes 2359296 | tf_op jit(solution)/shard_map/all_to_all | solution.py:413
  183.4 26.1 %all-to-all-start.1 = ((bf16[16,96,384]{2,1,0:T(8,128)(2,1)}), bf16[16,96,384]{2,1,0:T(8,128)(2,1)S(1)}, u32[]{:S(2)}, u32[]{:S(2)}) async-start(bf16[16,96,384]{2,1,0:T(8,128)(2,1)} %shard_map.97), calls=%async_computation.1 | async-start | bytes 2359296 | tf_op jit(solution)/shard_map/all_to_all | solution.py:416
  187.1 10.0 %copy-start.12 = (bf16[128,1536]{1,0:T(8,128)(2,1)S(1)}, bf16[128,1536]{1,0:T(8,128)(2,1)}, u32[]{:S(2)}) copy-start(bf16[128,1536]{1,0:T(8,128)(2,1)} %get-tuple-element.58) | copy-start | bytes 1179652
  189.2 12.3 %collective-permute-start.38 = (bf16[96,384]{1,0:T(8,128)(2,1)}, bf16[96,384]{1,0:T(8,128)(2,1)S(1)}, u32[]{:S(2)}, u32[]{:S(2)}) collective-permute-start(bf16[96,384]{1,0:T(8,128)(2,1)} %shard_map.98), channel_id=1, source_target_pairs={{0,0},{4,8},{8,4},{12,12},{1,1},{5,9},{9,5},{13,13},{2,2},{6,10},{... | collective-permute-start | bytes 221192 | tf_op jit(solution)/shard_map/ppermute | solution.py:359
  198.2 11.4 %collective-permute-start.42 = (bf16[128,1536]{1,0:T(8,128)(2,1)S(1)}, bf16[128,1536]{1,0:T(8,128)(2,1)S(1)}, u32[]{:S(2)}, u32[]{:S(2)}) collective-permute-start(bf16[128,1536]{1,0:T(8,128)(2,1)S(1)} %add_convert_fusion), channel_id=1, source_target_pairs={{0,0},{4,8},{8,4},{12,12},{1,1},{5,9},{9,5},{13,13},{2,2},{6,10},{... | collective-permute-start | bytes 1179656 | tf_op jit(solution)/shard_map/ppermute | solution.py:359
  201.6 6.4 %collective-permute-start.40 = (bf16[96,192]{1,0:T(8,128)(2,1)S(1)}, bf16[96,192]{1,0:T(8,128)(2,1)S(1)}, u32[]{:S(2)}, u32[]{:S(2)}) collective-permute-start(bf16[96,192]{1,0:T(8,128)(2,1)S(1)} %get-tuple-element.69), channel_id=1, source_target_pairs={{0,32},{16,48},{32,0},{48,16},{1,33},{17,49},{33,1},{49,17},{2,34}... | collective-permute-start | bytes 110600 | tf_op jit(solution)/shard_map/ppermute | solution.py:418
  205.3 4.2 %collective-permute-start.39 = (bf16[96,192]{1,0:T(8,128)(2,1)S(1)}, bf16[96,192]{1,0:T(8,128)(2,1)S(1)}, u32[]{:S(2)}, u32[]{:S(2)}) collective-permute-start(bf16[96,192]{1,0:T(8,128)(2,1)S(1)} %get-tuple-element.69), channel_id=1, source_target_pairs={{0,16},{16,32},{32,48},{48,0},{1,17},{17,33},{33,49},{49,1},{2,18}... | collective-permute-start | bytes 110600 | tf_op jit(solution)/shard_map/ppermute | solution.py:418
  206.4 3.1 %collective-permute-start.41 = (bf16[96,192]{1,0:T(8,128)(2,1)S(1)}, bf16[96,192]{1,0:T(8,128)(2,1)S(1)}, u32[]{:S(2)}, u32[]{:S(2)}) collective-permute-start(bf16[96,192]{1,0:T(8,128)(2,1)S(1)} %get-tuple-element.69), channel_id=1, source_target_pairs={{0,48},{16,0},{32,16},{48,32},{1,49},{17,1},{33,17},{49,33},{2,50}... | collective-permute-start | bytes 110600 | tf_op jit(solution)/shard_map/ppermute | solution.py:418
  212.6 6.3 %collective-permute-start.43 = (bf16[96,384]{1,0:T(8,128)(2,1)}, bf16[96,384]{1,0:T(8,128)(2,1)S(1)}, u32[]{:S(2)}, u32[]{:S(2)}) collective-permute-start(bf16[96,384]{1,0:T(8,128)(2,1)} %shard_map.99), channel_id=1, source_target_pairs={{0,0},{4,8},{8,4},{12,12},{1,1},{5,9},{9,5},{13,13},{2,2},{6,10},{... | collective-permute-start | bytes 221192 | tf_op jit(solution)/shard_map/ppermute | solution.py:359
  220.0 27.3 %all-to-all-start.2 = ((bf16[8,96,576]{2,1,0:T(8,128)(2,1)}), bf16[8,96,576]{2,1,0:T(8,128)(2,1)S(1)}, u32[]{:S(2)}, u32[]{:S(2)}) async-start(bf16[8,96,576]{2,1,0:T(8,128)(2,1)} %broadcast_in_dim.56), calls=%async_computation.3 | async-start | bytes 1966080 | tf_op jit(solution)/shard_map/all_to_all | solution.py:425
  223.5 18.4 %collective-permute-start.44 = (bf16[4,96,192]{2,1,0:T(8,128)(2,1)S(1)}, bf16[4,96,192]{2,1,0:T(8,128)(2,1)S(1)}, u32[]{:S(2)}, u32[]{:S(2)}) collective-permute-start(bf16[4,96,192]{2,1,0:T(8,128)(2,1)S(1)} %pad_maximum_fusion.5), channel_id=1, source_target_pairs={{0,64},{64,0},{1,65},{65,1},{2,66},{66,2},{3,67},{67,3},{4,68},{68... | collective-permute-start | bytes 442376 | tf_op jit(solution)/shard_map/ppermute | solution.py:423
  242.0 2.1 collective-permute-start.45
  (19 other events, 42.0 us)
Sparse Core Ops, SparseCore 0:
  80.2 30.1 all-gather.1
  158.0 39.0 reduce-scatter.1

commit v3 on v2

--- a/solution.py
+++ b/solution.py
@@ -18,6 +18,7 @@
 KW = 5
 EPS = 1e-06
 HALO = 16
+ROWS = 512
 
 bf16 = jnp.bfloat16
 f32 = jnp.float32
@@ -40,9 +41,9 @@
 
 
 def conv_kernel(pos_ref, *refs):
-    (x0, x1, x2, x3a, x3b, w0, w1, w2, w3a, w3b, o0, o1, o2, o3a, o3b, bias_ref, out_ref, wcat, xs, *accs) = refs
+    (x0, x1, x2, x3a, x3b, w0, w1, w2, w3, o0, o1, o2, o3, bias_ref, out_ref, wcat, xs, *accs) = refs
     row = 0
-    for ref in (w0, w1, w2, w3a, w3b, o0, o1, o2, o3a, o3b):
+    for ref in (w0, w1, w2, w3, o0, o1, o2, o3):
         for piece in range(ref.shape[0]):
             for off in range(KW):
                 wcat[row : row + SLOT, off * OUTC : (off + 1) * OUTC] = ref[piece, off]
@@ -70,19 +71,19 @@
     xs[pl.ds(pl.multiple_of(HALO + b * 256 + 128, HALO), 128), :] = x3b[0:128, :]
     place_halo(b, lambda: x3b[128 : 128 + HALO, :])
 
-    @pl.loop(0, 4)
+    @pl.loop(0, 1024 // ROWS)
     def _(r):
-        base = pl.multiple_of(r * 256, 256)
-        y = jnp.dot(xs[pl.ds(base, 256 + 2 * HALO), :], wcat[...], preferred_element_type=f32)
-        total = bias_ref[...] + jnp.zeros((256, OUTC), f32)
+        base = pl.multiple_of(r * ROWS, ROWS)
+        y = jnp.dot(xs[pl.ds(base, ROWS + 2 * HALO), :], wcat[...], preferred_element_type=f32)
+        total = bias_ref[...] + jnp.zeros((ROWS, OUTC), f32)
         for off in range(KW):
             first = HALO + off - 2
-            total = total + y[first : first + 256, off * OUTC : (off + 1) * OUTC]
+            total = total + y[first : first + ROWS, off * OUTC : (off + 1) * OUTC]
         activated = jax.nn.gelu(total)
         for n, acc in enumerate(accs):
             acc[...] = activated[:, n * 128 : (n + 1) * 128]
-            top = jnp.maximum(acc[pl.ds(0, 128, 2), :], acc[pl.ds(1, 128, 2), :])
-            out_ref[pl.ds(pl.multiple_of(r * 128, 128), 128), n * 128 : (n + 1) * 128] = top.astype(bf16)
+            top = jnp.maximum(acc[pl.ds(0, ROWS // 2, 2), :], acc[pl.ds(1, ROWS // 2, 2), :])
+            out_ref[pl.ds(pl.multiple_of(r * (ROWS // 2), ROWS // 2), ROWS // 2), n * 128 : (n + 1) * 128] = top.astype(bf16)
 
 
 VMEM = pl.BlockSpec(memory_space=pltpu.VMEM)
@@ -98,7 +99,7 @@
         scratch_shapes=[
             pltpu.VMEM((KPAD, KW * OUTC), bf16),
             pltpu.VMEM((1024 + 2 * HALO, KPAD), bf16),
-            *[pltpu.VMEM((256, 128), f32)] * 3,
+            *[pltpu.VMEM((ROWS, 128), f32)] * 3,
         ],
         compiler_params=pltpu.CompilerParams(vmem_limit_bytes=48 * 1024 * 1024),
         cost_estimate=pl.CostEstimate(flops=6_000_000_000, bytes_accessed=9_000_000, transcendentals=400_000),
@@ -108,7 +109,7 @@
 SCALE = HD ** (-0.5)
 WIDE = 256
 TOKENS = 1024
-BLOCK = 256
+BLOCK = 512
 NT = (((1,), (1,)), ((), ()))
 TN = (((0,), (0,)), ((), ()))
 
@@ -125,15 +126,14 @@
 
 def forward_kernel(pos_ref, *refs):
     feat_refs, refs = refs[:10], refs[10:]
-    (gain_ref, z0, z1, z2, z3a, z3b, cot_ref) = refs[:7]
-    (normed_ref, qkv_ref, dm_ref, partial_ref, own_ref, sent_ref, wo, feats, wq, mixed_ref, dv, dval, grads, outs) = refs[7:]
-    c, x, y, z = (pos_ref[i] for i in range(4))
+    (gain_ref, z0, z1, z2, z3a, z3b, normed_ref, qkv_ref, mixed_ref, partial_ref, own_ref, wo, feats, wq) = refs
+    c, x, z = pos_ref[0], pos_ref[1], pos_ref[3]
     for t in range(3):
         wq[:, t * WIDE + HD : (t + 1) * WIDE] = jnp.zeros((D, WIDE - HD), bf16)
     wo[:, HD:] = jnp.zeros((D, WIDE - HD), bf16)
     for ref, zstep, first in ((z0, 0, 0), (z1, 3, 0), (z2, 1, 0), (z3a, 2, 0), (z3b, 2, 2)):
         for k in range(ref.shape[0]):
-            src_z, src_y = (z + zstep) % 4, (y + 4 - (first + k)) % 4
+            src_z, src_y = (z + zstep) % 4, first + k
             rows = pl.ds(pl.multiple_of((((src_z // 2) * 4 + src_y) * 2 + src_z % 2) * 96, 96), 96)
             piece = ref[k]
             for t in range(3):
@@ -167,34 +167,9 @@
         mixed = dot(weights, qkv_ref[2]).astype(bf16)
         mixed_ref[rows, :] = mixed
         partial_ref[rows, :] = dot(mixed, wo[...], NT).astype(bf16)
-        d_mixed = dot(cot_ref[rows, :], wo[...]).astype(bf16)
-        dm_ref[rows, :] = d_mixed
-        d_value = dot(d_mixed, weights, TN)
-
-        @pl.when(r == 0)
-        def _():
-            dv[...] = d_value
-
-        @pl.when(r > 0)
-        def _():
-            dv[...] += d_value
-
-    dval[...] = dv[...].T.astype(bf16)
-
-    @pl.loop(0, 4)
-    def _(n):
-        lanes = pl.ds(pl.multiple_of(n * 384, 384), 384)
-        grads[lanes, :] = dot(normed_ref[:, lanes], dval[...], TN)
-        outs[:, lanes] = dot(mixed_ref[...], cot_ref[:, lanes], TN)[:HD]
-
-    for d in range(16):
-        sent_ref[d, :, :HD] = grads[d * 96 : (d + 1) * 96, :HD].astype(bf16)
-        g, lane = d // 2, (d % 2) * 768
-        packed = [outs[g * 24 : (g + 1) * 24, lane + j * HD : lane + (j + 1) * HD] for j in range(4)]
-        sent_ref[d, :, HD:] = jnp.concatenate(packed, axis=0).astype(bf16)
-
-
-def forward(pos, feats, gain, wpieces, cot):
+
+
+def forward(pos, feats, gain, wpieces):
     return pl.pallas_call(
         forward_kernel,
         out_shape=(
@@ -203,70 +178,74 @@
             jax.ShapeDtypeStruct((TOKENS, WIDE), bf16),
             jax.ShapeDtypeStruct((TOKENS, D), bf16),
             jax.ShapeDtypeStruct((128, D), bf16),
-            jax.ShapeDtypeStruct((16, 96, 2 * HD), bf16),
+            jax.ShapeDtypeStruct((D, WIDE), bf16),
         ),
-        in_specs=[SMEM] + [VMEM] * 17,
+        in_specs=[SMEM] + [VMEM] * 16,
         out_specs=[VMEM] * 6,
-        scratch_shapes=[
-            pltpu.VMEM((D, WIDE), bf16),
-            pltpu.VMEM((TOKENS, D), bf16),
-            pltpu.VMEM((D, 3 * WIDE), bf16),
-            pltpu.VMEM((TOKENS, WIDE), bf16),
-            pltpu.VMEM((WIDE, TOKENS), f32),
-            pltpu.VMEM((TOKENS, WIDE), bf16),
-            pltpu.VMEM((D, WIDE), f32),
-            pltpu.VMEM((HD, D), f32),
-        ],
-        compiler_params=pltpu.CompilerParams(vmem_limit_bytes=56 * 1024 * 1024),
-        cost_estimate=pl.CostEstimate(flops=8_000_000_000, bytes_accessed=20_000_000, transcendentals=1_100_000),
-    )(pos, *feats, gain, *wpieces, cot)
-
-
-def backward_kernel(qkv_ref, dm_ref, normed_ref, sent_ref, dcat, dk, grads):
+        scratch_shapes=[pltpu.VMEM((TOKENS, D), bf16), pltpu.VMEM((D, 3 * WIDE), bf16)],
+        compiler_params=pltpu.CompilerParams(vmem_limit_bytes=48 * 1024 * 1024),
+        cost_estimate=pl.CostEstimate(flops=4_000_000_000, bytes_accessed=16_000_000, transcendentals=1_100_000),
+    )(pos, *feats, gain, *wpieces)
+
+
+def backward_kernel(
+    qkv_ref, cot_ref, wo, normed_ref, mixed_ref, sent_ref, dcat, dk, dv, grads, outs
+):
     @pl.loop(0, TOKENS // BLOCK)
     def _(r):
         rows = pl.ds(pl.multiple_of(r * BLOCK, BLOCK), BLOCK)
+        d_mixed = dot(cot_ref[rows, :], wo[...]).astype(bf16)
         q_block = qkv_ref[0, rows, :]
         weights = softmax_rows(q_block, qkv_ref[1])
-        d_weights = dot(dm_ref[rows, :], qkv_ref[2], NT)
+        d_weights = dot(d_mixed, qkv_ref[2], NT)
         centre = jnp.sum(weights * d_weights, axis=-1, keepdims=True)
         d_scores = (weights * (d_weights - centre) * SCALE).astype(bf16)
         dcat[rows, 0:HD] = dot(d_scores, qkv_ref[1]).astype(bf16)[:, :HD]
+        d_value = dot(d_mixed, weights.astype(bf16), TN)
         d_key = dot(q_block, d_scores, TN)
 
         @pl.when(r == 0)
         def _():
+            dv[...] = d_value
             dk[...] = d_key
 
         @pl.when(r > 0)
         def _():
+            dv[...] += d_value
             dk[...] += d_key
 
-    dcat[:, HD:] = dk[...].T.astype(bf16)[:, :HD]
+    dcat[:, HD : 2 * HD] = dk[...].T.astype(bf16)[:, :HD]
+    dcat[:, 2 * HD : 3 * HD] = dv[...].T.astype(bf16)[:, :HD]
 
     @pl.loop(0, 4)
     def _(n):
         lanes = pl.ds(pl.multiple_of(n * 384, 384), 384)
         grads[lanes, :] = dot(normed_ref[:, lanes], dcat[...], TN)
+        outs[:, lanes] = dot(mixed_ref[...], cot_ref[:, lanes], TN)[:HD]
 
     for d in range(16):
-        sent_ref[d] = grads[d * 96 : (d + 1) * 96, :].astype(bf16)
-
-
-def backward(qkv, d_mixed, normed):
+        sent_ref[d, :, : 3 * HD] = grads[d * 96 : (d + 1) * 96, :].astype(bf16)
+        g, lane = d // 2, (d % 2) * 768
+        packed = [outs[g * 24 : (g + 1) * 24, lane + j * HD : lane + (j + 1) * HD] for j in range(4)]
+        sent_ref[d, :, 3 * HD :] = jnp.concatenate(packed, axis=0).astype(bf16)
+
+
+def backward(qkv, cot, wo, normed, mixed):
     return pl.pallas_call(
         backward_kernel,
-        out_shape=jax.ShapeDtypeStruct((16, 96, 2 * HD), bf16),
-        in_specs=[VMEM] * 3,
+        out_shape=jax.ShapeDtypeStruct((16, 96, 768), bf16),
+        in_specs=[VMEM] * 5,
         out_specs=VMEM,
         scratch_shapes=[
-            pltpu.VMEM((TOKENS, 2 * HD), bf16),
+            pltpu.VMEM((TOKENS, 3 * HD), bf16),
             pltpu.VMEM((WIDE, TOKENS), f32),
-            pltpu.VMEM((D, 2 * HD), f32),
+            pltpu.VMEM((WIDE, TOKENS), f32),
+            pltpu.VMEM((D, 3 * HD), f32),
+            pltpu.VMEM((HD, D), f32),
         ],
         compiler_params=pltpu.CompilerParams(vmem_limit_bytes=56 * 1024 * 1024),
-        cost_estimate=pl.CostEstimate(flops=6_000_000_000, bytes_accessed=8_000_000, transcendentals=1_100_000),
-    )(qkv, d_mixed, normed)
+        cost_estimate=pl.CostEstimate(flops=6_000_000_000, bytes_accessed=18_000_000, transcendentals=1_100_000),
+    )(qkv, cot, wo, normed, mixed)
 
 
 def total_kernel(parts_ref, out_ref):
@@ -279,7 +258,7 @@
 def total_parts(parts):
     return pl.pallas_call(
         total_kernel,
-        out_shape=jax.ShapeDtypeStruct((96, 2 * HD), bf16),
+        out_shape=jax.ShapeDtypeStruct((96, 768), bf16),
         in_specs=[VMEM],
         out_specs=VMEM,
     )(parts)
@@ -307,18 +286,18 @@
         for step in range(2):
             for k in range(4):
                 g = ((zh + step) % 2) * 4 + (y + 4 - k) % 4
-                piece = [ref[step, k, j * 24 : (j + 1) * 24, :] for j in range(4)]
+                piece = [ref[k, step, j * 24 : (j + 1) * 24, :] for j in range(4)]
                 rows = pl.ds(pl.multiple_of(g * 24, 8), 24)
                 out_ref[rows, lanes] = jnp.concatenate(piece, axis=1).astype(f32)
 
 
-def place_out(c, own, other):
+def place_out(pos, own, other):
     return pl.pallas_call(
         out_kernel,
         out_shape=jax.ShapeDtypeStruct((HD, D), f32),
         in_specs=[SMEM, VMEM, VMEM],
         out_specs=VMEM,
-    )(c, own, other)
+    )(pos, own, other)
 
 
 def lane_sources(zh, y, c, zl):
@@ -385,44 +364,40 @@
     later = jnp.concatenate([proj_weight.reshape(96, 3 * HD), out_weight.T], axis=1).reshape(48, D)
     later = swap_axes(jnp.concatenate([cotangent[0], later], axis=0))
 
-    block, mine = lax.optimization_barrier((block, mine))
+    head_w = lax.all_gather(later[128:].reshape(96, 768), "y", axis=0)
+
     ypieces = [mine] + [lax.ppermute(mine, "y", ring(4, k)) for k in (1, 2, 3)]
-    *ypieces, block, later = lax.optimization_barrier((*ypieces, block, later))
+    *ypieces, block = lax.optimization_barrier((*ypieces, block))
     ypieces = jnp.stack(ypieces)
-    head_w = later[128:].reshape(96, 768)
+    zpieces = [lax.ppermute(ypieces, zring, ring(4, k)) for k in (1, -1, 2)]
     xlow, xhigh = (lax.ppermute(block, "x", ring(4, k)) for k in (1, -1))
-    zlow, zhigh = (lax.ppermute(ypieces, zring, ring(4, k)) for k in (1, -1))
-    head_w = jnp.stack([head_w] + [lax.ppermute(head_w, "y", ring(4, k)) for k in (1, 2, 3)])
-    xlow, xhigh, zlow, zhigh, head_w = lax.optimization_barrier((xlow, xhigh, zlow, zhigh, head_w))
+    yother = lax.ppermute(ypieces, "c", ring(2, 1))
+    zpieces[0], xlow, xhigh, yother = lax.optimization_barrier((zpieces[0], xlow, xhigh, yother))
     xfar = across(xlow, xhigh, "x", 128)
-    zfar = across(zlow, zhigh, zring, 2)
-    *xfar, za, zb, head_w, cot = lax.optimization_barrier((*xfar, *zfar, head_w, later[:128]))
+    zothers = from_other_core(zpieces[:2])
+    *zpieces, xa, xb, za, zb, head_w, cot = lax.optimization_barrier((*zpieces, *xfar, *zothers, head_w, later[:128]))
     cot = lax.all_gather(cot, ("c", "x"), axis=0, tiled=True)
-    xpieces = [block, xlow, xhigh, *xfar]
-    wpieces = [ypieces, zlow, zhigh, za, zb]
+    xpieces = [block, xlow, xhigh, xa, xb]
+    wpieces = [ypieces, *zpieces, yother, za, zb, *from_other_core(zpieces[2:])]
     head_w = [head_w, *staged_ring(head_w, zring, 2)]
     bias = lax.dynamic_slice_in_dim(conv_bias, x * OUTC, OUTC)[None]
 
-    feat = swap_axes(conv_pool(pos, xpieces, wpieces + from_other_core(wpieces), bias))
+    feat = swap_axes(conv_pool(pos, xpieces, wpieces, bias))
     feats = [feat, *staged_ring(feat, "x", 256)]
     feats = feats + from_other_core(feats)
 
-    plane = ("zh", "y", "zl")
-    normed, qkv, d_mixed, partial, own, first = forward(pos, feats, norm_gain[None], head_w, cot)
+    normed, qkv, mixed, partial, own, wo = forward(pos, feats, norm_gain[None], head_w)
     attended = lax.psum_scatter(partial, ("c", "x"), scatter_dimension=0, tiled=True)
-    first = lax.all_to_all(first, plane, 0, 0)
-    second = backward(qkv, d_mixed, normed)
-    first, second = lax.optimization_barrier((first, second))
-    second = lax.all_to_all(second, plane, 0, 0)
-    first = swap_axes(total_parts(first))
-    rows = jnp.stack([first[:, HD:]] + [lax.ppermute(first[:, HD:], "y", ring(4, k)) for k in (1, 2, 3)])
-
-    block_out = swap_axes((own.astype(f32) + attended.astype(f32)).astype(bf16))
-    second, rows, block_out = lax.optimization_barrier((second, rows, block_out))
-    second = swap_axes(total_parts(second))
-    rows = jnp.stack([rows, lax.ppermute(rows, "zh", ring(2, 1))])
-    proj = jnp.concatenate([second, first[:, :HD]], axis=1)
-    heads = lax.all_to_all(jnp.broadcast_to(proj[None], (8, 96, 3 * HD)), ("zl", "x"), 0, 0)
+    block_out = (own.astype(f32) + attended.astype(f32)).astype(bf16)
+    parts = lax.all_to_all(backward(qkv, cot, wo, normed, mixed), ("zh", "y", "zl"), 0, 0)
+    parts, block_out = lax.optimization_barrier((parts, block_out))
+
+    sums = total_parts(parts)
+    rows = lax.ppermute(sums[:, 3 * HD :], ("zh", "c", "zl"), [(0, 4), (1, 6), (2, 5), (3, 7), (4, 0), (5, 2), (6, 1), (7, 3)])
+    sums, rows, block_out = lax.optimization_barrier((swap_axes(sums), rows, swap_axes(block_out)))
+    rows = jnp.stack([sums[:, 3 * HD :], rows])
+    rows = jnp.stack([rows] + [lax.ppermute(rows, "y", ring(4, k)) for k in (1, 2, 3)])
+    heads = lax.all_to_all(jnp.broadcast_to(sums[None, :, : 3 * HD], (8, 96, 3 * HD)), ("zl", "x"), 0, 0)
     proj_grad = place_proj(heads).transpose(1, 0, 2)
     out_grad = place_out(pos, rows, lax.ppermute(rows, "c", ring(2, 1)))
     return (block_out[None], proj_grad, out_grad)

time: 259 us -> 238 us (0.919)
  blocking collectives: 0 us -> 12 us
  starting transfers between devices: 77.4 us -> 68.3 us
  Pallas kernels: 58.5 us -> 49.9 us
  waiting for transfers between devices: 82.7 us -> 75.2 us
  local copies, waits for them, and re-layouts: 19.8 us -> 14.6 us
  other arithmetic: 5.23 us -> 2.49 us
    reduce_scatter x1, waiting for transfers between devices: 3.45 us -> 20.2 us  [per_device(): lax.psum_scatter(partial, ('c', 'x'), scatter_dimension=0, tiled=True)]
    all_gather x0 -> x1, blocking collectives: none -> 12 us  [per_device(): head_w = lax.all_gather(later[128:].reshape(96, 768), 'y', axis=0)]
    ppermute x9 -> x8, waiting for transfers between devices: 33 us -> 21 us  [the longest x3 13.5 us: per_device(): zpieces = [lax.ppermute(ypieces, zring, ring(4, k)) for k in (1, -1, 2)]]
    pallas_call x1, Pallas kernels: 23 us -> 11.6 us  [forward(): pl.pallas_call(forward_kernel, out_shape=(jax.ShapeDtypeStruct((TOKENS, D...]
    ppermute x3, waiting for transfers between devices: 11 us -> 2.59 us  [per_device(): ypieces = [mine] + [lax.ppermute(mine, 'y', ring(4, k)) for k in (1, 2, 3)]]
    ppermute x5 -> x4, starting transfers between devices: 17.1 us -> 9.78 us  [swap_axes(): return lax.ppermute(value, ('c', 'zl'), [(0, 0), (1, 2), (2, 1), (3, 3)])]
    ppermute x10 -> x8, starting transfers between devices: 10.7 us -> 3.61 us  [from_other_core(): return [lax.ppermute(p, 'c', ring(2, 1)) for p in parts]]
    all_to_all x3 -> x2, waiting for transfers between devices: 7.95 us -> 13.9 us  [the longest x1 12.7 us: per_device(): lax.all_to_all(backward(qkv, cot, wo, normed, mixed), ('zh', 'y', 'zl'),...]
  transfers between devices with their start and end apart: 51 -> 44, of which waited for: 22 -> 16; matrix products, arithmetic and copies ran while one was open for 5% -> 4% of each run, Pallas kernels for 12% -> 20%
where the time goes in v3:
time: 238 us; the launch traced here: 237 us
  waiting for transfers between devices  75.2 us (32%)
  starting transfers between devices  68.3 us (29%)
  Pallas kernels  49.9 us (21%)
  local copies, waits for them, and re-layouts  14.6 us (6%)
  between operations  14.6 us (6%)
  blocking collectives  12 us (5%)
  other arithmetic  2.49 us (1%)
    reduce_scatter x1, waiting for transfers between devices, per_device(): lax.psum_scatter(partial, ('c', 'x'), scatter_dimension=0, tiled=True)  20.2 us
    pallas_call x1, Pallas kernels, backward(): pl.pallas_call(backward_kernel, out_shape=jax.ShapeDtypeStruct((16, 96, 7...  16.5 us
    ppermute x3, waiting for transfers between devices, per_device(): zpieces = [lax.ppermute(ypieces, zring, ring(4, k)) for k in (1, -1, 2)]  13.5 us
    all_to_all x1, waiting for transfers between devices, per_device(): lax.all_to_all(backward(qkv, cot, wo, normed, mixed), ('zh', 'y', 'zl'),...  12.7 us
    all_gather x1, blocking collectives, per_device(): head_w = lax.all_gather(later[128:].reshape(96, 768), 'y', axis=0)  12 us
    pallas_call x1, Pallas kernels, conv_pool(): pl.pallas_call(conv_kernel, out_shape=jax.ShapeDtypeStruct((512, OUTC), b...  11.6 us
    pallas_call x1, Pallas kernels, forward(): pl.pallas_call(forward_kernel, out_shape=(jax.ShapeDtypeStruct((TOKENS, D...  11.6 us
    ppermute x4, starting transfers between devices, swap_axes(): return lax.ppermute(value, ('c', 'zl'), [(0, 0), (1, 2), (2, 1), (3, 3)])  9.78 us
  transfers between devices with their start and end apart: 44, of which 16 were waited for; matrix products, arithmetic and copies ran while one was open for 4% of the time, Pallas kernels for 20%

profile of v3, /device:TPU:1, one launch (start us, length us, event | category | flops | bytes accessed | tf_op | source)
XLA Modules:
  0.0 237.1 jit_solution(6064352241105766172)
XLA Ops:
  7.3 1.1 reshape.354
  8.8 2.1 collective-permute-start
  10.9 2.5 %collective-permute-start.1 = (bf16[5,11,384]{2,1,0:T(8,128)(2,1)S(1)}, bf16[5,11,384]{2,1,0:T(8,128)(2,1)S(1)}, u32[]{:S(2)}, u32[]{:S(2)}) collective-permute-start(bf16[5,11,384]{2,1,0:T(8,128)(2,1)S(1)} %bitcast.66), channel_id=1, source_target_pairs={{0,2},{1,3},{2,0},{3,1},{4,6},{5,7},{6,4},{7,5},{8,10},{9,11},{10,... | collective-permute-start | bytes 126728 | tf_op jit(solution)/shard_map/ppermute | solution.py:359
  13.5 1.2 collective-permute-start.2
  14.7 0.8 select_bitcast_fusion
  15.5 1.7 collective-permute-start.6
  17.5 1.4 collective-permute-start.3
  18.9 2.6 %collective-permute-start.4 = (bf16[5,48,384]{2,1,0:T(8,128)(2,1)S(1)}, bf16[5,48,384]{2,1,0:T(8,128)(2,1)S(1)}, u32[]{:S(2)}, u32[]{:S(2)}) collective-permute-start(bf16[5,48,384]{2,1,0:T(8,128)(2,1)S(1)} %pad.4), channel_id=1, source_target_pairs={{0,32},{16,48},{32,0},{48,16},{1,33},{17,49},{33,1},{49,17},{2,34}... | collective-permute-start | bytes 552968 | tf_op jit(solution)/shard_map/ppermute | solution.py:369
  21.5 1.1 collective-permute-start.5
  22.8 2.6 %shard_map.94.refs_0_ = bf16[272,1536]{1,0:T(8,128)(2,1)S(1)} custom-call(bf16[256,1408]{1,0:T(8,128)(2,1)S(1)} %bitcast.52, bf16[16,1408]{1,0:T(8,128)(2,1)S(1)} %collective-permute-done.6.edge_ref, s32[1,1536]{1,0:T(1,128)S(1)} %compare_select_fusion.10.sources_ref), custom_call_target="tpu_custom_call" | custom-call | flops 1200000000 | bytes 1600000 | tf_op jit(solution)/shard_map/pallas_call | solution.py:327
  25.5 2.6 %collective-permute-done.4 = bf16[5,48,384]{2,1,0:T(8,128)(2,1)S(1)} collective-permute-done((bf16[5,48,384]{2,1,0:T(8,128)(2,1)S(1)}, bf16[5,48,384]{2,1,0:T(8,128)(2,1)S(1)}, u32[]{:S(2)}, u32[]{:S(2)}) %collective-permute-start.4) | collective-permute-done | bytes 184352 | tf_op jit(solution)/shard_map/ppermute | solution.py:369
  28.2 3.1 %collective-permute-start.10 = (bf16[4,5,48,384]{3,2,1,0:T(8,128)(2,1)S(1)}, bf16[4,5,48,384]{3,2,1,0:T(8,128)(2,1)S(1)}, u32[]{:S(2)}, u32[]{:S(2)}) collective-permute-start(bf16[4,5,48,384]{3,2,1,0:T(8,128)(2,1)S(1)} %pad_maximum_fusion.refs_5_), channel_id=1, source_target_pairs={{0,8},{8,0},{1,9},{9,1},{2,10},{10,2},{3,11},{11,3},{4,12},{12,4},... | collective-permute-start | bytes 2211848 | tf_op jit(solution)/shard_map/ppermute | solution.py:374
  31.6 2.4 collective-permute-start.9
  33.9 1.3 collective-permute-start.7
  35.2 2.1 collective-permute-start.11
  37.8 2.3 collective-permute-start.17
  40.2 13.5 %collective-permute-done.7.refs_6_ = bf16[4,5,48,384]{3,2,1,0:T(8,128)(2,1)} collective-permute-done((bf16[4,5,48,384]{3,2,1,0:T(8,128)(2,1)S(1)}, bf16[4,5,48,384]{3,2,1,0:T(8,128)(2,1)}, u32[]{:S(2)}, u32[]{:S(2)}) %collective-permute-start.7) | collective-permute-done | bytes 737312 | tf_op jit(solution)/shard_map/ppermute | solution.py:372
  53.7 1.1 collective-permute-start.12
  54.8 1.8 collective-permute-start.16
  56.7 1.8 slice.42
  58.5 0.9 collective-permute-start.14
  59.4 1.8 slice.41
  61.2 1.7 collective-permute-done.17
  62.9 0.8 copy-done.7
  63.8 1.8 slice.53
  65.6 12.0 %all_gather.6.refs_11_ = bf16[4,96,768]{2,1,0:T(8,128)(2,1)S(1)} all-gather(bf16[1,96,768]{2,1,0:T(8,128)(2,1)S(1)} %all_gather_reshape.3), channel_id=1, replica_groups=mesh['zh'=2,'y'=4,'c'=2,'zl'=2,'x'=4] {'y'}, dimensions={0}, use_global_device_ids=true | all-gather | bytes 737280 | tf_op jit(solution)/shard_map/all_gather | solution.py:367
  78.4 0.8 dynamic_slice.20
  79.2 1.1 collective-permute-start.29
  80.3 3.6 %collective-permute-start.30 = (bf16[4,96,768]{2,1,0:T(8,128)(2,1)S(1)}, bf16[4,96,768]{2,1,0:T(8,128)(2,1)S(1)}, u32[]{:S(2)}, u32[]{:S(2)}) collective-permute-start(bf16[4,96,768]{2,1,0:T(8,128)(2,1)S(1)} %all_gather.6.refs_11_), channel_id=1, source_target_pairs={{0,68},{4,0},{64,4},{68,64},{1,69},{5,1},{65,5},{69,65},{2,70},{6,... | collective-permute-start | bytes 1769480 | tf_op jit(solution)/shard_map/ppermute | solution.py:39
  83.9 11.6 %shard_map.95 = bf16[512,384]{1,0:T(8,128)(2,1)S(1)} custom-call(s32[4]{0:T(128)S(1)} %pad_add_fusion.pos_ref, bf16[272,1536]{1,0:T(8,128)(2,1)} %copy-done.2, bf16[272,1536]{1,0:T(8,128)(2,1)} %collective-permute-done.8.refs_1_, bf16[272,1536]{1,0:T(8,128)(2,1)} %collective-permute-done.9.refs_2_, bf16[128,1536]{1,0:T(8,128)(2,1)} %collective-permute-done.13.refs_3_, ...), custom_call_target="tpu_custom_call" | custom-call | flops 6000000000 | bytes 9000000 | tf_op jit(solution)/shard_map/pallas_call | solution.py:94
  95.5 1.9 collective-permute-start.19
  97.4 7.6 %collective-permute-done.19.refs_0_ = bf16[512,384]{1,0:T(8,128)(2,1)S(1)} collective-permute-done((bf16[512,384]{1,0:T(8,128)(2,1)S(1)}, bf16[512,384]{1,0:T(8,128)(2,1)S(1)}, u32[]{:S(2)}, u32[]{:S(2)}) %collective-permute-start.19) | collective-permute-done | bytes 393248 | tf_op jit(solution)/shard_map/ppermute | solution.py:338
  105.0 2.7 %collective-permute-start.21 = (bf16[512,384]{1,0:T(8,128)(2,1)S(1)}, bf16[512,384]{1,0:T(8,128)(2,1)S(1)}, u32[]{:S(2)}, u32[]{:S(2)}) collective-permute-start(bf16[512,384]{1,0:T(8,128)(2,1)S(1)} %collective-permute-done.19.refs_0_), channel_id=1, source_target_pairs={{0,3},{1,0},{2,1},{3,2},{4,7},{5,4},{6,5},{7,6},{8,11},{9,8},{10,9... | collective-permute-start | bytes 1179656 | tf_op jit(solution)/shard_map/ppermute | solution.py:39
  107.8 2.7 %collective-permute-start.32 = (bf16[2,96,768]{2,1,0:T(8,128)(2,1)S(1)}, bf16[2,96,768]{2,1,0:T(8,128)(2,1)S(1)}, u32[]{:S(2)}, u32[]{:S(2)}) collective-permute-start(bf16[2,96,768]{2,1,0:T(8,128)(2,1)S(1)} %slice.57), channel_id=1, source_target_pairs={{0,68},{4,0},{64,4},{68,64},{1,69},{5,1},{65,5},{69,65},{2,70},{6,... | collective-permute-start | bytes 884744 | tf_op jit(solution)/shard_map/ppermute | solution.py:33
  110.5 2.9 %collective-permute-done.20.refs_1_ = bf16[512,384]{1,0:T(8,128)(2,1)S(1)} collective-permute-done((bf16[512,384]{1,0:T(8,128)(2,1)S(1)}, bf16[512,384]{1,0:T(8,128)(2,1)S(1)}, u32[]{:S(2)}, u32[]{:S(2)}) %collective-permute-start.20) | collective-permute-done | bytes 393248 | tf_op jit(solution)/shard_map/ppermute | solution.py:38
  113.7 2.6 %collective-permute-start.23 = (bf16[256,384]{1,0:T(8,128)(2,1)S(1)}, bf16[256,384]{1,0:T(8,128)(2,1)S(1)}, u32[]{:S(2)}, u32[]{:S(2)}) collective-permute-start(bf16[256,384]{1,0:T(8,128)(2,1)S(1)} %slice.55), channel_id=1, source_target_pairs={{0,3},{1,0},{2,1},{3,2},{4,7},{5,4},{6,5},{7,6},{8,11},{9,8},{10,9... | collective-permute-start | bytes 589832 | tf_op jit(solution)/shard_map/ppermute | solution.py:33
  116.3 1.1 collective-permute-done.31.refs_14_
  117.9 1.5 collective-permute-done.22.refs_3_
  120.0 0.9 collective-permute-done.27.refs_8_
  121.2 11.6 %shard_map.96 = (bf16[1024,1536]{1,0:T(8,128)(2,1)}, bf16[3,1024,256]{2,1,0:T(8,128)(2,1)}, bf16[1024,256]{1,0:T(8,128)(2,1)S(1)}, bf16[1024,1536]{1,0:T(8,128)(...) custom-call(s32[4]{0:T(128)S(1)} %pad_add_fusion.pos_ref, ...), custom_call_target="tpu_custom_call" | custom-call | flops 4000000000 | bytes 16000000 | tf_op jit(solution)/shard_map/pallas_call | solution.py:173
  132.7 0.8 copy-done.3
  133.6 16.5 %shard_map.97 = bf16[16,96,768]{2,1,0:T(8,128)(2,1)} custom-call(bf16[3,1024,256]{2,1,0:T(8,128)(2,1)} %get-tuple-element.49.qkv_ref, bf16[1024,1536]{1,0:T(8,128)(2,1)} %all-gather.2.cloned.1.call-done.cot_ref, bf16[1536,256]{1,0:T(8,128)(2,1)} %get-tuple-element.51.wo, bf16[1024,1536]{1,0:T(8,128)(2,1)} %get-tuple-element.52.normed_ref, ...), custom_call_target="tpu_custom_call" | custom-call | flops 6000000000 | bytes 18000000 | tf_op jit(solution)/shard_map/pallas_call | solution.py:234
  150.2 7.6 %all-to-all-start = ((bf16[16,96,768]{2,1,0:T(8,128)(2,1)}), bf16[16,96,768]{2,1,0:T(8,128)(2,1)S(1)}, u32[]{:S(2)}, u32[]{:S(2)}) async-start(bf16[16,96,768]{2,1,0:T(8,128)(2,1)} %shard_map.97), calls=%async_computation | async-start | bytes 4718592 | tf_op jit(solution)/shard_map/all_to_all | solution.py:392
  157.7 20.2 %reduce-scatter.2.cloned.1.call-done = bf16[128,1536]{1,0:T(8,128)(2,1)} async-done(((bf16[1024,1536]{1,0:T(8,128)(2,1)}), bf16[128,1536]{1,0:T(8,128)(2,1)}) %reduce-scatter.2.cloned.1.call-update) | async-done | bytes 393232 | tf_op jit(solution)/shard_map/reduce_scatter | solution.py:390
  178.0 1.1 add_convert_fusion
  179.1 12.7 %all-to-all-done.parts_ref = bf16[16,96,768]{2,1,0:T(8,128)(2,1)S(1)} async-done(((bf16[16,96,768]{2,1,0:T(8,128)(2,1)}), bf16[16,96,768]{2,1,0:T(8,128)(2,1)S(1)}, u32[]{:S(2)}, u32[]{:S(2)}) %all-to-all-start) | async-done | bytes 2359328 | tf_op jit(solution)/shard_map/all_to_all | solution.py:392
  191.8 3.2 %collective-permute-start.35 = (bf16[128,1536]{1,0:T(8,128)(2,1)S(1)}, bf16[128,1536]{1,0:T(8,128)(2,1)S(1)}, u32[]{:S(2)}, u32[]{:S(2)}) collective-permute-start(bf16[128,1536]{1,0:T(8,128)(2,1)S(1)} %add_convert_fusion), channel_id=1, source_target_pairs={{0,0},{4,8},{8,4},{12,12},{1,1},{5,9},{9,5},{13,13},{2,2},{6,10},{... | collective-permute-start | bytes 1179656 | tf_op jit(solution)/shard_map/ppermute | solution.py:338
  195.0 2.6 %shard_map.98 = bf16[96,768]{1,0:T(8,128)(2,1)} custom-call(bf16[16,96,768]{2,1,0:T(8,128)(2,1)} %copy-done.4), custom_call_target="tpu_custom_call" | custom-call | tf_op jit(solution)/shard_map/pallas_call | solution.py:259
  197.6 2.4 %collective-permute-start.33 = (bf16[96,768]{1,0:T(8,128)(2,1)}, bf16[96,768]{1,0:T(8,128)(2,1)S(1)}, u32[]{:S(2)}, u32[]{:S(2)}) collective-permute-start(bf16[96,768]{1,0:T(8,128)(2,1)} %shard_map.98), channel_id=1, source_target_pairs={{0,0},{4,8},{8,4},{12,12},{1,1},{5,9},{9,5},{13,13},{2,2},{6,10},{... | collective-permute-start | bytes 442376 | tf_op jit(solution)/shard_map/ppermute | solution.py:338
  200.0 0.9 slice.58
  200.9 2.4 %collective-permute-start.34 = (bf16[96,192]{1,0:T(8,128)(2,1)S(1)}, bf16[96,192]{1,0:T(8,128)(2,1)S(1)}, u32[]{:S(2)}, u32[]{:S(2)}) collective-permute-start(bf16[96,192]{1,0:T(8,128)(2,1)S(1)} %slice.58), channel_id=1, source_target_pairs={{0,64},{4,72},{8,68},{12,76},{64,0},{68,8},{72,4},{76,12},{1,65},{... | collective-permute-start | bytes 110600 | tf_op jit(solution)/shard_map/ppermute | solution.py:396
  203.3 2.4 %collective-permute-done.34 = bf16[96,192]{1,0:T(8,128)(2,1)S(1)} collective-permute-done((bf16[96,192]{1,0:T(8,128)(2,1)S(1)}, bf16[96,192]{1,0:T(8,128)(2,1)S(1)}, u32[]{:S(2)}, u32[]{:S(2)}) %collective-permute-start.34) | collective-permute-done | bytes 36896 | tf_op jit(solution)/shard_map/ppermute | solution.py:396
  205.7 1.0 broadcast_in_dim.56
  206.7 4.0 %all-to-all-start.1 = ((bf16[8,96,576]{2,1,0:T(8,128)(2,1)}), bf16[8,96,576]{2,1,0:T(8,128)(2,1)S(1)}, u32[]{:S(2)}, u32[]{:S(2)}) async-start(bf16[8,96,576]{2,1,0:T(8,128)(2,1)} %broadcast_in_dim.56), calls=%async_computation.2 | async-start | bytes 1966080 | tf_op jit(solution)/shard_map/all_to_all | solution.py:400
  210.9 1.7 collective-permute-start.37
  212.6 1.0 collective-permute-start.38
  213.5 4.8 %collective-permute-done.36 = bf16[2,96,192]{2,1,0:T(8,128)(2,1)S(1)} collective-permute-done((bf16[2,96,192]{2,1,0:T(8,128)(2,1)S(1)}, bf16[2,96,192]{2,1,0:T(8,128)(2,1)S(1)}, u32[]{:S(2)}, u32[]{:S(2)}) %collective-permute-start.36) | collective-permute-done | bytes 73760 | tf_op jit(solution)/shard_map/ppermute | solution.py:399
  218.7 1.5 collective-permute-start.39
  220.2 1.3 collective-permute-done.39.other_ref
  221.5 0.8 copy-done.9
  222.3 2.3 shard_map.100
  224.6 1.2 all-to-all-done.1.heads_ref
  225.9 1.0 copy-done.5
  226.9 2.6 %shard_map.99 = f32[3,96,1536]{2,1,0:T(8,128)} custom-call(bf16[8,96,576]{2,1,0:T(8,128)(2,1)} %copy-done.5), custom_call_target="tpu_custom_call" | custom-call | tf_op jit(solution)/shard_map/pallas_call | solution.py:274
  (103 shorter events, 5.8 us)
Async XLA Ops:
  7.2 15.6 %copy-start = (bf16[1,256,1408]{2,1,0:T(8,128)(2,1)S(1)}, bf16[1,256,1408]{2,1,0:T(8,128)(2,1)}, u32[]{:S(2)}) copy-start(bf16[1,256,1408]{2,1,0:T(8,128)(2,1)} %param.7) | copy-start | bytes 2162692
  7.2 126.4 %all-gather.2.cloned.1.call-start = ((), (), s32[]{:S(2)}) async-start(), calls=%async_computation.3 | async-start | bytes 3538944 | tf_op jit(solution)/shard_map/all_gather | solution.py:379
  8.8 8.5 %collective-permute-start = (bf16[5,11,384]{2,1,0:T(8,128)(2,1)S(1)}, bf16[5,11,384]{2,1,0:T(8,128)(2,1)S(1)}, u32[]{:S(2)}, u32[]{:S(2)}) collective-permute-start(bf16[5,11,384]{2,1,0:T(8,128)(2,1)S(1)} %bitcast.67), channel_id=1, source_target_pairs={{0,1},{1,2},{2,3},{3,0},{4,5},{5,6},{6,7},{7,4},{8,9},{9,10},{10,1... | collective-permute-start | bytes 126728 | tf_op jit(solution)/shard_map/ppermute | solution.py:359
  10.9 6.4 %collective-permute-start.1 = (bf16[5,11,384]{2,1,0:T(8,128)(2,1)S(1)}, bf16[5,11,384]{2,1,0:T(8,128)(2,1)S(1)}, u32[]{:S(2)}, u32[]{:S(2)}) collective-permute-start(bf16[5,11,384]{2,1,0:T(8,128)(2,1)S(1)} %bitcast.66), channel_id=1, source_target_pairs={{0,2},{1,3},{2,0},{3,1},{4,6},{5,7},{6,4},{7,5},{8,10},{9,11},{10,... | collective-permute-start | bytes 126728 | tf_op jit(solution)/shard_map/ppermute | solution.py:359
  13.5 3.9 %collective-permute-start.2 = (bf16[5,11,384]{2,1,0:T(8,128)(2,1)S(1)}, bf16[5,11,384]{2,1,0:T(8,128)(2,1)S(1)}, u32[]{:S(2)}, u32[]{:S(2)}) collective-permute-start(bf16[5,11,384]{2,1,0:T(8,128)(2,1)S(1)} %bitcast.65), channel_id=1, source_target_pairs={{0,3},{1,0},{2,1},{3,2},{4,7},{5,4},{6,5},{7,6},{8,11},{9,8},{10,9... | collective-permute-start | bytes 126728 | tf_op jit(solution)/shard_map/ppermute | solution.py:359
  15.5 7.3 %collective-permute-start.6 = (bf16[16,1408]{1,0:T(8,128)(2,1)S(1)}, bf16[16,1408]{1,0:T(8,128)(2,1)S(1)}, u32[]{:S(2)}, u32[]{:S(2)}) collective-permute-start(bf16[16,1408]{1,0:T(8,128)(2,1)S(1)} %select_bitcast_fusion), channel_id=1, source_target_pairs={{0,4},{4,0},{1,5},{5,1},{2,6},{6,2},{3,7},{7,3},{8,12},{12,8},{9,1... | collective-permute-start | bytes 135176 | tf_op jit(solution)/shard_map/ppermute | solution.py:351
  17.5 7.9 %collective-permute-start.3 = (bf16[5,48,384]{2,1,0:T(8,128)(2,1)S(1)}, bf16[5,48,384]{2,1,0:T(8,128)(2,1)S(1)}, u32[]{:S(2)}, u32[]{:S(2)}) collective-permute-start(bf16[5,48,384]{2,1,0:T(8,128)(2,1)S(1)} %pad.4), channel_id=1, source_target_pairs={{0,16},{16,32},{32,48},{48,0},{1,17},{17,33},{33,49},{49,1},{2,18}... | collective-permute-start | bytes 552968 | tf_op jit(solution)/shard_map/ppermute | solution.py:369
  18.9 9.1 %collective-permute-start.4 = (bf16[5,48,384]{2,1,0:T(8,128)(2,1)S(1)}, bf16[5,48,384]{2,1,0:T(8,128)(2,1)S(1)}, u32[]{:S(2)}, u32[]{:S(2)}) collective-permute-start(bf16[5,48,384]{2,1,0:T(8,128)(2,1)S(1)} %pad.4), channel_id=1, source_target_pairs={{0,32},{16,48},{32,0},{48,16},{1,33},{17,49},{33,1},{49,17},{2,34}... | collective-permute-start | bytes 552968 | tf_op jit(solution)/shard_map/ppermute | solution.py:369
  21.5 6.5 %collective-permute-start.5 = (bf16[5,48,384]{2,1,0:T(8,128)(2,1)S(1)}, bf16[5,48,384]{2,1,0:T(8,128)(2,1)S(1)}, u32[]{:S(2)}, u32[]{:S(2)}) collective-permute-start(bf16[5,48,384]{2,1,0:T(8,128)(2,1)S(1)} %pad.4), channel_id=1, source_target_pairs={{0,48},{16,0},{32,16},{48,32},{1,49},{17,1},{33,17},{49,33},{2,50}... | collective-permute-start | bytes 552968 | tf_op jit(solution)/shard_map/ppermute | solution.py:369
  22.8 14.5 %copy-start.11 = (bf16[96,3,192]{2,0,1:T(8,128)(2,1)S(1)}, bf16[96,3,192]{2,0,1:T(8,128)(2,1)}, u32[]{:S(2)}) copy-start(bf16[96,3,192]{2,0,1:T(8,128)(2,1)} %param.11) | copy-start | bytes 331780
  25.4 12.4 %copy-start.2 = (bf16[272,1536]{1,0:T(8,128)(2,1)}, bf16[272,1536]{1,0:T(8,128)(2,1)S(1)}, u32[]{:S(2)}) copy-start(bf16[272,1536]{1,0:T(8,128)(2,1)S(1)} %shard_map.94.refs_0_) | copy-start | bytes 2506756
  25.4 12.1 %copy-start.12 = (bf16[192,96]{1,0:T(8,128)(2,1)S(1)}, bf16[192,96]{1,0:T(8,128)(2,1)}, u32[]{:S(2)}) copy-start(bf16[192,96]{1,0:T(8,128)(2,1)} %param.12) | copy-start | bytes 110596
  25.4 12.3 %copy-start.8 = (bf16[1,128,1536]{2,1,0:T(8,128)(2,1)S(1)}, bf16[1,128,1536]{2,1,0:T(8,128)(2,1)}, u32[]{:S(2)}) copy-start(bf16[1,128,1536]{2,1,0:T(8,128)(2,1)} %param.13) | copy-start | bytes 1179652
  28.2 9.7 %collective-permute-start.10 = (bf16[4,5,48,384]{3,2,1,0:T(8,128)(2,1)S(1)}, bf16[4,5,48,384]{3,2,1,0:T(8,128)(2,1)S(1)}, u32[]{:S(2)}, u32[]{:S(2)}) collective-permute-start(bf16[4,5,48,384]{3,2,1,0:T(8,128)(2,1)S(1)} %pad_maximum_fusion.refs_5_), channel_id=1, source_target_pairs={{0,8},{8,0},{1,9},{9,1},{2,10},{10,2},{3,11},{11,3},{4,12},{12,4},... | collective-permute-start | bytes 2211848 | tf_op jit(solution)/shard_map/ppermute | solution.py:374
  31.3 25.4 %collective-permute-start.8 = (bf16[272,1536]{1,0:T(8,128)(2,1)S(1)}, bf16[272,1536]{1,0:T(8,128)(2,1)}, u32[]{:S(2)}, u32[]{:S(2)}) collective-permute-start(bf16[272,1536]{1,0:T(8,128)(2,1)S(1)} %shard_map.94.refs_0_), channel_id=1, source_target_pairs={{0,1},{1,2},{2,3},{3,0},{4,5},{5,6},{6,7},{7,4},{8,9},{9,10},{10,1... | collective-permute-start | bytes 2506760 | tf_op jit(solution)/shard_map/ppermute | solution.py:373
  31.6 25.0 %collective-permute-start.9 = (bf16[272,1536]{1,0:T(8,128)(2,1)S(1)}, bf16[272,1536]{1,0:T(8,128)(2,1)}, u32[]{:S(2)}, u32[]{:S(2)}) collective-permute-start(bf16[272,1536]{1,0:T(8,128)(2,1)S(1)} %shard_map.94.refs_0_), channel_id=1, source_target_pairs={{0,3},{1,0},{2,1},{3,2},{4,7},{5,4},{6,5},{7,6},{8,11},{9,8},{10,9... | collective-permute-start | bytes 2506760 | tf_op jit(solution)/shard_map/ppermute | solution.py:373
  33.9 19.8 %collective-permute-start.7 = (bf16[4,5,48,384]{3,2,1,0:T(8,128)(2,1)S(1)}, bf16[4,5,48,384]{3,2,1,0:T(8,128)(2,1)}, u32[]{:S(2)}, u32[]{:S(2)}) collective-permute-start(bf16[4,5,48,384]{3,2,1,0:T(8,128)(2,1)S(1)} %pad_maximum_fusion.refs_5_), channel_id=1, source_target_pairs={{0,4},{4,64},{64,68},{68,0},{1,5},{5,65},{65,69},{69,1},{2,6},{6,6... | collective-permute-start | bytes 2211848 | tf_op jit(solution)/shard_map/ppermute | solution.py:372
  35.2 19.5 %collective-permute-start.11 = (bf16[4,5,48,384]{3,2,1,0:T(8,128)(2,1)S(1)}, bf16[4,5,48,384]{3,2,1,0:T(8,128)(2,1)}, u32[]{:S(2)}, u32[]{:S(2)}) collective-permute-start(bf16[4,5,48,384]{3,2,1,0:T(8,128)(2,1)S(1)} %pad_maximum_fusion.refs_5_), channel_id=1, source_target_pairs={{0,68},{4,0},{64,4},{68,64},{1,69},{5,1},{65,5},{69,65},{2,70},{6,... | collective-permute-start | bytes 2211848 | tf_op jit(solution)/shard_map/ppermute | solution.py:372
  37.8 25.1 %collective-permute-start.17 = (bf16[176,1536]{1,0:T(8,128)(2,1)S(1)}, bf16[176,1536]{1,0:T(8,128)(2,1)S(1)}, u32[]{:S(2)}, u32[]{:S(2)}) collective-permute-start(bf16[176,1536]{1,0:T(8,128)(2,1)S(1)} %pad_maximum_fusion.1), channel_id=1, source_target_pairs={{0,0},{4,8},{8,4},{12,12},{1,1},{5,9},{9,5},{13,13},{2,2},{6,10},{... | collective-permute-start | bytes 1622024 | tf_op jit(solution)/shard_map/ppermute | solution.py:338
  53.7 23.9 %collective-permute-start.12 = (bf16[4,5,48,384]{3,2,1,0:T(8,128)(2,1)S(1)}, bf16[4,5,48,384]{3,2,1,0:T(8,128)(2,1)}, u32[]{:S(2)}, u32[]{:S(2)}) collective-permute-start(bf16[4,5,48,384]{3,2,1,0:T(8,128)(2,1)S(1)} %pad_maximum_fusion.refs_5_), channel_id=1, source_target_pairs={{0,64},{4,68},{64,0},{68,4},{1,65},{5,69},{65,1},{69,5},{2,66},{6,... | collective-permute-start | bytes 2211848 | tf_op jit(solution)/shard_map/ppermute | solution.py:372
  54.8 22.8 %collective-permute-start.16 = (bf16[4,5,48,384]{3,2,1,0:T(8,128)(2,1)}, bf16[4,5,48,384]{3,2,1,0:T(8,128)(2,1)}, u32[]{:S(2)}, u32[]{:S(2)}) collective-permute-start(bf16[4,5,48,384]{3,2,1,0:T(8,128)(2,1)} %collective-permute-done.11.refs_7_), channel_id=1, source_target_pairs={{0,8},{8,0},{1,9},{9,1},{2,10},{10,2},{3,11},{11,3},{4,12},{12,4},... | collective-permute-start | bytes 2211848 | tf_op jit(solution)/shard_map/ppermute | solution.py:342
  56.6 21.0 %collective-permute-start.15 = (bf16[4,5,48,384]{3,2,1,0:T(8,128)(2,1)}, bf16[4,5,48,384]{3,2,1,0:T(8,128)(2,1)S(1)}, u32[]{:S(2)}, u32[]{:S(2)}) collective-permute-start(bf16[4,5,48,384]{3,2,1,0:T(8,128)(2,1)} %collective-permute-done.7.refs_6_), channel_id=1, source_target_pairs={{0,8},{8,0},{1,9},{9,1},{2,10},{10,2},{3,11},{11,3},{4,12},{12,4},... | collective-permute-start | bytes 2211848 | tf_op jit(solution)/shard_map/ppermute | solution.py:342
  58.5 19.1 %collective-permute-start.14 = (bf16[144,1536]{1,0:T(8,128)(2,1)}, bf16[144,1536]{1,0:T(8,128)(2,1)S(1)}, u32[]{:S(2)}, u32[]{:S(2)}) collective-permute-start(bf16[144,1536]{1,0:T(8,128)(2,1)} %slice.42), channel_id=1, source_target_pairs={{0,3},{1,0},{2,1},{3,2},{4,7},{5,4},{6,5},{7,6},{8,11},{9,8},{10,9... | collective-permute-start | bytes 1327112 | tf_op jit(solution)/shard_map/ppermute | solution.py:33
  62.9 0.8 copy-start.7
  62.9 14.7 %collective-permute-start.13 = (bf16[128,1536]{1,0:T(8,128)(2,1)}, bf16[128,1536]{1,0:T(8,128)(2,1)}, u32[]{:S(2)}, u32[]{:S(2)}) collective-permute-start(bf16[128,1536]{1,0:T(8,128)(2,1)} %slice.41), channel_id=1, source_target_pairs={{0,1},{1,2},{2,3},{3,0},{4,5},{5,6},{6,7},{7,4},{8,9},{9,10},{10,1... | collective-permute-start | bytes 1179656 | tf_op jit(solution)/shard_map/ppermute | solution.py:32
  77.7 100.3 %reduce-scatter.2.cloned.1.call-start = ((), (), s32[]{:S(2)}) async-start(), calls=%async_computation.4 | async-start | bytes 3538944 | tf_op jit(solution)/shard_map/reduce_scatter | solution.py:390
  77.7 6.2 %collective-permute-start.18 = (bf16[4,5,48,384]{3,2,1,0:T(8,128)(2,1)}, bf16[4,5,48,384]{3,2,1,0:T(8,128)(2,1)}, u32[]{:S(2)}, u32[]{:S(2)}) collective-permute-start(bf16[4,5,48,384]{3,2,1,0:T(8,128)(2,1)} %collective-permute-done.12.refs_8_), channel_id=1, source_target_pairs={{0,8},{8,0},{1,9},{9,1},{2,10},{10,2},{3,11},{11,3},{4,12},{12,4},... | collective-permute-start | bytes 2211848 | tf_op jit(solution)/shard_map/ppermute | solution.py:342
  79.2 41.9 %copy-start.1 = (s32[4]{0:T(128)}, s32[4]{0:T(128)S(1)}, u32[]{:S(2)}) copy-start(s32[4]{0:T(128)S(1)} %pad_add_fusion.pos_ref) | copy-start | bytes 52
  79.2 28.4 %collective-permute-start.29 = (bf16[4,96,768]{2,1,0:T(8,128)(2,1)S(1)}, bf16[4,96,768]{2,1,0:T(8,128)(2,1)S(1)}, u32[]{:S(2)}, u32[]{:S(2)}) collective-permute-start(bf16[4,96,768]{2,1,0:T(8,128)(2,1)S(1)} %all_gather.6.refs_11_), channel_id=1, source_target_pairs={{0,4},{4,64},{64,68},{68,0},{1,5},{5,65},{65,69},{69,1},{2,6},{6,6... | collective-permute-start | bytes 1769480 | tf_op jit(solution)/shard_map/ppermute | solution.py:38
  80.3 27.5 %collective-permute-start.30 = (bf16[4,96,768]{2,1,0:T(8,128)(2,1)S(1)}, bf16[4,96,768]{2,1,0:T(8,128)(2,1)S(1)}, u32[]{:S(2)}, u32[]{:S(2)}) collective-permute-start(bf16[4,96,768]{2,1,0:T(8,128)(2,1)S(1)} %all_gather.6.refs_11_), channel_id=1, source_target_pairs={{0,68},{4,0},{64,4},{68,64},{1,69},{5,1},{65,5},{69,65},{2,70},{6,... | collective-permute-start | bytes 1769480 | tf_op jit(solution)/shard_map/ppermute | solution.py:39
  95.5 24.5 %copy-start.13 = (f32[1536]{0:T(1024)S(1)}, f32[1536]{0:T(1024)}, u32[]{:S(2)}) copy-start(f32[1536]{0:T(1024)} %param.10) | copy-start | bytes 18436
  95.5 9.5 %collective-permute-start.19 = (bf16[512,384]{1,0:T(8,128)(2,1)S(1)}, bf16[512,384]{1,0:T(8,128)(2,1)S(1)}, u32[]{:S(2)}, u32[]{:S(2)}) collective-permute-start(bf16[512,384]{1,0:T(8,128)(2,1)S(1)} %shard_map.95), channel_id=1, source_target_pairs={{0,0},{4,8},{8,4},{12,12},{1,1},{5,9},{9,5},{13,13},{2,2},{6,10},{... | collective-permute-start | bytes 1179656 | tf_op jit(solution)/shard_map/ppermute | solution.py:338
  105.0 8.5 %collective-permute-start.20 = (bf16[512,384]{1,0:T(8,128)(2,1)S(1)}, bf16[512,384]{1,0:T(8,128)(2,1)S(1)}, u32[]{:S(2)}, u32[]{:S(2)}) collective-permute-start(bf16[512,384]{1,0:T(8,128)(2,1)S(1)} %collective-permute-done.19.refs_0_), channel_id=1, source_target_pairs={{0,1},{1,2},{2,3},{3,0},{4,5},{5,6},{6,7},{7,4},{8,9},{9,10},{10,1... | collective-permute-start | bytes 1179656 | tf_op jit(solution)/shard_map/ppermute | solution.py:38
  105.0 8.7 %collective-permute-start.21 = (bf16[512,384]{1,0:T(8,128)(2,1)S(1)}, bf16[512,384]{1,0:T(8,128)(2,1)S(1)}, u32[]{:S(2)}, u32[]{:S(2)}) collective-permute-start(bf16[512,384]{1,0:T(8,128)(2,1)S(1)} %collective-permute-done.19.refs_0_), channel_id=1, source_target_pairs={{0,3},{1,0},{2,1},{3,2},{4,7},{5,4},{6,5},{7,6},{8,11},{9,8},{10,9... | collective-permute-start | bytes 1179656 | tf_op jit(solution)/shard_map/ppermute | solution.py:39
  107.7 9.8 %collective-permute-start.31 = (bf16[2,96,768]{2,1,0:T(8,128)(2,1)S(1)}, bf16[2,96,768]{2,1,0:T(8,128)(2,1)S(1)}, u32[]{:S(2)}, u32[]{:S(2)}) collective-permute-start(bf16[2,96,768]{2,1,0:T(8,128)(2,1)S(1)} %slice.56), channel_id=1, source_target_pairs={{0,4},{4,64},{64,68},{68,0},{1,5},{5,65},{65,69},{69,1},{2,6},{6,6... | collective-permute-start | bytes 884744 | tf_op jit(solution)/shard_map/ppermute | solution.py:32
  107.8 13.4 %copy-start.10 = (bf16[4,96,768]{2,1,0:T(8,128)(2,1)}, bf16[4,96,768]{2,1,0:T(8,128)(2,1)S(1)}, u32[]{:S(2)}) copy-start(bf16[4,96,768]{2,1,0:T(8,128)(2,1)S(1)} %collective-permute-done.30.refs_13_) | copy-start | bytes 1769476
  107.8 9.6 %collective-permute-start.32 = (bf16[2,96,768]{2,1,0:T(8,128)(2,1)S(1)}, bf16[2,96,768]{2,1,0:T(8,128)(2,1)S(1)}, u32[]{:S(2)}, u32[]{:S(2)}) collective-permute-start(bf16[2,96,768]{2,1,0:T(8,128)(2,1)S(1)} %slice.57), channel_id=1, source_target_pairs={{0,68},{4,0},{64,4},{68,64},{1,69},{5,1},{65,5},{69,65},{2,70},{6,... | collective-permute-start | bytes 884744 | tf_op jit(solution)/shard_map/ppermute | solution.py:33
  110.5 9.4 %collective-permute-start.24 = (bf16[512,384]{1,0:T(8,128)(2,1)S(1)}, bf16[512,384]{1,0:T(8,128)(2,1)S(1)}, u32[]{:S(2)}, u32[]{:S(2)}) collective-permute-start(bf16[512,384]{1,0:T(8,128)(2,1)S(1)} %collective-permute-done.19.refs_0_), channel_id=1, source_target_pairs={{0,8},{8,0},{1,9},{9,1},{2,10},{10,2},{3,11},{11,3},{4,12},{12,4},... | collective-permute-start | bytes 1179656 | tf_op jit(solution)/shard_map/ppermute | solution.py:342
  113.4 6.0 %collective-permute-start.22 = (bf16[256,384]{1,0:T(8,128)(2,1)S(1)}, bf16[256,384]{1,0:T(8,128)(2,1)S(1)}, u32[]{:S(2)}, u32[]{:S(2)}) collective-permute-start(bf16[256,384]{1,0:T(8,128)(2,1)S(1)} %slice.54), channel_id=1, source_target_pairs={{0,1},{1,2},{2,3},{3,0},{4,5},{5,6},{6,7},{7,4},{8,9},{9,10},{10,1... | collective-permute-start | bytes 589832 | tf_op jit(solution)/shard_map/ppermute | solution.py:32
  113.7 5.7 %collective-permute-start.23 = (bf16[256,384]{1,0:T(8,128)(2,1)S(1)}, bf16[256,384]{1,0:T(8,128)(2,1)S(1)}, u32[]{:S(2)}, u32[]{:S(2)}) collective-permute-start(bf16[256,384]{1,0:T(8,128)(2,1)S(1)} %slice.55), channel_id=1, source_target_pairs={{0,3},{1,0},{2,1},{3,2},{4,7},{5,4},{6,5},{7,6},{8,11},{9,8},{10,9... | collective-permute-start | bytes 589832 | tf_op jit(solution)/shard_map/ppermute | solution.py:33
  117.4 3.7 %collective-permute-start.25 = (bf16[512,384]{1,0:T(8,128)(2,1)S(1)}, bf16[512,384]{1,0:T(8,128)(2,1)S(1)}, u32[]{:S(2)}, u32[]{:S(2)}) collective-permute-start(bf16[512,384]{1,0:T(8,128)(2,1)S(1)} %collective-permute-done.20.refs_1_), channel_id=1, source_target_pairs={{0,8},{8,0},{1,9},{9,1},{2,10},{10,2},{3,11},{11,3},{4,12},{12,4},... | collective-permute-start | bytes 1179656 | tf_op jit(solution)/shard_map/ppermute | solution.py:342
  117.4 3.7 %collective-permute-start.26 = (bf16[512,384]{1,0:T(8,128)(2,1)S(1)}, bf16[512,384]{1,0:T(8,128)(2,1)S(1)}, u32[]{:S(2)}, u32[]{:S(2)}) collective-permute-start(bf16[512,384]{1,0:T(8,128)(2,1)S(1)} %collective-permute-done.21.refs_2_), channel_id=1, source_target_pairs={{0,8},{8,0},{1,9},{9,1},{2,10},{10,2},{3,11},{11,3},{4,12},{12,4},... | collective-permute-start | bytes 1179656 | tf_op jit(solution)/shard_map/ppermute | solution.py:342
  119.4 1.4 collective-permute-start.27
  119.4 1.7 collective-permute-start.28
  132.7 0.8 copy-start.3
  150.2 41.6 %all-to-all-start = ((bf16[16,96,768]{2,1,0:T(8,128)(2,1)}), bf16[16,96,768]{2,1,0:T(8,128)(2,1)S(1)}, u32[]{:S(2)}, u32[]{:S(2)}) async-start(bf16[16,96,768]{2,1,0:T(8,128)(2,1)} %shard_map.97), calls=%async_computation | async-start | bytes 4718592 | tf_op jit(solution)/shard_map/all_to_all | solution.py:392
  191.8 3.2 %copy-start.4 = (bf16[16,96,768]{2,1,0:T(8,128)(2,1)}, bf16[16,96,768]{2,1,0:T(8,128)(2,1)S(1)}, u32[]{:S(2)}) copy-start(bf16[16,96,768]{2,1,0:T(8,128)(2,1)S(1)} %all-to-all-done.parts_ref) | copy-start | bytes 7077892
  191.8 13.9 %collective-permute-start.35 = (bf16[128,1536]{1,0:T(8,128)(2,1)S(1)}, bf16[128,1536]{1,0:T(8,128)(2,1)S(1)}, u32[]{:S(2)}, u32[]{:S(2)}) collective-permute-start(bf16[128,1536]{1,0:T(8,128)(2,1)S(1)} %add_convert_fusion), channel_id=1, source_target_pairs={{0,0},{4,8},{8,4},{12,12},{1,1},{5,9},{9,5},{13,13},{2,2},{6,10},{... | collective-permute-start | bytes 1179656 | tf_op jit(solution)/shard_map/ppermute | solution.py:338
  197.6 8.1 %collective-permute-start.33 = (bf16[96,768]{1,0:T(8,128)(2,1)}, bf16[96,768]{1,0:T(8,128)(2,1)S(1)}, u32[]{:S(2)}, u32[]{:S(2)}) collective-permute-start(bf16[96,768]{1,0:T(8,128)(2,1)} %shard_map.98), channel_id=1, source_target_pairs={{0,0},{4,8},{8,4},{12,12},{1,1},{5,9},{9,5},{13,13},{2,2},{6,10},{... | collective-permute-start | bytes 442376 | tf_op jit(solution)/shard_map/ppermute | solution.py:338
  200.9 4.8 %collective-permute-start.34 = (bf16[96,192]{1,0:T(8,128)(2,1)S(1)}, bf16[96,192]{1,0:T(8,128)(2,1)S(1)}, u32[]{:S(2)}, u32[]{:S(2)}) collective-permute-start(bf16[96,192]{1,0:T(8,128)(2,1)S(1)} %slice.58), channel_id=1, source_target_pairs={{0,64},{4,72},{8,68},{12,76},{64,0},{68,8},{72,4},{76,12},{1,65},{... | collective-permute-start | bytes 110600 | tf_op jit(solution)/shard_map/ppermute | solution.py:396
  206.7 19.2 %all-to-all-start.1 = ((bf16[8,96,576]{2,1,0:T(8,128)(2,1)}), bf16[8,96,576]{2,1,0:T(8,128)(2,1)S(1)}, u32[]{:S(2)}, u32[]{:S(2)}) async-start(bf16[8,96,576]{2,1,0:T(8,128)(2,1)} %broadcast_in_dim.56), calls=%async_computation.2 | async-start | bytes 1966080 | tf_op jit(solution)/shard_map/all_to_all | solution.py:400
  210.8 7.6 %collective-permute-start.36 = (bf16[2,96,192]{2,1,0:T(8,128)(2,1)S(1)}, bf16[2,96,192]{2,1,0:T(8,128)(2,1)S(1)}, u32[]{:S(2)}, u32[]{:S(2)}) collective-permute-start(bf16[2,96,192]{2,1,0:T(8,128)(2,1)S(1)} %get-tuple-element.66), channel_id=1, source_target_pairs={{0,16},{16,32},{32,48},{48,0},{1,17},{17,33},{33,49},{49,1},{2,18}... | collective-permute-start | bytes 221192 | tf_op jit(solution)/shard_map/ppermute | solution.py:399
  210.9 7.5 %collective-permute-start.37 = (bf16[2,96,192]{2,1,0:T(8,128)(2,1)S(1)}, bf16[2,96,192]{2,1,0:T(8,128)(2,1)S(1)}, u32[]{:S(2)}, u32[]{:S(2)}) collective-permute-start(bf16[2,96,192]{2,1,0:T(8,128)(2,1)S(1)} %get-tuple-element.66), channel_id=1, source_target_pairs={{0,32},{16,48},{32,0},{48,16},{1,33},{17,49},{33,1},{49,17},{2,34}... | collective-permute-start | bytes 221192 | tf_op jit(solution)/shard_map/ppermute | solution.py:399
  212.6 6.1 %collective-permute-start.38 = (bf16[2,96,192]{2,1,0:T(8,128)(2,1)S(1)}, bf16[2,96,192]{2,1,0:T(8,128)(2,1)S(1)}, u32[]{:S(2)}, u32[]{:S(2)}) collective-permute-start(bf16[2,96,192]{2,1,0:T(8,128)(2,1)S(1)} %get-tuple-element.66), channel_id=1, source_target_pairs={{0,48},{16,0},{32,16},{48,32},{1,49},{17,1},{33,17},{49,33},{2,50}... | collective-permute-start | bytes 221192 | tf_op jit(solution)/shard_map/ppermute | solution.py:399
  218.7 2.8 %copy-start.6 = (bf16[4,2,96,192]{3,2,1,0:T(8,128)(2,1)}, bf16[4,2,96,192]{3,2,1,0:T(8,128)(2,1)S(1)}, u32[]{:S(2)}) copy-start(bf16[4,2,96,192]{3,2,1,0:T(8,128)(2,1)S(1)} %pad_maximum_fusion.2.own_ref) | copy-start | bytes 884740
  218.7 2.8 %collective-permute-start.39 = (bf16[4,2,96,192]{3,2,1,0:T(8,128)(2,1)S(1)}, bf16[4,2,96,192]{3,2,1,0:T(8,128)(2,1)S(1)}, u32[]{:S(2)}, u32[]{:S(2)}) collective-permute-start(bf16[4,2,96,192]{3,2,1,0:T(8,128)(2,1)S(1)} %pad_maximum_fusion.2.own_ref), channel_id=1, source_target_pairs={{0,8},{8,0},{1,9},{9,1},{2,10},{10,2},{3,11},{11,3},{4,12},{12,4},... | collective-permute-start | bytes 884744 | tf_op jit(solution)/shard_map/ppermute | solution.py:402
  221.5 0.8 copy-start.9
  225.9 1.0 copy-start.5
Sparse Core Ops, SparseCore 0:
  77.8 31.0 all-gather.1
  133.7 44.2 reduce-scatter.1

commit v4 on v3

--- a/solution.py
+++ b/solution.py
@@ -18,7 +18,7 @@
 KW = 5
 EPS = 1e-06
 HALO = 16
-ROWS = 512
+ROWS = 1024
 
 bf16 = jnp.bfloat16
 f32 = jnp.float32
@@ -248,19 +248,20 @@
     )(qkv, cot, wo, normed, mixed)
 
 
-def total_kernel(parts_ref, out_ref):
+def total_kernel(parts_ref, out_ref, rows_ref):
     total = parts_ref[0].astype(f32)
     for g in range(1, 16):
         total = total + parts_ref[g].astype(f32)
     out_ref[...] = total.astype(bf16)
+    rows_ref[...] = total[:, 3 * HD :].astype(bf16)
 
 
 def total_parts(parts):
     return pl.pallas_call(
         total_kernel,
-        out_shape=jax.ShapeDtypeStruct((96, 768), bf16),
+        out_shape=(jax.ShapeDtypeStruct((96, 768), bf16), jax.ShapeDtypeStruct((96, HD), bf16)),
         in_specs=[VMEM],
-        out_specs=VMEM,
+        out_specs=[VMEM] * 2,
     )(parts)
 
 
@@ -390,16 +391,16 @@
     attended = lax.psum_scatter(partial, ("c", "x"), scatter_dimension=0, tiled=True)
     block_out = (own.astype(f32) + attended.astype(f32)).astype(bf16)
     parts = lax.all_to_all(backward(qkv, cot, wo, normed, mixed), ("zh", "y", "zl"), 0, 0)
-    parts, block_out = lax.optimization_barrier((parts, block_out))
-
-    sums = total_parts(parts)
-    rows = lax.ppermute(sums[:, 3 * HD :], ("zh", "c", "zl"), [(0, 4), (1, 6), (2, 5), (3, 7), (4, 0), (5, 2), (6, 1), (7, 3)])
-    sums, rows, block_out = lax.optimization_barrier((swap_axes(sums), rows, swap_axes(block_out)))
+    sums, rows = total_parts(parts)
+    rows = lax.ppermute(rows, ("zh", "c", "zl"), [(0, 4), (1, 6), (2, 5), (3, 7), (4, 0), (5, 2), (6, 1), (7, 3)])
+    sums, rows, block_out = lax.optimization_barrier((swap_axes(sums), rows, block_out))
+    block_out = swap_axes(block_out)
     rows = jnp.stack([sums[:, 3 * HD :], rows])
     rows = jnp.stack([rows] + [lax.ppermute(rows, "y", ring(4, k)) for k in (1, 2, 3)])
     heads = lax.all_to_all(jnp.broadcast_to(sums[None, :, : 3 * HD], (8, 96, 3 * HD)), ("zl", "x"), 0, 0)
-    proj_grad = place_proj(heads).transpose(1, 0, 2)
     out_grad = place_out(pos, rows, lax.ppermute(rows, "c", ring(2, 1)))
+    proj_grad, block_out = lax.optimization_barrier((place_proj(heads), block_out))
+    proj_grad = proj_grad.transpose(1, 0, 2)
     return (block_out[None], proj_grad, out_grad)
 
 

time: 238 us -> 232 us (0.975)
  blocking collectives: 12 us -> 50.1 us
  waiting for transfers between devices: 75.2 us -> 38.5 us
  starting transfers between devices: 68.3 us -> 62.3 us
    all_to_all x0 -> x1, blocking collectives: none -> 38.1 us  [per_device(): lax.all_to_all(backward(qkv, cot, wo, normed, mixed), ('zh', 'y', 'zl'),...]
    reduce_scatter x1, waiting for transfers between devices: 20.2 us -> 0.01 us  [per_device(): lax.psum_scatter(partial, ('c', 'x'), scatter_dimension=0, tiled=True)]
    all_to_all x1 -> x0, waiting for transfers between devices: 12.7 us -> none  [per_device(): lax.all_to_all(backward(qkv, cot, wo, normed, mixed), ('zh', 'y', 'zl'),...]
    all_to_all x1 -> x0, starting transfers between devices: 7.58 us -> none  [per_device(): lax.all_to_all(backward(qkv, cot, wo, normed, mixed), ('zh', 'y', 'zl'),...]
    ppermute x3, waiting for transfers between devices: 5.1 us -> 0.01 us  [per_device(): lax.ppermute(rows, 'y', ring(4, k))]
    ppermute x4, starting transfers between devices: 9.78 us -> 13.2 us  [swap_axes(): return lax.ppermute(value, ('c', 'zl'), [(0, 0), (1, 2), (2, 1), (3, 3)])]
  transfers between devices with their start and end apart: 44 -> 43, of which waited for: 16 -> 12; matrix products, arithmetic and copies ran while one was open for 4% -> 4% of each run, Pallas kernels for 20% -> 21%
where the time goes in v4:
time: 232 us; the launch traced here: 231 us
  starting transfers between devices  62.3 us (27%)
  blocking collectives  50.1 us (22%)
  Pallas kernels  49.5 us (21%)
  waiting for transfers between devices  38.5 us (17%)
  between operations  14.6 us (6%)
  local copies, waits for them, and re-layouts  13.6 us (6%)
  other arithmetic  2.49 us (1%)
    all_to_all x1, blocking collectives, per_device(): lax.all_to_all(backward(qkv, cot, wo, normed, mixed), ('zh', 'y', 'zl'),...  38.1 us
    pallas_call x1, Pallas kernels, backward(): pl.pallas_call(backward_kernel, out_shape=jax.ShapeDtypeStruct((16, 96, 7...  16.5 us
    ppermute x3, waiting for transfers between devices, per_device(): zpieces = [lax.ppermute(ypieces, zring, ring(4, k)) for k in (1, -1, 2)]  13.5 us
    ppermute x4, starting transfers between devices, swap_axes(): return lax.ppermute(value, ('c', 'zl'), [(0, 0), (1, 2), (2, 1), (3, 3)])  13.2 us
    all_gather x1, blocking collectives, per_device(): head_w = lax.all_gather(later[128:].reshape(96, 768), 'y', axis=0)  12.1 us
    pallas_call x1, Pallas kernels, forward(): pl.pallas_call(forward_kernel, out_shape=(jax.ShapeDtypeStruct((TOKENS, D...  11.5 us
    pallas_call x1, Pallas kernels, conv_pool(): pl.pallas_call(conv_kernel, out_shape=jax.ShapeDtypeStruct((512, OUTC), b...  11.2 us
    ppermute x4, waiting for transfers between devices, swap_axes(): return lax.ppermute(value, ('c', 'zl'), [(0, 0), (1, 2), (2, 1), (3, 3)])  9.3 us
  transfers between devices with their start and end apart: 43, of which 12 were waited for; matrix products, arithmetic and copies ran while one was open for 4% of the time, Pallas kernels for 21%

profile of v4, /device:TPU:1, one launch (start us, length us, event | category | flops | bytes accessed | tf_op | source)
XLA Modules:
  0.0 231.2 jit_solution(13832679828498253603)
XLA Ops:
  7.3 1.1 reshape.354
  8.8 2.1 collective-permute-start
  10.9 2.5 %collective-permute-start.1 = (bf16[5,11,384]{2,1,0:T(8,128)(2,1)S(1)}, bf16[5,11,384]{2,1,0:T(8,128)(2,1)S(1)}, u32[]{:S(2)}, u32[]{:S(2)}) collective-permute-start(bf16[5,11,384]{2,1,0:T(8,128)(2,1)S(1)} %bitcast.66), channel_id=1, source_target_pairs={{0,2},{1,3},{2,0},{3,1},{4,6},{5,7},{6,4},{7,5},{8,10},{9,11},{10,... | collective-permute-start | bytes 126728 | tf_op jit(solution)/shard_map/ppermute | solution.py:360
  13.5 1.2 collective-permute-start.2
  14.7 0.8 select_bitcast_fusion
  15.5 1.7 collective-permute-start.6
  17.5 1.4 collective-permute-start.3
  18.9 2.6 %collective-permute-start.4 = (bf16[5,48,384]{2,1,0:T(8,128)(2,1)S(1)}, bf16[5,48,384]{2,1,0:T(8,128)(2,1)S(1)}, u32[]{:S(2)}, u32[]{:S(2)}) collective-permute-start(bf16[5,48,384]{2,1,0:T(8,128)(2,1)S(1)} %pad.4), channel_id=1, source_target_pairs={{0,32},{16,48},{32,0},{48,16},{1,33},{17,49},{33,1},{49,17},{2,34}... | collective-permute-start | bytes 552968 | tf_op jit(solution)/shard_map/ppermute | solution.py:370
  21.5 1.1 collective-permute-start.5
  22.8 2.6 %shard_map.94.refs_0_ = bf16[272,1536]{1,0:T(8,128)(2,1)S(1)} custom-call(bf16[256,1408]{1,0:T(8,128)(2,1)S(1)} %bitcast.52, bf16[16,1408]{1,0:T(8,128)(2,1)S(1)} %collective-permute-done.6.edge_ref, s32[1,1536]{1,0:T(1,128)S(1)} %compare_select_fusion.10.sources_ref), custom_call_target="tpu_custom_call" | custom-call | flops 1200000000 | bytes 1600000 | tf_op jit(solution)/shard_map/pallas_call | solution.py:328
  25.5 2.6 %collective-permute-done.4 = bf16[5,48,384]{2,1,0:T(8,128)(2,1)S(1)} collective-permute-done((bf16[5,48,384]{2,1,0:T(8,128)(2,1)S(1)}, bf16[5,48,384]{2,1,0:T(8,128)(2,1)S(1)}, u32[]{:S(2)}, u32[]{:S(2)}) %collective-permute-start.4) | collective-permute-done | bytes 184352 | tf_op jit(solution)/shard_map/ppermute | solution.py:370
  28.2 3.1 %collective-permute-start.10 = (bf16[4,5,48,384]{3,2,1,0:T(8,128)(2,1)S(1)}, bf16[4,5,48,384]{3,2,1,0:T(8,128)(2,1)S(1)}, u32[]{:S(2)}, u32[]{:S(2)}) collective-permute-start(bf16[4,5,48,384]{3,2,1,0:T(8,128)(2,1)S(1)} %pad_maximum_fusion.refs_5_), channel_id=1, source_target_pairs={{0,8},{8,0},{1,9},{9,1},{2,10},{10,2},{3,11},{11,3},{4,12},{12,4},... | collective-permute-start | bytes 2211848 | tf_op jit(solution)/shard_map/ppermute | solution.py:375
  31.6 2.4 %collective-permute-start.9 = (bf16[272,1536]{1,0:T(8,128)(2,1)S(1)}, bf16[272,1536]{1,0:T(8,128)(2,1)}, u32[]{:S(2)}, u32[]{:S(2)}) collective-permute-start(bf16[272,1536]{1,0:T(8,128)(2,1)S(1)} %shard_map.94.refs_0_), channel_id=1, source_target_pairs={{0,3},{1,0},{2,1},{3,2},{4,7},{5,4},{6,5},{7,6},{8,11},{9,8},{10,9... | collective-permute-start | bytes 2506760 | tf_op jit(solution)/shard_map/ppermute | solution.py:374
  33.9 1.3 collective-permute-start.7
  35.2 2.1 collective-permute-start.11
  37.8 2.3 %collective-permute-start.17 = (bf16[176,1536]{1,0:T(8,128)(2,1)S(1)}, bf16[176,1536]{1,0:T(8,128)(2,1)S(1)}, u32[]{:S(2)}, u32[]{:S(2)}) collective-permute-start(bf16[176,1536]{1,0:T(8,128)(2,1)S(1)} %pad_maximum_fusion.1), channel_id=1, source_target_pairs={{0,0},{4,8},{8,4},{12,12},{1,1},{5,9},{9,5},{13,13},{2,2},{6,10},{... | collective-permute-start | bytes 1622024 | tf_op jit(solution)/shard_map/ppermute | solution.py:339
  40.2 13.5 %collective-permute-done.7.refs_6_ = bf16[4,5,48,384]{3,2,1,0:T(8,128)(2,1)} collective-permute-done((bf16[4,5,48,384]{3,2,1,0:T(8,128)(2,1)S(1)}, bf16[4,5,48,384]{3,2,1,0:T(8,128)(2,1)}, u32[]{:S(2)}, u32[]{:S(2)}) %collective-permute-start.7) | collective-permute-done | bytes 737312 | tf_op jit(solution)/shard_map/ppermute | solution.py:373
  53.7 1.1 collective-permute-start.12
  54.8 1.8 collective-permute-start.16
  56.7 1.8 slice.39
  58.5 0.9 collective-permute-start.14
  59.4 1.8 slice.38
  61.2 1.7 collective-permute-done.17
  62.9 0.8 copy-done.6
  63.8 1.8 slice.49
  65.6 12.1 %all_gather.6.refs_11_ = bf16[4,96,768]{2,1,0:T(8,128)(2,1)S(1)} all-gather(bf16[1,96,768]{2,1,0:T(8,128)(2,1)S(1)} %all_gather_reshape.3), channel_id=1, replica_groups=mesh['zh'=2,'y'=4,'c'=2,'zl'=2,'x'=4] {'y'}, dimensions={0}, use_global_device_ids=true | all-gather | bytes 737280 | tf_op jit(solution)/shard_map/all_gather | solution.py:368
  77.7 0.6 collective-permute-start.18
  78.4 0.8 dynamic_slice.20
  79.2 1.0 collective-permute-start.29
  80.3 3.6 %collective-permute-start.30 = (bf16[4,96,768]{2,1,0:T(8,128)(2,1)S(1)}, bf16[4,96,768]{2,1,0:T(8,128)(2,1)S(1)}, u32[]{:S(2)}, u32[]{:S(2)}) collective-permute-start(bf16[4,96,768]{2,1,0:T(8,128)(2,1)S(1)} %all_gather.6.refs_11_), channel_id=1, source_target_pairs={{0,68},{4,0},{64,4},{68,64},{1,69},{5,1},{65,5},{69,65},{2,70},{6,... | collective-permute-start | bytes 1769480 | tf_op jit(solution)/shard_map/ppermute | solution.py:39
  83.9 11.2 %shard_map.95 = bf16[512,384]{1,0:T(8,128)(2,1)S(1)} custom-call(s32[4]{0:T(128)S(1)} %pad_add_fusion.pos_ref, bf16[272,1536]{1,0:T(8,128)(2,1)} %copy-done.2, bf16[272,1536]{1,0:T(8,128)(2,1)} %collective-permute-done.8.refs_1_, bf16[272,1536]{1,0:T(8,128)(2,1)} %collective-permute-done.9.refs_2_, bf16[128,1536]{1,0:T(8,128)(2,1)} %collective-permute-done.13.refs_3_, ...), custom_call_target="tpu_custom_call" | custom-call | flops 6000000000 | bytes 9000000 | tf_op jit(solution)/shard_map/pallas_call | solution.py:94
  95.1 1.9 collective-permute-start.19
  97.0 7.6 %collective-permute-done.19.refs_0_ = bf16[512,384]{1,0:T(8,128)(2,1)S(1)} collective-permute-done((bf16[512,384]{1,0:T(8,128)(2,1)S(1)}, bf16[512,384]{1,0:T(8,128)(2,1)S(1)}, u32[]{:S(2)}, u32[]{:S(2)}) %collective-permute-start.19) | collective-permute-done | bytes 393248 | tf_op jit(solution)/shard_map/ppermute | solution.py:339
  104.6 2.7 %collective-permute-start.21 = (bf16[512,384]{1,0:T(8,128)(2,1)S(1)}, bf16[512,384]{1,0:T(8,128)(2,1)S(1)}, u32[]{:S(2)}, u32[]{:S(2)}) collective-permute-start(bf16[512,384]{1,0:T(8,128)(2,1)S(1)} %collective-permute-done.19.refs_0_), channel_id=1, source_target_pairs={{0,3},{1,0},{2,1},{3,2},{4,7},{5,4},{6,5},{7,6},{8,11},{9,8},{10,9... | collective-permute-start | bytes 1179656 | tf_op jit(solution)/shard_map/ppermute | solution.py:39
  107.4 2.7 %collective-permute-start.32 = (bf16[2,96,768]{2,1,0:T(8,128)(2,1)S(1)}, bf16[2,96,768]{2,1,0:T(8,128)(2,1)S(1)}, u32[]{:S(2)}, u32[]{:S(2)}) collective-permute-start(bf16[2,96,768]{2,1,0:T(8,128)(2,1)S(1)} %slice.53), channel_id=1, source_target_pairs={{0,68},{4,0},{64,4},{68,64},{1,69},{5,1},{65,5},{69,65},{2,70},{6,... | collective-permute-start | bytes 884744 | tf_op jit(solution)/shard_map/ppermute | solution.py:33
  110.1 3.3 %collective-permute-done.20.refs_1_ = bf16[512,384]{1,0:T(8,128)(2,1)S(1)} collective-permute-done((bf16[512,384]{1,0:T(8,128)(2,1)S(1)}, bf16[512,384]{1,0:T(8,128)(2,1)S(1)}, u32[]{:S(2)}, u32[]{:S(2)}) %collective-permute-start.20) | collective-permute-done | bytes 393248 | tf_op jit(solution)/shard_map/ppermute | solution.py:38
  113.7 2.6 %collective-permute-start.23 = (bf16[256,384]{1,0:T(8,128)(2,1)S(1)}, bf16[256,384]{1,0:T(8,128)(2,1)S(1)}, u32[]{:S(2)}, u32[]{:S(2)}) collective-permute-start(bf16[256,384]{1,0:T(8,128)(2,1)S(1)} %slice.51), channel_id=1, source_target_pairs={{0,3},{1,0},{2,1},{3,2},{4,7},{5,4},{6,5},{7,6},{8,11},{9,8},{10,9... | collective-permute-start | bytes 589832 | tf_op jit(solution)/shard_map/ppermute | solution.py:33
  116.3 0.8 collective-permute-done.31.refs_14_
  117.1 0.5 collective-permute-start.26
  117.6 1.7 collective-permute-done.22.refs_3_
  119.3 0.5 collective-permute-start.28
  119.8 0.9 collective-permute-done.27.refs_8_
  121.0 11.5 %shard_map.96 = (bf16[1024,1536]{1,0:T(8,128)(2,1)}, bf16[3,1024,256]{2,1,0:T(8,128)(2,1)}, bf16[1024,256]{1,0:T(8,128)(2,1)S(1)}, bf16[1024,1536]{1,0:T(8,128)(...) custom-call(s32[4]{0:T(128)S(1)} %pad_add_fusion.pos_ref, ...), custom_call_target="tpu_custom_call" | custom-call | flops 4000000000 | bytes 16000000 | tf_op jit(solution)/shard_map/pallas_call | solution.py:173
  132.5 0.8 copy-done.3
  133.4 16.5 %shard_map.97 = bf16[16,96,768]{2,1,0:T(8,128)(2,1)} custom-call(bf16[3,1024,256]{2,1,0:T(8,128)(2,1)} %get-tuple-element.51.qkv_ref, bf16[1024,1536]{1,0:T(8,128)(2,1)} %all-gather.2.cloned.1.call-done.cot_ref, bf16[1536,256]{1,0:T(8,128)(2,1)} %get-tuple-element.53.wo, bf16[1024,1536]{1,0:T(8,128)(2,1)} %get-tuple-element.54.normed_ref, ...), custom_call_target="tpu_custom_call" | custom-call | flops 6000000000 | bytes 18000000 | tf_op jit(solution)/shard_map/pallas_call | solution.py:234
  149.9 38.1 %all_to_all.10.parts_ref = bf16[16,96,768]{2,1,0:T(8,128)(2,1)} all-to-all(bf16[16,96,768]{2,1,0:T(8,128)(2,1)} %shard_map.97), channel_id=1, replica_groups=mesh['zh'=2,'y'=4,'c'=2,'zl'=2,'x'=4] {'zh','y','zl'}, dimensions={0} | all-to-all | bytes 4718592 | tf_op jit(solution)/shard_map/all_to_all | solution.py:393
  188.0 2.7 %shard_map.98 = (bf16[96,768]{1,0:T(8,128)(2,1)}, bf16[96,192]{1,0:T(8,128)(2,1)}) custom-call(bf16[16,96,768]{2,1,0:T(8,128)(2,1)} %all_to_all.10.parts_ref), custom_call_target="tpu_custom_call" | custom-call | tf_op jit(solution)/shard_map/pallas_call | solution.py:260
  190.7 3.8 %collective-permute-start.33 = (bf16[96,768]{1,0:T(8,128)(2,1)}, bf16[96,768]{1,0:T(8,128)(2,1)S(1)}, u32[]{:S(2)}, u32[]{:S(2)}) collective-permute-start(bf16[96,768]{1,0:T(8,128)(2,1)} %get-tuple-element.56), channel_id=1, source_target_pairs={{0,0},{4,8},{8,4},{12,12},{1,1},{5,9},{9,5},{13,13},{2,2},{6,10},{... | collective-permute-start | bytes 442376 | tf_op jit(solution)/shard_map/ppermute | solution.py:339
  194.5 0.7 collective-permute-start.34
  195.2 1.1 add_convert_fusion
  196.3 3.6 %collective-permute-done.34 = bf16[96,192]{1,0:T(8,128)(2,1)S(1)} collective-permute-done((bf16[96,192]{1,0:T(8,128)(2,1)}, bf16[96,192]{1,0:T(8,128)(2,1)S(1)}, u32[]{:S(2)}, u32[]{:S(2)}) %collective-permute-start.34) | collective-permute-done | bytes 36896 | tf_op jit(solution)/shard_map/ppermute | solution.py:395
  199.9 1.0 broadcast_in_dim.55
  200.9 3.9 %all-to-all-start.1 = ((bf16[8,96,576]{2,1,0:T(8,128)(2,1)}), bf16[8,96,576]{2,1,0:T(8,128)(2,1)S(1)}, u32[]{:S(2)}, u32[]{:S(2)}) async-start(bf16[8,96,576]{2,1,0:T(8,128)(2,1)} %broadcast_in_dim.55), calls=%async_computation.2 | async-start | bytes 1966080 | tf_op jit(solution)/shard_map/all_to_all | solution.py:400
  205.1 1.9 collective-permute-start.37
  206.9 0.9 collective-permute-start.38
  207.8 5.1 %collective-permute-start.35 = (bf16[128,1536]{1,0:T(8,128)(2,1)S(1)}, bf16[128,1536]{1,0:T(8,128)(2,1)S(1)}, u32[]{:S(2)}, u32[]{:S(2)}) collective-permute-start(bf16[128,1536]{1,0:T(8,128)(2,1)S(1)} %add_convert_fusion), channel_id=1, source_target_pairs={{0,0},{4,8},{8,4},{12,12},{1,1},{5,9},{9,5},{13,13},{2,2},{6,10},{... | collective-permute-start | bytes 1179656 | tf_op jit(solution)/shard_map/ppermute | solution.py:339
  213.1 1.2 collective-permute-start.39
  214.4 1.3 collective-permute-done.39.other_ref
  215.7 0.7 copy-done.8
  216.5 2.3 %shard_map.100 = f32[192,1536]{1,0:T(8,128)} custom-call(s32[4]{0:T(128)} %copy-done.1, bf16[4,2,96,192]{3,2,1,0:T(8,128)(2,1)} %copy-done.5, bf16[4,2,96,192]{3,2,1,0:T(8,128)(2,1)} %copy-done.8), custom_call_target="tpu_custom_call" | custom-call | tf_op jit(solution)/shard_map/pallas_call | solution.py:296
  218.8 1.2 all-to-all-done.1.heads_ref
  220.0 1.0 copy-done.4
  221.0 2.6 %shard_map.99 = f32[3,96,1536]{2,1,0:T(8,128)} custom-call(bf16[8,96,576]{2,1,0:T(8,128)(2,1)} %copy-done.4), custom_call_target="tpu_custom_call" | custom-call | tf_op jit(solution)/shard_map/pallas_call | solution.py:275
  223.6 0.7 copy.45
  (99 shorter events, 3.1 us)
Async XLA Ops:
  7.2 15.6 %copy-start = (bf16[1,256,1408]{2,1,0:T(8,128)(2,1)S(1)}, bf16[1,256,1408]{2,1,0:T(8,128)(2,1)}, u32[]{:S(2)}) copy-start(bf16[1,256,1408]{2,1,0:T(8,128)(2,1)} %param.7) | copy-start | bytes 2162692
  7.2 126.2 %all-gather.2.cloned.1.call-start = ((), (), s32[]{:S(2)}) async-start(), calls=%async_computation.3 | async-start | bytes 3538944 | tf_op jit(solution)/shard_map/all_gather | solution.py:380
  8.8 8.5 %collective-permute-start = (bf16[5,11,384]{2,1,0:T(8,128)(2,1)S(1)}, bf16[5,11,384]{2,1,0:T(8,128)(2,1)S(1)}, u32[]{:S(2)}, u32[]{:S(2)}) collective-permute-start(bf16[5,11,384]{2,1,0:T(8,128)(2,1)S(1)} %bitcast.67), channel_id=1, source_target_pairs={{0,1},{1,2},{2,3},{3,0},{4,5},{5,6},{6,7},{7,4},{8,9},{9,10},{10,1... | collective-permute-start | bytes 126728 | tf_op jit(solution)/shard_map/ppermute | solution.py:360
  10.9 6.4 %collective-permute-start.1 = (bf16[5,11,384]{2,1,0:T(8,128)(2,1)S(1)}, bf16[5,11,384]{2,1,0:T(8,128)(2,1)S(1)}, u32[]{:S(2)}, u32[]{:S(2)}) collective-permute-start(bf16[5,11,384]{2,1,0:T(8,128)(2,1)S(1)} %bitcast.66), channel_id=1, source_target_pairs={{0,2},{1,3},{2,0},{3,1},{4,6},{5,7},{6,4},{7,5},{8,10},{9,11},{10,... | collective-permute-start | bytes 126728 | tf_op jit(solution)/shard_map/ppermute | solution.py:360
  13.5 3.9 %collective-permute-start.2 = (bf16[5,11,384]{2,1,0:T(8,128)(2,1)S(1)}, bf16[5,11,384]{2,1,0:T(8,128)(2,1)S(1)}, u32[]{:S(2)}, u32[]{:S(2)}) collective-permute-start(bf16[5,11,384]{2,1,0:T(8,128)(2,1)S(1)} %bitcast.65), channel_id=1, source_target_pairs={{0,3},{1,0},{2,1},{3,2},{4,7},{5,4},{6,5},{7,6},{8,11},{9,8},{10,9... | collective-permute-start | bytes 126728 | tf_op jit(solution)/shard_map/ppermute | solution.py:360
  15.5 7.3 %collective-permute-start.6 = (bf16[16,1408]{1,0:T(8,128)(2,1)S(1)}, bf16[16,1408]{1,0:T(8,128)(2,1)S(1)}, u32[]{:S(2)}, u32[]{:S(2)}) collective-permute-start(bf16[16,1408]{1,0:T(8,128)(2,1)S(1)} %select_bitcast_fusion), channel_id=1, source_target_pairs={{0,4},{4,0},{1,5},{5,1},{2,6},{6,2},{3,7},{7,3},{8,12},{12,8},{9,1... | collective-permute-start | bytes 135176 | tf_op jit(solution)/shard_map/ppermute | solution.py:352
  17.5 7.9 %collective-permute-start.3 = (bf16[5,48,384]{2,1,0:T(8,128)(2,1)S(1)}, bf16[5,48,384]{2,1,0:T(8,128)(2,1)S(1)}, u32[]{:S(2)}, u32[]{:S(2)}) collective-permute-start(bf16[5,48,384]{2,1,0:T(8,128)(2,1)S(1)} %pad.4), channel_id=1, source_target_pairs={{0,16},{16,32},{32,48},{48,0},{1,17},{17,33},{33,49},{49,1},{2,18}... | collective-permute-start | bytes 552968 | tf_op jit(solution)/shard_map/ppermute | solution.py:370
  18.9 9.1 %collective-permute-start.4 = (bf16[5,48,384]{2,1,0:T(8,128)(2,1)S(1)}, bf16[5,48,384]{2,1,0:T(8,128)(2,1)S(1)}, u32[]{:S(2)}, u32[]{:S(2)}) collective-permute-start(bf16[5,48,384]{2,1,0:T(8,128)(2,1)S(1)} %pad.4), channel_id=1, source_target_pairs={{0,32},{16,48},{32,0},{48,16},{1,33},{17,49},{33,1},{49,17},{2,34}... | collective-permute-start | bytes 552968 | tf_op jit(solution)/shard_map/ppermute | solution.py:370
  21.5 6.5 %collective-permute-start.5 = (bf16[5,48,384]{2,1,0:T(8,128)(2,1)S(1)}, bf16[5,48,384]{2,1,0:T(8,128)(2,1)S(1)}, u32[]{:S(2)}, u32[]{:S(2)}) collective-permute-start(bf16[5,48,384]{2,1,0:T(8,128)(2,1)S(1)} %pad.4), channel_id=1, source_target_pairs={{0,48},{16,0},{32,16},{48,32},{1,49},{17,1},{33,17},{49,33},{2,50}... | collective-permute-start | bytes 552968 | tf_op jit(solution)/shard_map/ppermute | solution.py:370
  22.8 14.5 %copy-start.10 = (bf16[96,3,192]{2,0,1:T(8,128)(2,1)S(1)}, bf16[96,3,192]{2,0,1:T(8,128)(2,1)}, u32[]{:S(2)}) copy-start(bf16[96,3,192]{2,0,1:T(8,128)(2,1)} %param.11) | copy-start | bytes 331780
  25.4 12.4 %copy-start.2 = (bf16[272,1536]{1,0:T(8,128)(2,1)}, bf16[272,1536]{1,0:T(8,128)(2,1)S(1)}, u32[]{:S(2)}) copy-start(bf16[272,1536]{1,0:T(8,128)(2,1)S(1)} %shard_map.94.refs_0_) | copy-start | bytes 2506756
  25.4 12.1 %copy-start.11 = (bf16[192,96]{1,0:T(8,128)(2,1)S(1)}, bf16[192,96]{1,0:T(8,128)(2,1)}, u32[]{:S(2)}) copy-start(bf16[192,96]{1,0:T(8,128)(2,1)} %param.12) | copy-start | bytes 110596
  25.4 12.3 %copy-start.7 = (bf16[1,128,1536]{2,1,0:T(8,128)(2,1)S(1)}, bf16[1,128,1536]{2,1,0:T(8,128)(2,1)}, u32[]{:S(2)}) copy-start(bf16[1,128,1536]{2,1,0:T(8,128)(2,1)} %param.13) | copy-start | bytes 1179652
  28.2 9.7 %collective-permute-start.10 = (bf16[4,5,48,384]{3,2,1,0:T(8,128)(2,1)S(1)}, bf16[4,5,48,384]{3,2,1,0:T(8,128)(2,1)S(1)}, u32[]{:S(2)}, u32[]{:S(2)}) collective-permute-start(bf16[4,5,48,384]{3,2,1,0:T(8,128)(2,1)S(1)} %pad_maximum_fusion.refs_5_), channel_id=1, source_target_pairs={{0,8},{8,0},{1,9},{9,1},{2,10},{10,2},{3,11},{11,3},{4,12},{12,4},... | collective-permute-start | bytes 2211848 | tf_op jit(solution)/shard_map/ppermute | solution.py:375
  31.3 25.4 %collective-permute-start.8 = (bf16[272,1536]{1,0:T(8,128)(2,1)S(1)}, bf16[272,1536]{1,0:T(8,128)(2,1)}, u32[]{:S(2)}, u32[]{:S(2)}) collective-permute-start(bf16[272,1536]{1,0:T(8,128)(2,1)S(1)} %shard_map.94.refs_0_), channel_id=1, source_target_pairs={{0,1},{1,2},{2,3},{3,0},{4,5},{5,6},{6,7},{7,4},{8,9},{9,10},{10,1... | collective-permute-start | bytes 2506760 | tf_op jit(solution)/shard_map/ppermute | solution.py:374
  31.6 25.0 %collective-permute-start.9 = (bf16[272,1536]{1,0:T(8,128)(2,1)S(1)}, bf16[272,1536]{1,0:T(8,128)(2,1)}, u32[]{:S(2)}, u32[]{:S(2)}) collective-permute-start(bf16[272,1536]{1,0:T(8,128)(2,1)S(1)} %shard_map.94.refs_0_), channel_id=1, source_target_pairs={{0,3},{1,0},{2,1},{3,2},{4,7},{5,4},{6,5},{7,6},{8,11},{9,8},{10,9... | collective-permute-start | bytes 2506760 | tf_op jit(solution)/shard_map/ppermute | solution.py:374
  33.9 19.8 %collective-permute-start.7 = (bf16[4,5,48,384]{3,2,1,0:T(8,128)(2,1)S(1)}, bf16[4,5,48,384]{3,2,1,0:T(8,128)(2,1)}, u32[]{:S(2)}, u32[]{:S(2)}) collective-permute-start(bf16[4,5,48,384]{3,2,1,0:T(8,128)(2,1)S(1)} %pad_maximum_fusion.refs_5_), channel_id=1, source_target_pairs={{0,4},{4,64},{64,68},{68,0},{1,5},{5,65},{65,69},{69,1},{2,6},{6,6... | collective-permute-start | bytes 2211848 | tf_op jit(solution)/shard_map/ppermute | solution.py:373
  35.2 19.5 %collective-permute-start.11 = (bf16[4,5,48,384]{3,2,1,0:T(8,128)(2,1)S(1)}, bf16[4,5,48,384]{3,2,1,0:T(8,128)(2,1)}, u32[]{:S(2)}, u32[]{:S(2)}) collective-permute-start(bf16[4,5,48,384]{3,2,1,0:T(8,128)(2,1)S(1)} %pad_maximum_fusion.refs_5_), channel_id=1, source_target_pairs={{0,68},{4,0},{64,4},{68,64},{1,69},{5,1},{65,5},{69,65},{2,70},{6,... | collective-permute-start | bytes 2211848 | tf_op jit(solution)/shard_map/ppermute | solution.py:373
  37.8 25.1 %collective-permute-start.17 = (bf16[176,1536]{1,0:T(8,128)(2,1)S(1)}, bf16[176,1536]{1,0:T(8,128)(2,1)S(1)}, u32[]{:S(2)}, u32[]{:S(2)}) collective-permute-start(bf16[176,1536]{1,0:T(8,128)(2,1)S(1)} %pad_maximum_fusion.1), channel_id=1, source_target_pairs={{0,0},{4,8},{8,4},{12,12},{1,1},{5,9},{9,5},{13,13},{2,2},{6,10},{... | collective-permute-start | bytes 1622024 | tf_op jit(solution)/shard_map/ppermute | solution.py:339
  53.7 23.9 %collective-permute-start.12 = (bf16[4,5,48,384]{3,2,1,0:T(8,128)(2,1)S(1)}, bf16[4,5,48,384]{3,2,1,0:T(8,128)(2,1)}, u32[]{:S(2)}, u32[]{:S(2)}) collective-permute-start(bf16[4,5,48,384]{3,2,1,0:T(8,128)(2,1)S(1)} %pad_maximum_fusion.refs_5_), channel_id=1, source_target_pairs={{0,64},{4,68},{64,0},{68,4},{1,65},{5,69},{65,1},{69,5},{2,66},{6,... | collective-permute-start | bytes 2211848 | tf_op jit(solution)/shard_map/ppermute | solution.py:373
  54.8 22.9 %collective-permute-start.16 = (bf16[4,5,48,384]{3,2,1,0:T(8,128)(2,1)}, bf16[4,5,48,384]{3,2,1,0:T(8,128)(2,1)}, u32[]{:S(2)}, u32[]{:S(2)}) collective-permute-start(bf16[4,5,48,384]{3,2,1,0:T(8,128)(2,1)} %collective-permute-done.11.refs_7_), channel_id=1, source_target_pairs={{0,8},{8,0},{1,9},{9,1},{2,10},{10,2},{3,11},{11,3},{4,12},{12,4},... | collective-permute-start | bytes 2211848 | tf_op jit(solution)/shard_map/ppermute | solution.py:343
  56.6 21.0 %collective-permute-start.15 = (bf16[4,5,48,384]{3,2,1,0:T(8,128)(2,1)}, bf16[4,5,48,384]{3,2,1,0:T(8,128)(2,1)S(1)}, u32[]{:S(2)}, u32[]{:S(2)}) collective-permute-start(bf16[4,5,48,384]{3,2,1,0:T(8,128)(2,1)} %collective-permute-done.7.refs_6_), channel_id=1, source_target_pairs={{0,8},{8,0},{1,9},{9,1},{2,10},{10,2},{3,11},{11,3},{4,12},{12,4},... | collective-permute-start | bytes 2211848 | tf_op jit(solution)/shard_map/ppermute | solution.py:343
  58.5 19.1 %collective-permute-start.14 = (bf16[144,1536]{1,0:T(8,128)(2,1)}, bf16[144,1536]{1,0:T(8,128)(2,1)S(1)}, u32[]{:S(2)}, u32[]{:S(2)}) collective-permute-start(bf16[144,1536]{1,0:T(8,128)(2,1)} %slice.39), channel_id=1, source_target_pairs={{0,3},{1,0},{2,1},{3,2},{4,7},{5,4},{6,5},{7,6},{8,11},{9,8},{10,9... | collective-permute-start | bytes 1327112 | tf_op jit(solution)/shard_map/ppermute | solution.py:33
  62.9 0.8 copy-start.6
  62.9 14.7 %collective-permute-start.13 = (bf16[128,1536]{1,0:T(8,128)(2,1)}, bf16[128,1536]{1,0:T(8,128)(2,1)}, u32[]{:S(2)}, u32[]{:S(2)}) collective-permute-start(bf16[128,1536]{1,0:T(8,128)(2,1)} %slice.38), channel_id=1, source_target_pairs={{0,1},{1,2},{2,3},{3,0},{4,5},{5,6},{6,7},{7,4},{8,9},{9,10},{10,1... | collective-permute-start | bytes 1179656 | tf_op jit(solution)/shard_map/ppermute | solution.py:32
  77.7 117.5 %reduce-scatter.2.cloned.1.call-start = ((), (), s32[]{:S(2)}) async-start(), calls=%async_computation.4 | async-start | bytes 3538944 | tf_op jit(solution)/shard_map/reduce_scatter | solution.py:391
  77.7 6.2 %collective-permute-start.18 = (bf16[4,5,48,384]{3,2,1,0:T(8,128)(2,1)}, bf16[4,5,48,384]{3,2,1,0:T(8,128)(2,1)}, u32[]{:S(2)}, u32[]{:S(2)}) collective-permute-start(bf16[4,5,48,384]{3,2,1,0:T(8,128)(2,1)} %collective-permute-done.12.refs_8_), channel_id=1, source_target_pairs={{0,8},{8,0},{1,9},{9,1},{2,10},{10,2},{3,11},{11,3},{4,12},{12,4},... | collective-permute-start | bytes 2211848 | tf_op jit(solution)/shard_map/ppermute | solution.py:343
  79.2 41.8 %copy-start.1 = (s32[4]{0:T(128)}, s32[4]{0:T(128)S(1)}, u32[]{:S(2)}) copy-start(s32[4]{0:T(128)S(1)} %pad_add_fusion.pos_ref) | copy-start | bytes 52
  79.2 28.0 %collective-permute-start.29 = (bf16[4,96,768]{2,1,0:T(8,128)(2,1)S(1)}, bf16[4,96,768]{2,1,0:T(8,128)(2,1)S(1)}, u32[]{:S(2)}, u32[]{:S(2)}) collective-permute-start(bf16[4,96,768]{2,1,0:T(8,128)(2,1)S(1)} %all_gather.6.refs_11_), channel_id=1, source_target_pairs={{0,4},{4,64},{64,68},{68,0},{1,5},{5,65},{65,69},{69,1},{2,6},{6,6... | collective-permute-start | bytes 1769480 | tf_op jit(solution)/shard_map/ppermute | solution.py:38
  80.3 27.1 %collective-permute-start.30 = (bf16[4,96,768]{2,1,0:T(8,128)(2,1)S(1)}, bf16[4,96,768]{2,1,0:T(8,128)(2,1)S(1)}, u32[]{:S(2)}, u32[]{:S(2)}) collective-permute-start(bf16[4,96,768]{2,1,0:T(8,128)(2,1)S(1)} %all_gather.6.refs_11_), channel_id=1, source_target_pairs={{0,68},{4,0},{64,4},{68,64},{1,69},{5,1},{65,5},{69,65},{2,70},{6,... | collective-permute-start | bytes 1769480 | tf_op jit(solution)/shard_map/ppermute | solution.py:39
  95.1 24.7 %copy-start.12 = (f32[1536]{0:T(1024)S(1)}, f32[1536]{0:T(1024)}, u32[]{:S(2)}) copy-start(f32[1536]{0:T(1024)} %param.10) | copy-start | bytes 18436
  95.1 9.5 %collective-permute-start.19 = (bf16[512,384]{1,0:T(8,128)(2,1)S(1)}, bf16[512,384]{1,0:T(8,128)(2,1)S(1)}, u32[]{:S(2)}, u32[]{:S(2)}) collective-permute-start(bf16[512,384]{1,0:T(8,128)(2,1)S(1)} %shard_map.95), channel_id=1, source_target_pairs={{0,0},{4,8},{8,4},{12,12},{1,1},{5,9},{9,5},{13,13},{2,2},{6,10},{... | collective-permute-start | bytes 1179656 | tf_op jit(solution)/shard_map/ppermute | solution.py:339
  104.6 8.8 %collective-permute-start.20 = (bf16[512,384]{1,0:T(8,128)(2,1)S(1)}, bf16[512,384]{1,0:T(8,128)(2,1)S(1)}, u32[]{:S(2)}, u32[]{:S(2)}) collective-permute-start(bf16[512,384]{1,0:T(8,128)(2,1)S(1)} %collective-permute-done.19.refs_0_), channel_id=1, source_target_pairs={{0,1},{1,2},{2,3},{3,0},{4,5},{5,6},{6,7},{7,4},{8,9},{9,10},{10,1... | collective-permute-start | bytes 1179656 | tf_op jit(solution)/shard_map/ppermute | solution.py:38
  104.6 9.1 %collective-permute-start.21 = (bf16[512,384]{1,0:T(8,128)(2,1)S(1)}, bf16[512,384]{1,0:T(8,128)(2,1)S(1)}, u32[]{:S(2)}, u32[]{:S(2)}) collective-permute-start(bf16[512,384]{1,0:T(8,128)(2,1)S(1)} %collective-permute-done.19.refs_0_), channel_id=1, source_target_pairs={{0,3},{1,0},{2,1},{3,2},{4,7},{5,4},{6,5},{7,6},{8,11},{9,8},{10,9... | collective-permute-start | bytes 1179656 | tf_op jit(solution)/shard_map/ppermute | solution.py:39
  107.3 9.8 %collective-permute-start.31 = (bf16[2,96,768]{2,1,0:T(8,128)(2,1)S(1)}, bf16[2,96,768]{2,1,0:T(8,128)(2,1)S(1)}, u32[]{:S(2)}, u32[]{:S(2)}) collective-permute-start(bf16[2,96,768]{2,1,0:T(8,128)(2,1)S(1)} %slice.52), channel_id=1, source_target_pairs={{0,4},{4,64},{64,68},{68,0},{1,5},{5,65},{65,69},{69,1},{2,6},{6,6... | collective-permute-start | bytes 884744 | tf_op jit(solution)/shard_map/ppermute | solution.py:32
  107.4 13.6 %copy-start.9 = (bf16[4,96,768]{2,1,0:T(8,128)(2,1)}, bf16[4,96,768]{2,1,0:T(8,128)(2,1)S(1)}, u32[]{:S(2)}) copy-start(bf16[4,96,768]{2,1,0:T(8,128)(2,1)S(1)} %collective-permute-done.30.refs_13_) | copy-start | bytes 1769476
  107.4 9.6 %collective-permute-start.32 = (bf16[2,96,768]{2,1,0:T(8,128)(2,1)S(1)}, bf16[2,96,768]{2,1,0:T(8,128)(2,1)S(1)}, u32[]{:S(2)}, u32[]{:S(2)}) collective-permute-start(bf16[2,96,768]{2,1,0:T(8,128)(2,1)S(1)} %slice.53), channel_id=1, source_target_pairs={{0,68},{4,0},{64,4},{68,64},{1,69},{5,1},{65,5},{69,65},{2,70},{6,... | collective-permute-start | bytes 884744 | tf_op jit(solution)/shard_map/ppermute | solution.py:33
  110.1 9.6 %collective-permute-start.24 = (bf16[512,384]{1,0:T(8,128)(2,1)S(1)}, bf16[512,384]{1,0:T(8,128)(2,1)S(1)}, u32[]{:S(2)}, u32[]{:S(2)}) collective-permute-start(bf16[512,384]{1,0:T(8,128)(2,1)S(1)} %collective-permute-done.19.refs_0_), channel_id=1, source_target_pairs={{0,8},{8,0},{1,9},{9,1},{2,10},{10,2},{3,11},{11,3},{4,12},{12,4},... | collective-permute-start | bytes 1179656 | tf_op jit(solution)/shard_map/ppermute | solution.py:343
  113.4 5.8 %collective-permute-start.22 = (bf16[256,384]{1,0:T(8,128)(2,1)S(1)}, bf16[256,384]{1,0:T(8,128)(2,1)S(1)}, u32[]{:S(2)}, u32[]{:S(2)}) collective-permute-start(bf16[256,384]{1,0:T(8,128)(2,1)S(1)} %slice.50), channel_id=1, source_target_pairs={{0,1},{1,2},{2,3},{3,0},{4,5},{5,6},{6,7},{7,4},{8,9},{9,10},{10,1... | collective-permute-start | bytes 589832 | tf_op jit(solution)/shard_map/ppermute | solution.py:32
  113.7 5.6 %collective-permute-start.23 = (bf16[256,384]{1,0:T(8,128)(2,1)S(1)}, bf16[256,384]{1,0:T(8,128)(2,1)S(1)}, u32[]{:S(2)}, u32[]{:S(2)}) collective-permute-start(bf16[256,384]{1,0:T(8,128)(2,1)S(1)} %slice.51), channel_id=1, source_target_pairs={{0,3},{1,0},{2,1},{3,2},{4,7},{5,4},{6,5},{7,6},{8,11},{9,8},{10,9... | collective-permute-start | bytes 589832 | tf_op jit(solution)/shard_map/ppermute | solution.py:33
  117.0 3.9 %collective-permute-start.25 = (bf16[512,384]{1,0:T(8,128)(2,1)S(1)}, bf16[512,384]{1,0:T(8,128)(2,1)S(1)}, u32[]{:S(2)}, u32[]{:S(2)}) collective-permute-start(bf16[512,384]{1,0:T(8,128)(2,1)S(1)} %collective-permute-done.20.refs_1_), channel_id=1, source_target_pairs={{0,8},{8,0},{1,9},{9,1},{2,10},{10,2},{3,11},{11,3},{4,12},{12,4},... | collective-permute-start | bytes 1179656 | tf_op jit(solution)/shard_map/ppermute | solution.py:343
  117.1 3.9 %collective-permute-start.26 = (bf16[512,384]{1,0:T(8,128)(2,1)S(1)}, bf16[512,384]{1,0:T(8,128)(2,1)S(1)}, u32[]{:S(2)}, u32[]{:S(2)}) collective-permute-start(bf16[512,384]{1,0:T(8,128)(2,1)S(1)} %collective-permute-done.21.refs_2_), channel_id=1, source_target_pairs={{0,8},{8,0},{1,9},{9,1},{2,10},{10,2},{3,11},{11,3},{4,12},{12,4},... | collective-permute-start | bytes 1179656 | tf_op jit(solution)/shard_map/ppermute | solution.py:343
  119.2 1.4 collective-permute-start.27
  119.3 1.7 collective-permute-start.28
  132.5 0.8 copy-start.3
  190.7 9.2 %collective-permute-start.33 = (bf16[96,768]{1,0:T(8,128)(2,1)}, bf16[96,768]{1,0:T(8,128)(2,1)S(1)}, u32[]{:S(2)}, u32[]{:S(2)}) collective-permute-start(bf16[96,768]{1,0:T(8,128)(2,1)} %get-tuple-element.56), channel_id=1, source_target_pairs={{0,0},{4,8},{8,4},{12,12},{1,1},{5,9},{9,5},{13,13},{2,2},{6,10},{... | collective-permute-start | bytes 442376 | tf_op jit(solution)/shard_map/ppermute | solution.py:339
  194.5 5.3 %collective-permute-start.34 = (bf16[96,192]{1,0:T(8,128)(2,1)}, bf16[96,192]{1,0:T(8,128)(2,1)S(1)}, u32[]{:S(2)}, u32[]{:S(2)}) collective-permute-start(bf16[96,192]{1,0:T(8,128)(2,1)} %get-tuple-element.57), channel_id=1, source_target_pairs={{0,64},{4,72},{8,68},{12,76},{64,0},{68,8},{72,4},{76,12},{1,65},{... | collective-permute-start | bytes 110600 | tf_op jit(solution)/shard_map/ppermute | solution.py:395
  200.9 19.1 %all-to-all-start.1 = ((bf16[8,96,576]{2,1,0:T(8,128)(2,1)}), bf16[8,96,576]{2,1,0:T(8,128)(2,1)S(1)}, u32[]{:S(2)}, u32[]{:S(2)}) async-start(bf16[8,96,576]{2,1,0:T(8,128)(2,1)} %broadcast_in_dim.55), calls=%async_computation.2 | async-start | bytes 1966080 | tf_op jit(solution)/shard_map/all_to_all | solution.py:400
  205.0 8.0 %collective-permute-start.36 = (bf16[2,96,192]{2,1,0:T(8,128)(2,1)S(1)}, bf16[2,96,192]{2,1,0:T(8,128)(2,1)S(1)}, u32[]{:S(2)}, u32[]{:S(2)}) collective-permute-start(bf16[2,96,192]{2,1,0:T(8,128)(2,1)S(1)} %get-tuple-element.70), channel_id=1, source_target_pairs={{0,16},{16,32},{32,48},{48,0},{1,17},{17,33},{33,49},{49,1},{2,18}... | collective-permute-start | bytes 221192 | tf_op jit(solution)/shard_map/ppermute | solution.py:399
  205.1 8.0 %collective-permute-start.37 = (bf16[2,96,192]{2,1,0:T(8,128)(2,1)S(1)}, bf16[2,96,192]{2,1,0:T(8,128)(2,1)S(1)}, u32[]{:S(2)}, u32[]{:S(2)}) collective-permute-start(bf16[2,96,192]{2,1,0:T(8,128)(2,1)S(1)} %get-tuple-element.70), channel_id=1, source_target_pairs={{0,32},{16,48},{32,0},{48,16},{1,33},{17,49},{33,1},{49,17},{2,34}... | collective-permute-start | bytes 221192 | tf_op jit(solution)/shard_map/ppermute | solution.py:399
  206.9 6.1 %collective-permute-start.38 = (bf16[2,96,192]{2,1,0:T(8,128)(2,1)S(1)}, bf16[2,96,192]{2,1,0:T(8,128)(2,1)S(1)}, u32[]{:S(2)}, u32[]{:S(2)}) collective-permute-start(bf16[2,96,192]{2,1,0:T(8,128)(2,1)S(1)} %get-tuple-element.70), channel_id=1, source_target_pairs={{0,48},{16,0},{32,16},{48,32},{1,49},{17,1},{33,17},{49,33},{2,50}... | collective-permute-start | bytes 221192 | tf_op jit(solution)/shard_map/ppermute | solution.py:399
  207.8 15.8 %collective-permute-start.35 = (bf16[128,1536]{1,0:T(8,128)(2,1)S(1)}, bf16[128,1536]{1,0:T(8,128)(2,1)S(1)}, u32[]{:S(2)}, u32[]{:S(2)}) collective-permute-start(bf16[128,1536]{1,0:T(8,128)(2,1)S(1)} %add_convert_fusion), channel_id=1, source_target_pairs={{0,0},{4,8},{8,4},{12,12},{1,1},{5,9},{9,5},{13,13},{2,2},{6,10},{... | collective-permute-start | bytes 1179656 | tf_op jit(solution)/shard_map/ppermute | solution.py:339
  213.1 2.6 %copy-start.5 = (bf16[4,2,96,192]{3,2,1,0:T(8,128)(2,1)}, bf16[4,2,96,192]{3,2,1,0:T(8,128)(2,1)S(1)}, u32[]{:S(2)}) copy-start(bf16[4,2,96,192]{3,2,1,0:T(8,128)(2,1)S(1)} %pad_maximum_fusion.2.own_ref) | copy-start | bytes 884740
  213.1 2.6 %collective-permute-start.39 = (bf16[4,2,96,192]{3,2,1,0:T(8,128)(2,1)S(1)}, bf16[4,2,96,192]{3,2,1,0:T(8,128)(2,1)S(1)}, u32[]{:S(2)}, u32[]{:S(2)}) collective-permute-start(bf16[4,2,96,192]{3,2,1,0:T(8,128)(2,1)S(1)} %pad_maximum_fusion.2.own_ref), channel_id=1, source_target_pairs={{0,8},{8,0},{1,9},{9,1},{2,10},{10,2},{3,11},{11,3},{4,12},{12,4},... | collective-permute-start | bytes 884744 | tf_op jit(solution)/shard_map/ppermute | solution.py:401
  215.7 0.8 copy-start.8
  220.0 1.0 copy-start.4
Sparse Core Ops, SparseCore 0:
  77.8 31.2 all-gather.1
  133.5 44.4 reduce-scatter.1

commit v5 on v4

--- a/solution.py
+++ b/solution.py
@@ -217,9 +217,9 @@
     dcat[:, HD : 2 * HD] = dk[...].T.astype(bf16)[:, :HD]
     dcat[:, 2 * HD : 3 * HD] = dv[...].T.astype(bf16)[:, :HD]
 
-    @pl.loop(0, 4)
+    @pl.loop(0, 2)
     def _(n):
-        lanes = pl.ds(pl.multiple_of(n * 384, 384), 384)
+        lanes = pl.ds(pl.multiple_of(n * 768, 768), 768)
         grads[lanes, :] = dot(normed_ref[:, lanes], dcat[...], TN)
         outs[:, lanes] = dot(mixed_ref[...], cot_ref[:, lanes], TN)[:HD]
 

time: 232 us -> 231 us (level)
  no operation moved by 1% of the time
where the time goes in v5:
time: 231 us
  starting transfers between devices  62.3 us (27%)
  blocking collectives  50.1 us (22%)
  Pallas kernels  48.8 us (21%)
  waiting for transfers between devices  38.5 us (17%)
  between operations  14.6 us (6%)
  local copies, waits for them, and re-layouts  13.6 us (6%)
  other arithmetic  2.49 us (1%)
    all_to_all x1, blocking collectives, per_device(): lax.all_to_all(backward(qkv, cot, wo, normed, mixed), ('zh', 'y', 'zl'),...  38.1 us
    pallas_call x1, Pallas kernels, backward(): pl.pallas_call(backward_kernel, out_shape=jax.ShapeDtypeStruct((16, 96, 7...  15.8 us
    ppermute x3, waiting for transfers between devices, per_device(): zpieces = [lax.ppermute(ypieces, zring, ring(4, k)) for k in (1, -1, 2)]  13.5 us
    ppermute x4, starting transfers between devices, swap_axes(): return lax.ppermute(value, ('c', 'zl'), [(0, 0), (1, 2), (2, 1), (3, 3)])  13.2 us
    all_gather x1, blocking collectives, per_device(): head_w = lax.all_gather(later[128:].reshape(96, 768), 'y', axis=0)  12.1 us
    pallas_call x1, Pallas kernels, forward(): pl.pallas_call(forward_kernel, out_shape=(jax.ShapeDtypeStruct((TOKENS, D...  11.5 us
    pallas_call x1, Pallas kernels, conv_pool(): pl.pallas_call(conv_kernel, out_shape=jax.ShapeDtypeStruct((512, OUTC), b...  11.2 us
    ppermute x4, waiting for transfers between devices, swap_axes(): return lax.ppermute(value, ('c', 'zl'), [(0, 0), (1, 2), (2, 1), (3, 3)])  9.3 us
  transfers between devices with their start and end apart: 43, of which 12 were waited for; matrix products, arithmetic and copies ran while one was open for 4% of the time, Pallas kernels for 21%

profile of v5, /device:TPU:1, one launch (start us, length us, event | category | flops | bytes accessed | tf_op | source)
XLA Modules:
  0.0 230.5 jit_solution(4197941960257782789)
XLA Ops:
  7.3 1.1 reshape.354
  8.8 2.1 collective-permute-start
  10.9 2.5 %collective-permute-start.1 = (bf16[5,11,384]{2,1,0:T(8,128)(2,1)S(1)}, bf16[5,11,384]{2,1,0:T(8,128)(2,1)S(1)}, u32[]{:S(2)}, u32[]{:S(2)}) collective-permute-start(bf16[5,11,384]{2,1,0:T(8,128)(2,1)S(1)} %bitcast.66), channel_id=1, source_target_pairs={{0,2},{1,3},{2,0},{3,1},{4,6},{5,7},{6,4},{7,5},{8,10},{9,11},{10,... | collective-permute-start | bytes 126728 | tf_op jit(solution)/shard_map/ppermute | solution.py:360
  13.5 1.2 collective-permute-start.2
  14.7 0.8 select_bitcast_fusion
  15.5 1.7 collective-permute-start.6
  17.5 1.4 collective-permute-start.3
  18.9 2.6 %collective-permute-start.4 = (bf16[5,48,384]{2,1,0:T(8,128)(2,1)S(1)}, bf16[5,48,384]{2,1,0:T(8,128)(2,1)S(1)}, u32[]{:S(2)}, u32[]{:S(2)}) collective-permute-start(bf16[5,48,384]{2,1,0:T(8,128)(2,1)S(1)} %pad.4), channel_id=1, source_target_pairs={{0,32},{16,48},{32,0},{48,16},{1,33},{17,49},{33,1},{49,17},{2,34}... | collective-permute-start | bytes 552968 | tf_op jit(solution)/shard_map/ppermute | solution.py:370
  21.5 1.1 collective-permute-start.5
  22.8 2.6 %shard_map.94.refs_0_ = bf16[272,1536]{1,0:T(8,128)(2,1)S(1)} custom-call(bf16[256,1408]{1,0:T(8,128)(2,1)S(1)} %bitcast.52, bf16[16,1408]{1,0:T(8,128)(2,1)S(1)} %collective-permute-done.6.edge_ref, s32[1,1536]{1,0:T(1,128)S(1)} %compare_select_fusion.10.sources_ref), custom_call_target="tpu_custom_call" | custom-call | flops 1200000000 | bytes 1600000 | tf_op jit(solution)/shard_map/pallas_call | solution.py:328
  25.5 2.6 %collective-permute-done.4 = bf16[5,48,384]{2,1,0:T(8,128)(2,1)S(1)} collective-permute-done((bf16[5,48,384]{2,1,0:T(8,128)(2,1)S(1)}, bf16[5,48,384]{2,1,0:T(8,128)(2,1)S(1)}, u32[]{:S(2)}, u32[]{:S(2)}) %collective-permute-start.4) | collective-permute-done | bytes 184352 | tf_op jit(solution)/shard_map/ppermute | solution.py:370
  28.2 3.1 %collective-permute-start.10 = (bf16[4,5,48,384]{3,2,1,0:T(8,128)(2,1)S(1)}, bf16[4,5,48,384]{3,2,1,0:T(8,128)(2,1)S(1)}, u32[]{:S(2)}, u32[]{:S(2)}) collective-permute-start(bf16[4,5,48,384]{3,2,1,0:T(8,128)(2,1)S(1)} %pad_maximum_fusion.refs_5_), channel_id=1, source_target_pairs={{0,8},{8,0},{1,9},{9,1},{2,10},{10,2},{3,11},{11,3},{4,12},{12,4},... | collective-permute-start | bytes 2211848 | tf_op jit(solution)/shard_map/ppermute | solution.py:375
  31.6 2.4 %collective-permute-start.9 = (bf16[272,1536]{1,0:T(8,128)(2,1)S(1)}, bf16[272,1536]{1,0:T(8,128)(2,1)}, u32[]{:S(2)}, u32[]{:S(2)}) collective-permute-start(bf16[272,1536]{1,0:T(8,128)(2,1)S(1)} %shard_map.94.refs_0_), channel_id=1, source_target_pairs={{0,3},{1,0},{2,1},{3,2},{4,7},{5,4},{6,5},{7,6},{8,11},{9,8},{10,9... | collective-permute-start | bytes 2506760 | tf_op jit(solution)/shard_map/ppermute | solution.py:374
  33.9 1.3 collective-permute-start.7
  35.2 2.1 collective-permute-start.11
  37.8 2.3 %collective-permute-start.17 = (bf16[176,1536]{1,0:T(8,128)(2,1)S(1)}, bf16[176,1536]{1,0:T(8,128)(2,1)S(1)}, u32[]{:S(2)}, u32[]{:S(2)}) collective-permute-start(bf16[176,1536]{1,0:T(8,128)(2,1)S(1)} %pad_maximum_fusion.1), channel_id=1, source_target_pairs={{0,0},{4,8},{8,4},{12,12},{1,1},{5,9},{9,5},{13,13},{2,2},{6,10},{... | collective-permute-start | bytes 1622024 | tf_op jit(solution)/shard_map/ppermute | solution.py:339
  40.2 13.5 %collective-permute-done.7.refs_6_ = bf16[4,5,48,384]{3,2,1,0:T(8,128)(2,1)} collective-permute-done((bf16[4,5,48,384]{3,2,1,0:T(8,128)(2,1)S(1)}, bf16[4,5,48,384]{3,2,1,0:T(8,128)(2,1)}, u32[]{:S(2)}, u32[]{:S(2)}) %collective-permute-start.7) | collective-permute-done | bytes 737312 | tf_op jit(solution)/shard_map/ppermute | solution.py:373
  53.7 1.1 collective-permute-start.12
  54.8 1.8 collective-permute-start.16
  56.7 1.8 slice.39
  58.5 0.9 collective-permute-start.14
  59.4 1.8 slice.38
  61.2 1.7 collective-permute-done.17
  62.9 0.8 copy-done.6
  63.8 1.8 slice.49
  65.6 12.1 %all_gather.6.refs_11_ = bf16[4,96,768]{2,1,0:T(8,128)(2,1)S(1)} all-gather(bf16[1,96,768]{2,1,0:T(8,128)(2,1)S(1)} %all_gather_reshape.3), channel_id=1, replica_groups=mesh['zh'=2,'y'=4,'c'=2,'zl'=2,'x'=4] {'y'}, dimensions={0}, use_global_device_ids=true | all-gather | bytes 737280 | tf_op jit(solution)/shard_map/all_gather | solution.py:368
  77.7 0.6 collective-permute-start.18
  78.4 0.8 dynamic_slice.20
  79.2 1.0 collective-permute-start.29
  80.3 3.6 %collective-permute-start.30 = (bf16[4,96,768]{2,1,0:T(8,128)(2,1)S(1)}, bf16[4,96,768]{2,1,0:T(8,128)(2,1)S(1)}, u32[]{:S(2)}, u32[]{:S(2)}) collective-permute-start(bf16[4,96,768]{2,1,0:T(8,128)(2,1)S(1)} %all_gather.6.refs_11_), channel_id=1, source_target_pairs={{0,68},{4,0},{64,4},{68,64},{1,69},{5,1},{65,5},{69,65},{2,70},{6,... | collective-permute-start | bytes 1769480 | tf_op jit(solution)/shard_map/ppermute | solution.py:39
  83.9 11.2 %shard_map.95 = bf16[512,384]{1,0:T(8,128)(2,1)S(1)} custom-call(s32[4]{0:T(128)S(1)} %pad_add_fusion.pos_ref, bf16[272,1536]{1,0:T(8,128)(2,1)} %copy-done.2, bf16[272,1536]{1,0:T(8,128)(2,1)} %collective-permute-done.8.refs_1_, bf16[272,1536]{1,0:T(8,128)(2,1)} %collective-permute-done.9.refs_2_, bf16[128,1536]{1,0:T(8,128)(2,1)} %collective-permute-done.13.refs_3_, ...), custom_call_target="tpu_custom_call" | custom-call | flops 6000000000 | bytes 9000000 | tf_op jit(solution)/shard_map/pallas_call | solution.py:94
  95.1 1.9 collective-permute-start.19
  97.0 7.6 %collective-permute-done.19.refs_0_ = bf16[512,384]{1,0:T(8,128)(2,1)S(1)} collective-permute-done((bf16[512,384]{1,0:T(8,128)(2,1)S(1)}, bf16[512,384]{1,0:T(8,128)(2,1)S(1)}, u32[]{:S(2)}, u32[]{:S(2)}) %collective-permute-start.19) | collective-permute-done | bytes 393248 | tf_op jit(solution)/shard_map/ppermute | solution.py:339
  104.6 2.7 %collective-permute-start.21 = (bf16[512,384]{1,0:T(8,128)(2,1)S(1)}, bf16[512,384]{1,0:T(8,128)(2,1)S(1)}, u32[]{:S(2)}, u32[]{:S(2)}) collective-permute-start(bf16[512,384]{1,0:T(8,128)(2,1)S(1)} %collective-permute-done.19.refs_0_), channel_id=1, source_target_pairs={{0,3},{1,0},{2,1},{3,2},{4,7},{5,4},{6,5},{7,6},{8,11},{9,8},{10,9... | collective-permute-start | bytes 1179656 | tf_op jit(solution)/shard_map/ppermute | solution.py:39
  107.4 2.7 %collective-permute-start.32 = (bf16[2,96,768]{2,1,0:T(8,128)(2,1)S(1)}, bf16[2,96,768]{2,1,0:T(8,128)(2,1)S(1)}, u32[]{:S(2)}, u32[]{:S(2)}) collective-permute-start(bf16[2,96,768]{2,1,0:T(8,128)(2,1)S(1)} %slice.53), channel_id=1, source_target_pairs={{0,68},{4,0},{64,4},{68,64},{1,69},{5,1},{65,5},{69,65},{2,70},{6,... | collective-permute-start | bytes 884744 | tf_op jit(solution)/shard_map/ppermute | solution.py:33
  110.1 3.3 %collective-permute-done.20.refs_1_ = bf16[512,384]{1,0:T(8,128)(2,1)S(1)} collective-permute-done((bf16[512,384]{1,0:T(8,128)(2,1)S(1)}, bf16[512,384]{1,0:T(8,128)(2,1)S(1)}, u32[]{:S(2)}, u32[]{:S(2)}) %collective-permute-start.20) | collective-permute-done | bytes 393248 | tf_op jit(solution)/shard_map/ppermute | solution.py:38
  113.7 2.6 %collective-permute-start.23 = (bf16[256,384]{1,0:T(8,128)(2,1)S(1)}, bf16[256,384]{1,0:T(8,128)(2,1)S(1)}, u32[]{:S(2)}, u32[]{:S(2)}) collective-permute-start(bf16[256,384]{1,0:T(8,128)(2,1)S(1)} %slice.51), channel_id=1, source_target_pairs={{0,3},{1,0},{2,1},{3,2},{4,7},{5,4},{6,5},{7,6},{8,11},{9,8},{10,9... | collective-permute-start | bytes 589832 | tf_op jit(solution)/shard_map/ppermute | solution.py:33
  116.3 0.8 collective-permute-done.31.refs_14_
  117.1 0.5 collective-permute-start.26
  117.6 1.7 collective-permute-done.22.refs_3_
  119.3 0.5 collective-permute-start.28
  119.8 0.9 collective-permute-done.27.refs_8_
  121.0 11.5 %shard_map.96 = (bf16[1024,1536]{1,0:T(8,128)(2,1)}, bf16[3,1024,256]{2,1,0:T(8,128)(2,1)}, bf16[1024,256]{1,0:T(8,128)(2,1)S(1)}, bf16[1024,1536]{1,0:T(8,128)(...) custom-call(s32[4]{0:T(128)S(1)} %pad_add_fusion.pos_ref, ...), custom_call_target="tpu_custom_call" | custom-call | flops 4000000000 | bytes 16000000 | tf_op jit(solution)/shard_map/pallas_call | solution.py:173
  132.5 0.8 copy-done.3
  133.4 15.8 %shard_map.97 = bf16[16,96,768]{2,1,0:T(8,128)(2,1)} custom-call(bf16[3,1024,256]{2,1,0:T(8,128)(2,1)} %get-tuple-element.51.qkv_ref, bf16[1024,1536]{1,0:T(8,128)(2,1)} %all-gather.2.cloned.1.call-done.cot_ref, bf16[1536,256]{1,0:T(8,128)(2,1)} %get-tuple-element.53.wo, bf16[1024,1536]{1,0:T(8,128)(2,1)} %get-tuple-element.54.normed_ref, ...), custom_call_target="tpu_custom_call" | custom-call | flops 6000000000 | bytes 18000000 | tf_op jit(solution)/shard_map/pallas_call | solution.py:234
  149.2 38.1 %all_to_all.10.parts_ref = bf16[16,96,768]{2,1,0:T(8,128)(2,1)} all-to-all(bf16[16,96,768]{2,1,0:T(8,128)(2,1)} %shard_map.97), channel_id=1, replica_groups=mesh['zh'=2,'y'=4,'c'=2,'zl'=2,'x'=4] {'zh','y','zl'}, dimensions={0} | all-to-all | bytes 4718592 | tf_op jit(solution)/shard_map/all_to_all | solution.py:393
  187.3 2.7 %shard_map.98 = (bf16[96,768]{1,0:T(8,128)(2,1)}, bf16[96,192]{1,0:T(8,128)(2,1)}) custom-call(bf16[16,96,768]{2,1,0:T(8,128)(2,1)} %all_to_all.10.parts_ref), custom_call_target="tpu_custom_call" | custom-call | tf_op jit(solution)/shard_map/pallas_call | solution.py:260
  190.0 3.8 %collective-permute-start.33 = (bf16[96,768]{1,0:T(8,128)(2,1)}, bf16[96,768]{1,0:T(8,128)(2,1)S(1)}, u32[]{:S(2)}, u32[]{:S(2)}) collective-permute-start(bf16[96,768]{1,0:T(8,128)(2,1)} %get-tuple-element.56), channel_id=1, source_target_pairs={{0,0},{4,8},{8,4},{12,12},{1,1},{5,9},{9,5},{13,13},{2,2},{6,10},{... | collective-permute-start | bytes 442376 | tf_op jit(solution)/shard_map/ppermute | solution.py:339
  193.8 0.7 collective-permute-start.34
  194.5 1.1 add_convert_fusion
  195.6 3.6 %collective-permute-done.34 = bf16[96,192]{1,0:T(8,128)(2,1)S(1)} collective-permute-done((bf16[96,192]{1,0:T(8,128)(2,1)}, bf16[96,192]{1,0:T(8,128)(2,1)S(1)}, u32[]{:S(2)}, u32[]{:S(2)}) %collective-permute-start.34) | collective-permute-done | bytes 36896 | tf_op jit(solution)/shard_map/ppermute | solution.py:395
  199.2 1.0 broadcast_in_dim.55
  200.2 3.9 %all-to-all-start.1 = ((bf16[8,96,576]{2,1,0:T(8,128)(2,1)}), bf16[8,96,576]{2,1,0:T(8,128)(2,1)S(1)}, u32[]{:S(2)}, u32[]{:S(2)}) async-start(bf16[8,96,576]{2,1,0:T(8,128)(2,1)} %broadcast_in_dim.55), calls=%async_computation.2 | async-start | bytes 1966080 | tf_op jit(solution)/shard_map/all_to_all | solution.py:400
  204.4 1.9 collective-permute-start.37
  206.2 0.9 collective-permute-start.38
  207.1 5.1 %collective-permute-start.35 = (bf16[128,1536]{1,0:T(8,128)(2,1)S(1)}, bf16[128,1536]{1,0:T(8,128)(2,1)S(1)}, u32[]{:S(2)}, u32[]{:S(2)}) collective-permute-start(bf16[128,1536]{1,0:T(8,128)(2,1)S(1)} %add_convert_fusion), channel_id=1, source_target_pairs={{0,0},{4,8},{8,4},{12,12},{1,1},{5,9},{9,5},{13,13},{2,2},{6,10},{... | collective-permute-start | bytes 1179656 | tf_op jit(solution)/shard_map/ppermute | solution.py:339
  212.4 1.2 collective-permute-start.39
  213.7 1.3 collective-permute-done.39.other_ref
  215.0 0.7 copy-done.8
  215.8 2.3 %shard_map.100 = f32[192,1536]{1,0:T(8,128)} custom-call(s32[4]{0:T(128)} %copy-done.1, bf16[4,2,96,192]{3,2,1,0:T(8,128)(2,1)} %copy-done.5, bf16[4,2,96,192]{3,2,1,0:T(8,128)(2,1)} %copy-done.8), custom_call_target="tpu_custom_call" | custom-call | tf_op jit(solution)/shard_map/pallas_call | solution.py:296
  218.1 1.2 all-to-all-done.1.heads_ref
  219.3 1.0 copy-done.4
  220.3 2.6 %shard_map.99 = f32[3,96,1536]{2,1,0:T(8,128)} custom-call(bf16[8,96,576]{2,1,0:T(8,128)(2,1)} %copy-done.4), custom_call_target="tpu_custom_call" | custom-call | tf_op jit(solution)/shard_map/pallas_call | solution.py:275
  222.9 0.7 copy.45
  (99 shorter events, 3.1 us)
Async XLA Ops:
  7.2 15.6 %copy-start = (bf16[1,256,1408]{2,1,0:T(8,128)(2,1)S(1)}, bf16[1,256,1408]{2,1,0:T(8,128)(2,1)}, u32[]{:S(2)}) copy-start(bf16[1,256,1408]{2,1,0:T(8,128)(2,1)} %param.7) | copy-start | bytes 2162692
  7.2 126.2 %all-gather.2.cloned.1.call-start = ((), (), s32[]{:S(2)}) async-start(), calls=%async_computation.3 | async-start | bytes 3538944 | tf_op jit(solution)/shard_map/all_gather | solution.py:380
  8.8 8.5 %collective-permute-start = (bf16[5,11,384]{2,1,0:T(8,128)(2,1)S(1)}, bf16[5,11,384]{2,1,0:T(8,128)(2,1)S(1)}, u32[]{:S(2)}, u32[]{:S(2)}) collective-permute-start(bf16[5,11,384]{2,1,0:T(8,128)(2,1)S(1)} %bitcast.67), channel_id=1, source_target_pairs={{0,1},{1,2},{2,3},{3,0},{4,5},{5,6},{6,7},{7,4},{8,9},{9,10},{10,1... | collective-permute-start | bytes 126728 | tf_op jit(solution)/shard_map/ppermute | solution.py:360
  10.9 6.4 %collective-permute-start.1 = (bf16[5,11,384]{2,1,0:T(8,128)(2,1)S(1)}, bf16[5,11,384]{2,1,0:T(8,128)(2,1)S(1)}, u32[]{:S(2)}, u32[]{:S(2)}) collective-permute-start(bf16[5,11,384]{2,1,0:T(8,128)(2,1)S(1)} %bitcast.66), channel_id=1, source_target_pairs={{0,2},{1,3},{2,0},{3,1},{4,6},{5,7},{6,4},{7,5},{8,10},{9,11},{10,... | collective-permute-start | bytes 126728 | tf_op jit(solution)/shard_map/ppermute | solution.py:360
  13.5 3.9 %collective-permute-start.2 = (bf16[5,11,384]{2,1,0:T(8,128)(2,1)S(1)}, bf16[5,11,384]{2,1,0:T(8,128)(2,1)S(1)}, u32[]{:S(2)}, u32[]{:S(2)}) collective-permute-start(bf16[5,11,384]{2,1,0:T(8,128)(2,1)S(1)} %bitcast.65), channel_id=1, source_target_pairs={{0,3},{1,0},{2,1},{3,2},{4,7},{5,4},{6,5},{7,6},{8,11},{9,8},{10,9... | collective-permute-start | bytes 126728 | tf_op jit(solution)/shard_map/ppermute | solution.py:360
  15.5 7.3 %collective-permute-start.6 = (bf16[16,1408]{1,0:T(8,128)(2,1)S(1)}, bf16[16,1408]{1,0:T(8,128)(2,1)S(1)}, u32[]{:S(2)}, u32[]{:S(2)}) collective-permute-start(bf16[16,1408]{1,0:T(8,128)(2,1)S(1)} %select_bitcast_fusion), channel_id=1, source_target_pairs={{0,4},{4,0},{1,5},{5,1},{2,6},{6,2},{3,7},{7,3},{8,12},{12,8},{9,1... | collective-permute-start | bytes 135176 | tf_op jit(solution)/shard_map/ppermute | solution.py:352
  17.5 7.9 %collective-permute-start.3 = (bf16[5,48,384]{2,1,0:T(8,128)(2,1)S(1)}, bf16[5,48,384]{2,1,0:T(8,128)(2,1)S(1)}, u32[]{:S(2)}, u32[]{:S(2)}) collective-permute-start(bf16[5,48,384]{2,1,0:T(8,128)(2,1)S(1)} %pad.4), channel_id=1, source_target_pairs={{0,16},{16,32},{32,48},{48,0},{1,17},{17,33},{33,49},{49,1},{2,18}... | collective-permute-start | bytes 552968 | tf_op jit(solution)/shard_map/ppermute | solution.py:370
  18.9 9.1 %collective-permute-start.4 = (bf16[5,48,384]{2,1,0:T(8,128)(2,1)S(1)}, bf16[5,48,384]{2,1,0:T(8,128)(2,1)S(1)}, u32[]{:S(2)}, u32[]{:S(2)}) collective-permute-start(bf16[5,48,384]{2,1,0:T(8,128)(2,1)S(1)} %pad.4), channel_id=1, source_target_pairs={{0,32},{16,48},{32,0},{48,16},{1,33},{17,49},{33,1},{49,17},{2,34}... | collective-permute-start | bytes 552968 | tf_op jit(solution)/shard_map/ppermute | solution.py:370
  21.5 6.5 %collective-permute-start.5 = (bf16[5,48,384]{2,1,0:T(8,128)(2,1)S(1)}, bf16[5,48,384]{2,1,0:T(8,128)(2,1)S(1)}, u32[]{:S(2)}, u32[]{:S(2)}) collective-permute-start(bf16[5,48,384]{2,1,0:T(8,128)(2,1)S(1)} %pad.4), channel_id=1, source_target_pairs={{0,48},{16,0},{32,16},{48,32},{1,49},{17,1},{33,17},{49,33},{2,50}... | collective-permute-start | bytes 552968 | tf_op jit(solution)/shard_map/ppermute | solution.py:370
  22.8 14.5 %copy-start.10 = (bf16[96,3,192]{2,0,1:T(8,128)(2,1)S(1)}, bf16[96,3,192]{2,0,1:T(8,128)(2,1)}, u32[]{:S(2)}) copy-start(bf16[96,3,192]{2,0,1:T(8,128)(2,1)} %param.11) | copy-start | bytes 331780
  25.4 12.4 %copy-start.2 = (bf16[272,1536]{1,0:T(8,128)(2,1)}, bf16[272,1536]{1,0:T(8,128)(2,1)S(1)}, u32[]{:S(2)}) copy-start(bf16[272,1536]{1,0:T(8,128)(2,1)S(1)} %shard_map.94.refs_0_) | copy-start | bytes 2506756
  25.4 12.1 %copy-start.11 = (bf16[192,96]{1,0:T(8,128)(2,1)S(1)}, bf16[192,96]{1,0:T(8,128)(2,1)}, u32[]{:S(2)}) copy-start(bf16[192,96]{1,0:T(8,128)(2,1)} %param.12) | copy-start | bytes 110596
  25.4 12.3 %copy-start.7 = (bf16[1,128,1536]{2,1,0:T(8,128)(2,1)S(1)}, bf16[1,128,1536]{2,1,0:T(8,128)(2,1)}, u32[]{:S(2)}) copy-start(bf16[1,128,1536]{2,1,0:T(8,128)(2,1)} %param.13) | copy-start | bytes 1179652
  28.2 9.7 %collective-permute-start.10 = (bf16[4,5,48,384]{3,2,1,0:T(8,128)(2,1)S(1)}, bf16[4,5,48,384]{3,2,1,0:T(8,128)(2,1)S(1)}, u32[]{:S(2)}, u32[]{:S(2)}) collective-permute-start(bf16[4,5,48,384]{3,2,1,0:T(8,128)(2,1)S(1)} %pad_maximum_fusion.refs_5_), channel_id=1, source_target_pairs={{0,8},{8,0},{1,9},{9,1},{2,10},{10,2},{3,11},{11,3},{4,12},{12,4},... | collective-permute-start | bytes 2211848 | tf_op jit(solution)/shard_map/ppermute | solution.py:375
  31.3 25.4 %collective-permute-start.8 = (bf16[272,1536]{1,0:T(8,128)(2,1)S(1)}, bf16[272,1536]{1,0:T(8,128)(2,1)}, u32[]{:S(2)}, u32[]{:S(2)}) collective-permute-start(bf16[272,1536]{1,0:T(8,128)(2,1)S(1)} %shard_map.94.refs_0_), channel_id=1, source_target_pairs={{0,1},{1,2},{2,3},{3,0},{4,5},{5,6},{6,7},{7,4},{8,9},{9,10},{10,1... | collective-permute-start | bytes 2506760 | tf_op jit(solution)/shard_map/ppermute | solution.py:374
  31.6 25.0 %collective-permute-start.9 = (bf16[272,1536]{1,0:T(8,128)(2,1)S(1)}, bf16[272,1536]{1,0:T(8,128)(2,1)}, u32[]{:S(2)}, u32[]{:S(2)}) collective-permute-start(bf16[272,1536]{1,0:T(8,128)(2,1)S(1)} %shard_map.94.refs_0_), channel_id=1, source_target_pairs={{0,3},{1,0},{2,1},{3,2},{4,7},{5,4},{6,5},{7,6},{8,11},{9,8},{10,9... | collective-permute-start | bytes 2506760 | tf_op jit(solution)/shard_map/ppermute | solution.py:374
  33.9 19.8 %collective-permute-start.7 = (bf16[4,5,48,384]{3,2,1,0:T(8,128)(2,1)S(1)}, bf16[4,5,48,384]{3,2,1,0:T(8,128)(2,1)}, u32[]{:S(2)}, u32[]{:S(2)}) collective-permute-start(bf16[4,5,48,384]{3,2,1,0:T(8,128)(2,1)S(1)} %pad_maximum_fusion.refs_5_), channel_id=1, source_target_pairs={{0,4},{4,64},{64,68},{68,0},{1,5},{5,65},{65,69},{69,1},{2,6},{6,6... | collective-permute-start | bytes 2211848 | tf_op jit(solution)/shard_map/ppermute | solution.py:373
  35.2 19.5 %collective-permute-start.11 = (bf16[4,5,48,384]{3,2,1,0:T(8,128)(2,1)S(1)}, bf16[4,5,48,384]{3,2,1,0:T(8,128)(2,1)}, u32[]{:S(2)}, u32[]{:S(2)}) collective-permute-start(bf16[4,5,48,384]{3,2,1,0:T(8,128)(2,1)S(1)} %pad_maximum_fusion.refs_5_), channel_id=1, source_target_pairs={{0,68},{4,0},{64,4},{68,64},{1,69},{5,1},{65,5},{69,65},{2,70},{6,... | collective-permute-start | bytes 2211848 | tf_op jit(solution)/shard_map/ppermute | solution.py:373
  37.8 25.1 %collective-permute-start.17 = (bf16[176,1536]{1,0:T(8,128)(2,1)S(1)}, bf16[176,1536]{1,0:T(8,128)(2,1)S(1)}, u32[]{:S(2)}, u32[]{:S(2)}) collective-permute-start(bf16[176,1536]{1,0:T(8,128)(2,1)S(1)} %pad_maximum_fusion.1), channel_id=1, source_target_pairs={{0,0},{4,8},{8,4},{12,12},{1,1},{5,9},{9,5},{13,13},{2,2},{6,10},{... | collective-permute-start | bytes 1622024 | tf_op jit(solution)/shard_map/ppermute | solution.py:339
  53.7 23.9 %collective-permute-start.12 = (bf16[4,5,48,384]{3,2,1,0:T(8,128)(2,1)S(1)}, bf16[4,5,48,384]{3,2,1,0:T(8,128)(2,1)}, u32[]{:S(2)}, u32[]{:S(2)}) collective-permute-start(bf16[4,5,48,384]{3,2,1,0:T(8,128)(2,1)S(1)} %pad_maximum_fusion.refs_5_), channel_id=1, source_target_pairs={{0,64},{4,68},{64,0},{68,4},{1,65},{5,69},{65,1},{69,5},{2,66},{6,... | collective-permute-start | bytes 2211848 | tf_op jit(solution)/shard_map/ppermute | solution.py:373
  54.8 22.9 %collective-permute-start.16 = (bf16[4,5,48,384]{3,2,1,0:T(8,128)(2,1)}, bf16[4,5,48,384]{3,2,1,0:T(8,128)(2,1)}, u32[]{:S(2)}, u32[]{:S(2)}) collective-permute-start(bf16[4,5,48,384]{3,2,1,0:T(8,128)(2,1)} %collective-permute-done.11.refs_7_), channel_id=1, source_target_pairs={{0,8},{8,0},{1,9},{9,1},{2,10},{10,2},{3,11},{11,3},{4,12},{12,4},... | collective-permute-start | bytes 2211848 | tf_op jit(solution)/shard_map/ppermute | solution.py:343
  56.6 21.0 %collective-permute-start.15 = (bf16[4,5,48,384]{3,2,1,0:T(8,128)(2,1)}, bf16[4,5,48,384]{3,2,1,0:T(8,128)(2,1)S(1)}, u32[]{:S(2)}, u32[]{:S(2)}) collective-permute-start(bf16[4,5,48,384]{3,2,1,0:T(8,128)(2,1)} %collective-permute-done.7.refs_6_), channel_id=1, source_target_pairs={{0,8},{8,0},{1,9},{9,1},{2,10},{10,2},{3,11},{11,3},{4,12},{12,4},... | collective-permute-start | bytes 2211848 | tf_op jit(solution)/shard_map/ppermute | solution.py:343
  58.5 19.1 %collective-permute-start.14 = (bf16[144,1536]{1,0:T(8,128)(2,1)}, bf16[144,1536]{1,0:T(8,128)(2,1)S(1)}, u32[]{:S(2)}, u32[]{:S(2)}) collective-permute-start(bf16[144,1536]{1,0:T(8,128)(2,1)} %slice.39), channel_id=1, source_target_pairs={{0,3},{1,0},{2,1},{3,2},{4,7},{5,4},{6,5},{7,6},{8,11},{9,8},{10,9... | collective-permute-start | bytes 1327112 | tf_op jit(solution)/shard_map/ppermute | solution.py:33
  62.9 0.8 copy-start.6
  62.9 14.7 %collective-permute-start.13 = (bf16[128,1536]{1,0:T(8,128)(2,1)}, bf16[128,1536]{1,0:T(8,128)(2,1)}, u32[]{:S(2)}, u32[]{:S(2)}) collective-permute-start(bf16[128,1536]{1,0:T(8,128)(2,1)} %slice.38), channel_id=1, source_target_pairs={{0,1},{1,2},{2,3},{3,0},{4,5},{5,6},{6,7},{7,4},{8,9},{9,10},{10,1... | collective-permute-start | bytes 1179656 | tf_op jit(solution)/shard_map/ppermute | solution.py:32
  77.7 116.8 %reduce-scatter.2.cloned.1.call-start = ((), (), s32[]{:S(2)}) async-start(), calls=%async_computation.4 | async-start | bytes 3538944 | tf_op jit(solution)/shard_map/reduce_scatter | solution.py:391
  77.7 6.2 %collective-permute-start.18 = (bf16[4,5,48,384]{3,2,1,0:T(8,128)(2,1)}, bf16[4,5,48,384]{3,2,1,0:T(8,128)(2,1)}, u32[]{:S(2)}, u32[]{:S(2)}) collective-permute-start(bf16[4,5,48,384]{3,2,1,0:T(8,128)(2,1)} %collective-permute-done.12.refs_8_), channel_id=1, source_target_pairs={{0,8},{8,0},{1,9},{9,1},{2,10},{10,2},{3,11},{11,3},{4,12},{12,4},... | collective-permute-start | bytes 2211848 | tf_op jit(solution)/shard_map/ppermute | solution.py:343
  79.2 41.8 %copy-start.1 = (s32[4]{0:T(128)}, s32[4]{0:T(128)S(1)}, u32[]{:S(2)}) copy-start(s32[4]{0:T(128)S(1)} %pad_add_fusion.pos_ref) | copy-start | bytes 52
  79.2 28.0 %collective-permute-start.29 = (bf16[4,96,768]{2,1,0:T(8,128)(2,1)S(1)}, bf16[4,96,768]{2,1,0:T(8,128)(2,1)S(1)}, u32[]{:S(2)}, u32[]{:S(2)}) collective-permute-start(bf16[4,96,768]{2,1,0:T(8,128)(2,1)S(1)} %all_gather.6.refs_11_), channel_id=1, source_target_pairs={{0,4},{4,64},{64,68},{68,0},{1,5},{5,65},{65,69},{69,1},{2,6},{6,6... | collective-permute-start | bytes 1769480 | tf_op jit(solution)/shard_map/ppermute | solution.py:38
  80.3 27.1 %collective-permute-start.30 = (bf16[4,96,768]{2,1,0:T(8,128)(2,1)S(1)}, bf16[4,96,768]{2,1,0:T(8,128)(2,1)S(1)}, u32[]{:S(2)}, u32[]{:S(2)}) collective-permute-start(bf16[4,96,768]{2,1,0:T(8,128)(2,1)S(1)} %all_gather.6.refs_11_), channel_id=1, source_target_pairs={{0,68},{4,0},{64,4},{68,64},{1,69},{5,1},{65,5},{69,65},{2,70},{6,... | collective-permute-start | bytes 1769480 | tf_op jit(solution)/shard_map/ppermute | solution.py:39
  95.1 24.7 %copy-start.12 = (f32[1536]{0:T(1024)S(1)}, f32[1536]{0:T(1024)}, u32[]{:S(2)}) copy-start(f32[1536]{0:T(1024)} %param.10) | copy-start | bytes 18436
  95.1 9.5 %collective-permute-start.19 = (bf16[512,384]{1,0:T(8,128)(2,1)S(1)}, bf16[512,384]{1,0:T(8,128)(2,1)S(1)}, u32[]{:S(2)}, u32[]{:S(2)}) collective-permute-start(bf16[512,384]{1,0:T(8,128)(2,1)S(1)} %shard_map.95), channel_id=1, source_target_pairs={{0,0},{4,8},{8,4},{12,12},{1,1},{5,9},{9,5},{13,13},{2,2},{6,10},{... | collective-permute-start | bytes 1179656 | tf_op jit(solution)/shard_map/ppermute | solution.py:339
  104.6 8.8 %collective-permute-start.20 = (bf16[512,384]{1,0:T(8,128)(2,1)S(1)}, bf16[512,384]{1,0:T(8,128)(2,1)S(1)}, u32[]{:S(2)}, u32[]{:S(2)}) collective-permute-start(bf16[512,384]{1,0:T(8,128)(2,1)S(1)} %collective-permute-done.19.refs_0_), channel_id=1, source_target_pairs={{0,1},{1,2},{2,3},{3,0},{4,5},{5,6},{6,7},{7,4},{8,9},{9,10},{10,1... | collective-permute-start | bytes 1179656 | tf_op jit(solution)/shard_map/ppermute | solution.py:38
  104.6 9.1 %collective-permute-start.21 = (bf16[512,384]{1,0:T(8,128)(2,1)S(1)}, bf16[512,384]{1,0:T(8,128)(2,1)S(1)}, u32[]{:S(2)}, u32[]{:S(2)}) collective-permute-start(bf16[512,384]{1,0:T(8,128)(2,1)S(1)} %collective-permute-done.19.refs_0_), channel_id=1, source_target_pairs={{0,3},{1,0},{2,1},{3,2},{4,7},{5,4},{6,5},{7,6},{8,11},{9,8},{10,9... | collective-permute-start | bytes 1179656 | tf_op jit(solution)/shard_map/ppermute | solution.py:39
  107.3 9.8 %collective-permute-start.31 = (bf16[2,96,768]{2,1,0:T(8,128)(2,1)S(1)}, bf16[2,96,768]{2,1,0:T(8,128)(2,1)S(1)}, u32[]{:S(2)}, u32[]{:S(2)}) collective-permute-start(bf16[2,96,768]{2,1,0:T(8,128)(2,1)S(1)} %slice.52), channel_id=1, source_target_pairs={{0,4},{4,64},{64,68},{68,0},{1,5},{5,65},{65,69},{69,1},{2,6},{6,6... | collective-permute-start | bytes 884744 | tf_op jit(solution)/shard_map/ppermute | solution.py:32
  107.4 13.6 %copy-start.9 = (bf16[4,96,768]{2,1,0:T(8,128)(2,1)}, bf16[4,96,768]{2,1,0:T(8,128)(2,1)S(1)}, u32[]{:S(2)}) copy-start(bf16[4,96,768]{2,1,0:T(8,128)(2,1)S(1)} %collective-permute-done.30.refs_13_) | copy-start | bytes 1769476
  107.4 9.6 %collective-permute-start.32 = (bf16[2,96,768]{2,1,0:T(8,128)(2,1)S(1)}, bf16[2,96,768]{2,1,0:T(8,128)(2,1)S(1)}, u32[]{:S(2)}, u32[]{:S(2)}) collective-permute-start(bf16[2,96,768]{2,1,0:T(8,128)(2,1)S(1)} %slice.53), channel_id=1, source_target_pairs={{0,68},{4,0},{64,4},{68,64},{1,69},{5,1},{65,5},{69,65},{2,70},{6,... | collective-permute-start | bytes 884744 | tf_op jit(solution)/shard_map/ppermute | solution.py:33
  110.1 9.6 %collective-permute-start.24 = (bf16[512,384]{1,0:T(8,128)(2,1)S(1)}, bf16[512,384]{1,0:T(8,128)(2,1)S(1)}, u32[]{:S(2)}, u32[]{:S(2)}) collective-permute-start(bf16[512,384]{1,0:T(8,128)(2,1)S(1)} %collective-permute-done.19.refs_0_), channel_id=1, source_target_pairs={{0,8},{8,0},{1,9},{9,1},{2,10},{10,2},{3,11},{11,3},{4,12},{12,4},... | collective-permute-start | bytes 1179656 | tf_op jit(solution)/shard_map/ppermute | solution.py:343
  113.4 5.8 %collective-permute-start.22 = (bf16[256,384]{1,0:T(8,128)(2,1)S(1)}, bf16[256,384]{1,0:T(8,128)(2,1)S(1)}, u32[]{:S(2)}, u32[]{:S(2)}) collective-permute-start(bf16[256,384]{1,0:T(8,128)(2,1)S(1)} %slice.50), channel_id=1, source_target_pairs={{0,1},{1,2},{2,3},{3,0},{4,5},{5,6},{6,7},{7,4},{8,9},{9,10},{10,1... | collective-permute-start | bytes 589832 | tf_op jit(solution)/shard_map/ppermute | solution.py:32
  113.7 5.6 %collective-permute-start.23 = (bf16[256,384]{1,0:T(8,128)(2,1)S(1)}, bf16[256,384]{1,0:T(8,128)(2,1)S(1)}, u32[]{:S(2)}, u32[]{:S(2)}) collective-permute-start(bf16[256,384]{1,0:T(8,128)(2,1)S(1)} %slice.51), channel_id=1, source_target_pairs={{0,3},{1,0},{2,1},{3,2},{4,7},{5,4},{6,5},{7,6},{8,11},{9,8},{10,9... | collective-permute-start | bytes 589832 | tf_op jit(solution)/shard_map/ppermute | solution.py:33
  117.0 3.9 %collective-permute-start.25 = (bf16[512,384]{1,0:T(8,128)(2,1)S(1)}, bf16[512,384]{1,0:T(8,128)(2,1)S(1)}, u32[]{:S(2)}, u32[]{:S(2)}) collective-permute-start(bf16[512,384]{1,0:T(8,128)(2,1)S(1)} %collective-permute-done.20.refs_1_), channel_id=1, source_target_pairs={{0,8},{8,0},{1,9},{9,1},{2,10},{10,2},{3,11},{11,3},{4,12},{12,4},... | collective-permute-start | bytes 1179656 | tf_op jit(solution)/shard_map/ppermute | solution.py:343
  117.1 3.9 %collective-permute-start.26 = (bf16[512,384]{1,0:T(8,128)(2,1)S(1)}, bf16[512,384]{1,0:T(8,128)(2,1)S(1)}, u32[]{:S(2)}, u32[]{:S(2)}) collective-permute-start(bf16[512,384]{1,0:T(8,128)(2,1)S(1)} %collective-permute-done.21.refs_2_), channel_id=1, source_target_pairs={{0,8},{8,0},{1,9},{9,1},{2,10},{10,2},{3,11},{11,3},{4,12},{12,4},... | collective-permute-start | bytes 1179656 | tf_op jit(solution)/shard_map/ppermute | solution.py:343
  119.2 1.4 collective-permute-start.27
  119.3 1.7 collective-permute-start.28
  132.5 0.8 copy-start.3
  190.0 9.2 %collective-permute-start.33 = (bf16[96,768]{1,0:T(8,128)(2,1)}, bf16[96,768]{1,0:T(8,128)(2,1)S(1)}, u32[]{:S(2)}, u32[]{:S(2)}) collective-permute-start(bf16[96,768]{1,0:T(8,128)(2,1)} %get-tuple-element.56), channel_id=1, source_target_pairs={{0,0},{4,8},{8,4},{12,12},{1,1},{5,9},{9,5},{13,13},{2,2},{6,10},{... | collective-permute-start | bytes 442376 | tf_op jit(solution)/shard_map/ppermute | solution.py:339
  193.8 5.3 %collective-permute-start.34 = (bf16[96,192]{1,0:T(8,128)(2,1)}, bf16[96,192]{1,0:T(8,128)(2,1)S(1)}, u32[]{:S(2)}, u32[]{:S(2)}) collective-permute-start(bf16[96,192]{1,0:T(8,128)(2,1)} %get-tuple-element.57), channel_id=1, source_target_pairs={{0,64},{4,72},{8,68},{12,76},{64,0},{68,8},{72,4},{76,12},{1,65},{... | collective-permute-start | bytes 110600 | tf_op jit(solution)/shard_map/ppermute | solution.py:395
  200.2 19.1 %all-to-all-start.1 = ((bf16[8,96,576]{2,1,0:T(8,128)(2,1)}), bf16[8,96,576]{2,1,0:T(8,128)(2,1)S(1)}, u32[]{:S(2)}, u32[]{:S(2)}) async-start(bf16[8,96,576]{2,1,0:T(8,128)(2,1)} %broadcast_in_dim.55), calls=%async_computation.2 | async-start | bytes 1966080 | tf_op jit(solution)/shard_map/all_to_all | solution.py:400
  204.3 8.0 %collective-permute-start.36 = (bf16[2,96,192]{2,1,0:T(8,128)(2,1)S(1)}, bf16[2,96,192]{2,1,0:T(8,128)(2,1)S(1)}, u32[]{:S(2)}, u32[]{:S(2)}) collective-permute-start(bf16[2,96,192]{2,1,0:T(8,128)(2,1)S(1)} %get-tuple-element.70), channel_id=1, source_target_pairs={{0,16},{16,32},{32,48},{48,0},{1,17},{17,33},{33,49},{49,1},{2,18}... | collective-permute-start | bytes 221192 | tf_op jit(solution)/shard_map/ppermute | solution.py:399
  204.4 8.0 %collective-permute-start.37 = (bf16[2,96,192]{2,1,0:T(8,128)(2,1)S(1)}, bf16[2,96,192]{2,1,0:T(8,128)(2,1)S(1)}, u32[]{:S(2)}, u32[]{:S(2)}) collective-permute-start(bf16[2,96,192]{2,1,0:T(8,128)(2,1)S(1)} %get-tuple-element.70), channel_id=1, source_target_pairs={{0,32},{16,48},{32,0},{48,16},{1,33},{17,49},{33,1},{49,17},{2,34}... | collective-permute-start | bytes 221192 | tf_op jit(solution)/shard_map/ppermute | solution.py:399
  206.2 6.1 %collective-permute-start.38 = (bf16[2,96,192]{2,1,0:T(8,128)(2,1)S(1)}, bf16[2,96,192]{2,1,0:T(8,128)(2,1)S(1)}, u32[]{:S(2)}, u32[]{:S(2)}) collective-permute-start(bf16[2,96,192]{2,1,0:T(8,128)(2,1)S(1)} %get-tuple-element.70), channel_id=1, source_target_pairs={{0,48},{16,0},{32,16},{48,32},{1,49},{17,1},{33,17},{49,33},{2,50}... | collective-permute-start | bytes 221192 | tf_op jit(solution)/shard_map/ppermute | solution.py:399
  207.1 15.8 %collective-permute-start.35 = (bf16[128,1536]{1,0:T(8,128)(2,1)S(1)}, bf16[128,1536]{1,0:T(8,128)(2,1)S(1)}, u32[]{:S(2)}, u32[]{:S(2)}) collective-permute-start(bf16[128,1536]{1,0:T(8,128)(2,1)S(1)} %add_convert_fusion), channel_id=1, source_target_pairs={{0,0},{4,8},{8,4},{12,12},{1,1},{5,9},{9,5},{13,13},{2,2},{6,10},{... | collective-permute-start | bytes 1179656 | tf_op jit(solution)/shard_map/ppermute | solution.py:339
  212.4 2.6 %copy-start.5 = (bf16[4,2,96,192]{3,2,1,0:T(8,128)(2,1)}, bf16[4,2,96,192]{3,2,1,0:T(8,128)(2,1)S(1)}, u32[]{:S(2)}) copy-start(bf16[4,2,96,192]{3,2,1,0:T(8,128)(2,1)S(1)} %pad_maximum_fusion.2.own_ref) | copy-start | bytes 884740
  212.4 2.6 %collective-permute-start.39 = (bf16[4,2,96,192]{3,2,1,0:T(8,128)(2,1)S(1)}, bf16[4,2,96,192]{3,2,1,0:T(8,128)(2,1)S(1)}, u32[]{:S(2)}, u32[]{:S(2)}) collective-permute-start(bf16[4,2,96,192]{3,2,1,0:T(8,128)(2,1)S(1)} %pad_maximum_fusion.2.own_ref), channel_id=1, source_target_pairs={{0,8},{8,0},{1,9},{9,1},{2,10},{10,2},{3,11},{11,3},{4,12},{12,4},... | collective-permute-start | bytes 884744 | tf_op jit(solution)/shard_map/ppermute | solution.py:401
  215.0 0.8 copy-start.8
  219.3 1.0 copy-start.4
Sparse Core Ops, SparseCore 0:
  77.8 31.2 all-gather.1
  133.5 44.4 reduce-scatter.1

commit v6 on v5

--- a/solution.py
+++ b/solution.py
@@ -217,11 +217,8 @@
     dcat[:, HD : 2 * HD] = dk[...].T.astype(bf16)[:, :HD]
     dcat[:, 2 * HD : 3 * HD] = dv[...].T.astype(bf16)[:, :HD]
 
-    @pl.loop(0, 2)
-    def _(n):
-        lanes = pl.ds(pl.multiple_of(n * 768, 768), 768)
-        grads[lanes, :] = dot(normed_ref[:, lanes], dcat[...], TN)
-        outs[:, lanes] = dot(mixed_ref[...], cot_ref[:, lanes], TN)[:HD]
+    outs[...] = dot(mixed_ref[...], cot_ref[...], TN)[:HD]
+    grads[...] = dot(normed_ref[...], dcat[...], TN)
 
     for d in range(16):
         sent_ref[d, :, : 3 * HD] = grads[d * 96 : (d + 1) * 96, :].astype(bf16)

time: 231 us -> 230 us (level)
  no operation moved by 1% of the time
where the time goes in v6:
time: 230 us; the launch traced here: 229 us
  starting transfers between devices  62.3 us (27%)
  blocking collectives  50.1 us (22%)
  Pallas kernels  47.3 us (21%)
  waiting for transfers between devices  38.5 us (17%)
  between operations  14.6 us (6%)
  local copies, waits for them, and re-layouts  13.6 us (6%)
  other arithmetic  2.49 us (1%)
    all_to_all x1, blocking collectives, per_device(): lax.all_to_all(backward(qkv, cot, wo, normed, mixed), ('zh', 'y', 'zl'),...  38.1 us
    pallas_call x1, Pallas kernels, backward(): pl.pallas_call(backward_kernel, out_shape=jax.ShapeDtypeStruct((16, 96, 7...  14.2 us
    ppermute x3, waiting for transfers between devices, per_device(): zpieces = [lax.ppermute(ypieces, zring, ring(4, k)) for k in (1, -1, 2)]  13.5 us
    ppermute x4, starting transfers between devices, swap_axes(): return lax.ppermute(value, ('c', 'zl'), [(0, 0), (1, 2), (2, 1), (3, 3)])  13.2 us
    all_gather x1, blocking collectives, per_device(): head_w = lax.all_gather(later[128:].reshape(96, 768), 'y', axis=0)  12.1 us
    pallas_call x1, Pallas kernels, forward(): pl.pallas_call(forward_kernel, out_shape=(jax.ShapeDtypeStruct((TOKENS, D...  11.5 us
    pallas_call x1, Pallas kernels, conv_pool(): pl.pallas_call(conv_kernel, out_shape=jax.ShapeDtypeStruct((512, OUTC), b...  11.2 us
    ppermute x4, waiting for transfers between devices, swap_axes(): return lax.ppermute(value, ('c', 'zl'), [(0, 0), (1, 2), (2, 1), (3, 3)])  9.3 us
  transfers between devices with their start and end apart: 43, of which 12 were waited for; matrix products, arithmetic and copies ran while one was open for 4% of the time, Pallas kernels for 21%

profile of v6, /device:TPU:1, one launch (start us, length us, event | category | flops | bytes accessed | tf_op | source)
XLA Modules:
  0.0 229.0 jit_solution(12057344417309520068)
XLA Ops:
  7.3 1.1 reshape.354
  8.8 2.1 collective-permute-start
  10.9 2.5 %collective-permute-start.1 = (bf16[5,11,384]{2,1,0:T(8,128)(2,1)S(1)}, bf16[5,11,384]{2,1,0:T(8,128)(2,1)S(1)}, u32[]{:S(2)}, u32[]{:S(2)}) collective-permute-start(bf16[5,11,384]{2,1,0:T(8,128)(2,1)S(1)} %bitcast.66), channel_id=1, source_target_pairs={{0,2},{1,3},{2,0},{3,1},{4,6},{5,7},{6,4},{7,5},{8,10},{9,11},{10,... | collective-permute-start | bytes 126728 | tf_op jit(solution)/shard_map/ppermute | solution.py:357
  13.5 1.2 collective-permute-start.2
  14.7 0.8 select_bitcast_fusion
  15.5 1.7 collective-permute-start.6
  17.5 1.4 collective-permute-start.3
  18.9 2.6 %collective-permute-start.4 = (bf16[5,48,384]{2,1,0:T(8,128)(2,1)S(1)}, bf16[5,48,384]{2,1,0:T(8,128)(2,1)S(1)}, u32[]{:S(2)}, u32[]{:S(2)}) collective-permute-start(bf16[5,48,384]{2,1,0:T(8,128)(2,1)S(1)} %pad.4), channel_id=1, source_target_pairs={{0,32},{16,48},{32,0},{48,16},{1,33},{17,49},{33,1},{49,17},{2,34}... | collective-permute-start | bytes 552968 | tf_op jit(solution)/shard_map/ppermute | solution.py:367
  21.5 1.1 collective-permute-start.5
  22.8 2.6 %shard_map.94.refs_0_ = bf16[272,1536]{1,0:T(8,128)(2,1)S(1)} custom-call(bf16[256,1408]{1,0:T(8,128)(2,1)S(1)} %bitcast.52, bf16[16,1408]{1,0:T(8,128)(2,1)S(1)} %collective-permute-done.6.edge_ref, s32[1,1536]{1,0:T(1,128)S(1)} %compare_select_fusion.10.sources_ref), custom_call_target="tpu_custom_call" | custom-call | flops 1200000000 | bytes 1600000 | tf_op jit(solution)/shard_map/pallas_call | solution.py:325
  25.5 2.6 %collective-permute-done.4 = bf16[5,48,384]{2,1,0:T(8,128)(2,1)S(1)} collective-permute-done((bf16[5,48,384]{2,1,0:T(8,128)(2,1)S(1)}, bf16[5,48,384]{2,1,0:T(8,128)(2,1)S(1)}, u32[]{:S(2)}, u32[]{:S(2)}) %collective-permute-start.4) | collective-permute-done | bytes 184352 | tf_op jit(solution)/shard_map/ppermute | solution.py:367
  28.2 3.1 %collective-permute-start.10 = (bf16[4,5,48,384]{3,2,1,0:T(8,128)(2,1)S(1)}, bf16[4,5,48,384]{3,2,1,0:T(8,128)(2,1)S(1)}, u32[]{:S(2)}, u32[]{:S(2)}) collective-permute-start(bf16[4,5,48,384]{3,2,1,0:T(8,128)(2,1)S(1)} %pad_maximum_fusion.refs_5_), channel_id=1, source_target_pairs={{0,8},{8,0},{1,9},{9,1},{2,10},{10,2},{3,11},{11,3},{4,12},{12,4},... | collective-permute-start | bytes 2211848 | tf_op jit(solution)/shard_map/ppermute | solution.py:372
  31.6 2.4 %collective-permute-start.9 = (bf16[272,1536]{1,0:T(8,128)(2,1)S(1)}, bf16[272,1536]{1,0:T(8,128)(2,1)}, u32[]{:S(2)}, u32[]{:S(2)}) collective-permute-start(bf16[272,1536]{1,0:T(8,128)(2,1)S(1)} %shard_map.94.refs_0_), channel_id=1, source_target_pairs={{0,3},{1,0},{2,1},{3,2},{4,7},{5,4},{6,5},{7,6},{8,11},{9,8},{10,9... | collective-permute-start | bytes 2506760 | tf_op jit(solution)/shard_map/ppermute | solution.py:371
  33.9 1.3 collective-permute-start.7
  35.2 2.1 collective-permute-start.11
  37.8 2.3 %collective-permute-start.17 = (bf16[176,1536]{1,0:T(8,128)(2,1)S(1)}, bf16[176,1536]{1,0:T(8,128)(2,1)S(1)}, u32[]{:S(2)}, u32[]{:S(2)}) collective-permute-start(bf16[176,1536]{1,0:T(8,128)(2,1)S(1)} %pad_maximum_fusion.1), channel_id=1, source_target_pairs={{0,0},{4,8},{8,4},{12,12},{1,1},{5,9},{9,5},{13,13},{2,2},{6,10},{... | collective-permute-start | bytes 1622024 | tf_op jit(solution)/shard_map/ppermute | solution.py:336
  40.2 13.5 %collective-permute-done.7.refs_6_ = bf16[4,5,48,384]{3,2,1,0:T(8,128)(2,1)} collective-permute-done((bf16[4,5,48,384]{3,2,1,0:T(8,128)(2,1)S(1)}, bf16[4,5,48,384]{3,2,1,0:T(8,128)(2,1)}, u32[]{:S(2)}, u32[]{:S(2)}) %collective-permute-start.7) | collective-permute-done | bytes 737312 | tf_op jit(solution)/shard_map/ppermute | solution.py:370
  53.7 1.1 collective-permute-start.12
  54.8 1.8 collective-permute-start.16
  56.7 1.8 slice.39
  58.5 0.9 collective-permute-start.14
  59.4 1.8 slice.38
  61.2 1.7 collective-permute-done.17
  62.9 0.8 copy-done.6
  63.8 1.8 slice.49
  65.6 12.1 %all_gather.6.refs_11_ = bf16[4,96,768]{2,1,0:T(8,128)(2,1)S(1)} all-gather(bf16[1,96,768]{2,1,0:T(8,128)(2,1)S(1)} %all_gather_reshape.3), channel_id=1, replica_groups=mesh['zh'=2,'y'=4,'c'=2,'zl'=2,'x'=4] {'y'}, dimensions={0}, use_global_device_ids=true | all-gather | bytes 737280 | tf_op jit(solution)/shard_map/all_gather | solution.py:365
  77.7 0.6 collective-permute-start.18
  78.4 0.8 dynamic_slice.20
  79.2 1.0 collective-permute-start.29
  80.3 3.6 %collective-permute-start.30 = (bf16[4,96,768]{2,1,0:T(8,128)(2,1)S(1)}, bf16[4,96,768]{2,1,0:T(8,128)(2,1)S(1)}, u32[]{:S(2)}, u32[]{:S(2)}) collective-permute-start(bf16[4,96,768]{2,1,0:T(8,128)(2,1)S(1)} %all_gather.6.refs_11_), channel_id=1, source_target_pairs={{0,68},{4,0},{64,4},{68,64},{1,69},{5,1},{65,5},{69,65},{2,70},{6,... | collective-permute-start | bytes 1769480 | tf_op jit(solution)/shard_map/ppermute | solution.py:39
  83.9 11.2 %shard_map.95 = bf16[512,384]{1,0:T(8,128)(2,1)S(1)} custom-call(s32[4]{0:T(128)S(1)} %pad_add_fusion.pos_ref, bf16[272,1536]{1,0:T(8,128)(2,1)} %copy-done.2, bf16[272,1536]{1,0:T(8,128)(2,1)} %collective-permute-done.8.refs_1_, bf16[272,1536]{1,0:T(8,128)(2,1)} %collective-permute-done.9.refs_2_, bf16[128,1536]{1,0:T(8,128)(2,1)} %collective-permute-done.13.refs_3_, ...), custom_call_target="tpu_custom_call" | custom-call | flops 6000000000 | bytes 9000000 | tf_op jit(solution)/shard_map/pallas_call | solution.py:94
  95.1 1.9 collective-permute-start.19
  97.0 7.6 %collective-permute-done.19.refs_0_ = bf16[512,384]{1,0:T(8,128)(2,1)S(1)} collective-permute-done((bf16[512,384]{1,0:T(8,128)(2,1)S(1)}, bf16[512,384]{1,0:T(8,128)(2,1)S(1)}, u32[]{:S(2)}, u32[]{:S(2)}) %collective-permute-start.19) | collective-permute-done | bytes 393248 | tf_op jit(solution)/shard_map/ppermute | solution.py:336
  104.6 2.7 %collective-permute-start.21 = (bf16[512,384]{1,0:T(8,128)(2,1)S(1)}, bf16[512,384]{1,0:T(8,128)(2,1)S(1)}, u32[]{:S(2)}, u32[]{:S(2)}) collective-permute-start(bf16[512,384]{1,0:T(8,128)(2,1)S(1)} %collective-permute-done.19.refs_0_), channel_id=1, source_target_pairs={{0,3},{1,0},{2,1},{3,2},{4,7},{5,4},{6,5},{7,6},{8,11},{9,8},{10,9... | collective-permute-start | bytes 1179656 | tf_op jit(solution)/shard_map/ppermute | solution.py:39
  107.4 2.7 %collective-permute-start.32 = (bf16[2,96,768]{2,1,0:T(8,128)(2,1)S(1)}, bf16[2,96,768]{2,1,0:T(8,128)(2,1)S(1)}, u32[]{:S(2)}, u32[]{:S(2)}) collective-permute-start(bf16[2,96,768]{2,1,0:T(8,128)(2,1)S(1)} %slice.53), channel_id=1, source_target_pairs={{0,68},{4,0},{64,4},{68,64},{1,69},{5,1},{65,5},{69,65},{2,70},{6,... | collective-permute-start | bytes 884744 | tf_op jit(solution)/shard_map/ppermute | solution.py:33
  110.1 3.3 %collective-permute-done.20.refs_1_ = bf16[512,384]{1,0:T(8,128)(2,1)S(1)} collective-permute-done((bf16[512,384]{1,0:T(8,128)(2,1)S(1)}, bf16[512,384]{1,0:T(8,128)(2,1)S(1)}, u32[]{:S(2)}, u32[]{:S(2)}) %collective-permute-start.20) | collective-permute-done | bytes 393248 | tf_op jit(solution)/shard_map/ppermute | solution.py:38
  113.7 2.6 %collective-permute-start.23 = (bf16[256,384]{1,0:T(8,128)(2,1)S(1)}, bf16[256,384]{1,0:T(8,128)(2,1)S(1)}, u32[]{:S(2)}, u32[]{:S(2)}) collective-permute-start(bf16[256,384]{1,0:T(8,128)(2,1)S(1)} %slice.51), channel_id=1, source_target_pairs={{0,3},{1,0},{2,1},{3,2},{4,7},{5,4},{6,5},{7,6},{8,11},{9,8},{10,9... | collective-permute-start | bytes 589832 | tf_op jit(solution)/shard_map/ppermute | solution.py:33
  116.3 0.8 collective-permute-done.31.refs_14_
  117.1 0.5 collective-permute-start.26
  117.6 1.7 collective-permute-done.22.refs_3_
  119.3 0.5 collective-permute-start.28
  119.8 0.9 collective-permute-done.27.refs_8_
  121.0 11.5 %shard_map.96 = (bf16[1024,1536]{1,0:T(8,128)(2,1)}, bf16[3,1024,256]{2,1,0:T(8,128)(2,1)}, bf16[1024,256]{1,0:T(8,128)(2,1)S(1)}, bf16[1024,1536]{1,0:T(8,128)(...) custom-call(s32[4]{0:T(128)S(1)} %pad_add_fusion.pos_ref, ...), custom_call_target="tpu_custom_call" | custom-call | flops 4000000000 | bytes 16000000 | tf_op jit(solution)/shard_map/pallas_call | solution.py:173
  132.5 0.8 copy-done.3
  133.4 14.2 %shard_map.97 = bf16[16,96,768]{2,1,0:T(8,128)(2,1)} custom-call(bf16[3,1024,256]{2,1,0:T(8,128)(2,1)} %get-tuple-element.51.qkv_ref, bf16[1024,1536]{1,0:T(8,128)(2,1)} %all-gather.2.cloned.1.call-done.cot_ref, bf16[1536,256]{1,0:T(8,128)(2,1)} %get-tuple-element.53.wo, bf16[1024,1536]{1,0:T(8,128)(2,1)} %get-tuple-element.54.normed_ref, ...), custom_call_target="tpu_custom_call" | custom-call | flops 6000000000 | bytes 18000000 | tf_op jit(solution)/shard_map/pallas_call | solution.py:231
  147.7 38.1 %all_to_all.10.parts_ref = bf16[16,96,768]{2,1,0:T(8,128)(2,1)} all-to-all(bf16[16,96,768]{2,1,0:T(8,128)(2,1)} %shard_map.97), channel_id=1, replica_groups=mesh['zh'=2,'y'=4,'c'=2,'zl'=2,'x'=4] {'zh','y','zl'}, dimensions={0} | all-to-all | bytes 4718592 | tf_op jit(solution)/shard_map/all_to_all | solution.py:390
  185.7 2.7 %shard_map.98 = (bf16[96,768]{1,0:T(8,128)(2,1)}, bf16[96,192]{1,0:T(8,128)(2,1)}) custom-call(bf16[16,96,768]{2,1,0:T(8,128)(2,1)} %all_to_all.10.parts_ref), custom_call_target="tpu_custom_call" | custom-call | tf_op jit(solution)/shard_map/pallas_call | solution.py:257
  188.4 3.8 %collective-permute-start.33 = (bf16[96,768]{1,0:T(8,128)(2,1)}, bf16[96,768]{1,0:T(8,128)(2,1)S(1)}, u32[]{:S(2)}, u32[]{:S(2)}) collective-permute-start(bf16[96,768]{1,0:T(8,128)(2,1)} %get-tuple-element.56), channel_id=1, source_target_pairs={{0,0},{4,8},{8,4},{12,12},{1,1},{5,9},{9,5},{13,13},{2,2},{6,10},{... | collective-permute-start | bytes 442376 | tf_op jit(solution)/shard_map/ppermute | solution.py:336
  192.2 0.7 collective-permute-start.34
  192.9 1.1 add_convert_fusion
  194.0 3.6 %collective-permute-done.34 = bf16[96,192]{1,0:T(8,128)(2,1)S(1)} collective-permute-done((bf16[96,192]{1,0:T(8,128)(2,1)}, bf16[96,192]{1,0:T(8,128)(2,1)S(1)}, u32[]{:S(2)}, u32[]{:S(2)}) %collective-permute-start.34) | collective-permute-done | bytes 36896 | tf_op jit(solution)/shard_map/ppermute | solution.py:392
  197.6 1.0 broadcast_in_dim.55
  198.6 3.9 %all-to-all-start.1 = ((bf16[8,96,576]{2,1,0:T(8,128)(2,1)}), bf16[8,96,576]{2,1,0:T(8,128)(2,1)S(1)}, u32[]{:S(2)}, u32[]{:S(2)}) async-start(bf16[8,96,576]{2,1,0:T(8,128)(2,1)} %broadcast_in_dim.55), calls=%async_computation.2 | async-start | bytes 1966080 | tf_op jit(solution)/shard_map/all_to_all | solution.py:397
  202.8 1.9 collective-permute-start.37
  204.6 0.9 collective-permute-start.38
  205.6 5.1 %collective-permute-start.35 = (bf16[128,1536]{1,0:T(8,128)(2,1)S(1)}, bf16[128,1536]{1,0:T(8,128)(2,1)S(1)}, u32[]{:S(2)}, u32[]{:S(2)}) collective-permute-start(bf16[128,1536]{1,0:T(8,128)(2,1)S(1)} %add_convert_fusion), channel_id=1, source_target_pairs={{0,0},{4,8},{8,4},{12,12},{1,1},{5,9},{9,5},{13,13},{2,2},{6,10},{... | collective-permute-start | bytes 1179656 | tf_op jit(solution)/shard_map/ppermute | solution.py:336
  210.9 1.2 collective-permute-start.39
  212.1 1.3 collective-permute-done.39.other_ref
  213.5 0.7 copy-done.8
  214.2 2.3 %shard_map.100 = f32[192,1536]{1,0:T(8,128)} custom-call(s32[4]{0:T(128)} %copy-done.1, bf16[4,2,96,192]{3,2,1,0:T(8,128)(2,1)} %copy-done.5, bf16[4,2,96,192]{3,2,1,0:T(8,128)(2,1)} %copy-done.8), custom_call_target="tpu_custom_call" | custom-call | tf_op jit(solution)/shard_map/pallas_call | solution.py:293
  216.5 1.2 all-to-all-done.1.heads_ref
  217.7 1.0 copy-done.4
  218.7 2.6 %shard_map.99 = f32[3,96,1536]{2,1,0:T(8,128)} custom-call(bf16[8,96,576]{2,1,0:T(8,128)(2,1)} %copy-done.4), custom_call_target="tpu_custom_call" | custom-call | tf_op jit(solution)/shard_map/pallas_call | solution.py:272
  221.4 0.7 copy.45
  (99 shorter events, 3.1 us)
Async XLA Ops:
  7.2 15.6 %copy-start = (bf16[1,256,1408]{2,1,0:T(8,128)(2,1)S(1)}, bf16[1,256,1408]{2,1,0:T(8,128)(2,1)}, u32[]{:S(2)}) copy-start(bf16[1,256,1408]{2,1,0:T(8,128)(2,1)} %param.7) | copy-start | bytes 2162692
  7.2 126.2 %all-gather.2.cloned.1.call-start = ((), (), s32[]{:S(2)}) async-start(), calls=%async_computation.3 | async-start | bytes 3538944 | tf_op jit(solution)/shard_map/all_gather | solution.py:377
  8.8 8.5 %collective-permute-start = (bf16[5,11,384]{2,1,0:T(8,128)(2,1)S(1)}, bf16[5,11,384]{2,1,0:T(8,128)(2,1)S(1)}, u32[]{:S(2)}, u32[]{:S(2)}) collective-permute-start(bf16[5,11,384]{2,1,0:T(8,128)(2,1)S(1)} %bitcast.67), channel_id=1, source_target_pairs={{0,1},{1,2},{2,3},{3,0},{4,5},{5,6},{6,7},{7,4},{8,9},{9,10},{10,1... | collective-permute-start | bytes 126728 | tf_op jit(solution)/shard_map/ppermute | solution.py:357
  10.9 6.4 %collective-permute-start.1 = (bf16[5,11,384]{2,1,0:T(8,128)(2,1)S(1)}, bf16[5,11,384]{2,1,0:T(8,128)(2,1)S(1)}, u32[]{:S(2)}, u32[]{:S(2)}) collective-permute-start(bf16[5,11,384]{2,1,0:T(8,128)(2,1)S(1)} %bitcast.66), channel_id=1, source_target_pairs={{0,2},{1,3},{2,0},{3,1},{4,6},{5,7},{6,4},{7,5},{8,10},{9,11},{10,... | collective-permute-start | bytes 126728 | tf_op jit(solution)/shard_map/ppermute | solution.py:357
  13.5 3.9 %collective-permute-start.2 = (bf16[5,11,384]{2,1,0:T(8,128)(2,1)S(1)}, bf16[5,11,384]{2,1,0:T(8,128)(2,1)S(1)}, u32[]{:S(2)}, u32[]{:S(2)}) collective-permute-start(bf16[5,11,384]{2,1,0:T(8,128)(2,1)S(1)} %bitcast.65), channel_id=1, source_target_pairs={{0,3},{1,0},{2,1},{3,2},{4,7},{5,4},{6,5},{7,6},{8,11},{9,8},{10,9... | collective-permute-start | bytes 126728 | tf_op jit(solution)/shard_map/ppermute | solution.py:357
  15.5 7.3 %collective-permute-start.6 = (bf16[16,1408]{1,0:T(8,128)(2,1)S(1)}, bf16[16,1408]{1,0:T(8,128)(2,1)S(1)}, u32[]{:S(2)}, u32[]{:S(2)}) collective-permute-start(bf16[16,1408]{1,0:T(8,128)(2,1)S(1)} %select_bitcast_fusion), channel_id=1, source_target_pairs={{0,4},{4,0},{1,5},{5,1},{2,6},{6,2},{3,7},{7,3},{8,12},{12,8},{9,1... | collective-permute-start | bytes 135176 | tf_op jit(solution)/shard_map/ppermute | solution.py:349
  17.5 7.9 %collective-permute-start.3 = (bf16[5,48,384]{2,1,0:T(8,128)(2,1)S(1)}, bf16[5,48,384]{2,1,0:T(8,128)(2,1)S(1)}, u32[]{:S(2)}, u32[]{:S(2)}) collective-permute-start(bf16[5,48,384]{2,1,0:T(8,128)(2,1)S(1)} %pad.4), channel_id=1, source_target_pairs={{0,16},{16,32},{32,48},{48,0},{1,17},{17,33},{33,49},{49,1},{2,18}... | collective-permute-start | bytes 552968 | tf_op jit(solution)/shard_map/ppermute | solution.py:367
  18.9 9.1 %collective-permute-start.4 = (bf16[5,48,384]{2,1,0:T(8,128)(2,1)S(1)}, bf16[5,48,384]{2,1,0:T(8,128)(2,1)S(1)}, u32[]{:S(2)}, u32[]{:S(2)}) collective-permute-start(bf16[5,48,384]{2,1,0:T(8,128)(2,1)S(1)} %pad.4), channel_id=1, source_target_pairs={{0,32},{16,48},{32,0},{48,16},{1,33},{17,49},{33,1},{49,17},{2,34}... | collective-permute-start | bytes 552968 | tf_op jit(solution)/shard_map/ppermute | solution.py:367
  21.5 6.5 %collective-permute-start.5 = (bf16[5,48,384]{2,1,0:T(8,128)(2,1)S(1)}, bf16[5,48,384]{2,1,0:T(8,128)(2,1)S(1)}, u32[]{:S(2)}, u32[]{:S(2)}) collective-permute-start(bf16[5,48,384]{2,1,0:T(8,128)(2,1)S(1)} %pad.4), channel_id=1, source_target_pairs={{0,48},{16,0},{32,16},{48,32},{1,49},{17,1},{33,17},{49,33},{2,50}... | collective-permute-start | bytes 552968 | tf_op jit(solution)/shard_map/ppermute | solution.py:367
  22.8 14.5 %copy-start.10 = (bf16[96,3,192]{2,0,1:T(8,128)(2,1)S(1)}, bf16[96,3,192]{2,0,1:T(8,128)(2,1)}, u32[]{:S(2)}) copy-start(bf16[96,3,192]{2,0,1:T(8,128)(2,1)} %param.11) | copy-start | bytes 331780
  25.4 12.4 %copy-start.2 = (bf16[272,1536]{1,0:T(8,128)(2,1)}, bf16[272,1536]{1,0:T(8,128)(2,1)S(1)}, u32[]{:S(2)}) copy-start(bf16[272,1536]{1,0:T(8,128)(2,1)S(1)} %shard_map.94.refs_0_) | copy-start | bytes 2506756
  25.4 12.1 %copy-start.11 = (bf16[192,96]{1,0:T(8,128)(2,1)S(1)}, bf16[192,96]{1,0:T(8,128)(2,1)}, u32[]{:S(2)}) copy-start(bf16[192,96]{1,0:T(8,128)(2,1)} %param.12) | copy-start | bytes 110596
  25.4 12.3 %copy-start.7 = (bf16[1,128,1536]{2,1,0:T(8,128)(2,1)S(1)}, bf16[1,128,1536]{2,1,0:T(8,128)(2,1)}, u32[]{:S(2)}) copy-start(bf16[1,128,1536]{2,1,0:T(8,128)(2,1)} %param.13) | copy-start | bytes 1179652
  28.2 9.7 %collective-permute-start.10 = (bf16[4,5,48,384]{3,2,1,0:T(8,128)(2,1)S(1)}, bf16[4,5,48,384]{3,2,1,0:T(8,128)(2,1)S(1)}, u32[]{:S(2)}, u32[]{:S(2)}) collective-permute-start(bf16[4,5,48,384]{3,2,1,0:T(8,128)(2,1)S(1)} %pad_maximum_fusion.refs_5_), channel_id=1, source_target_pairs={{0,8},{8,0},{1,9},{9,1},{2,10},{10,2},{3,11},{11,3},{4,12},{12,4},... | collective-permute-start | bytes 2211848 | tf_op jit(solution)/shard_map/ppermute | solution.py:372
  31.3 25.4 %collective-permute-start.8 = (bf16[272,1536]{1,0:T(8,128)(2,1)S(1)}, bf16[272,1536]{1,0:T(8,128)(2,1)}, u32[]{:S(2)}, u32[]{:S(2)}) collective-permute-start(bf16[272,1536]{1,0:T(8,128)(2,1)S(1)} %shard_map.94.refs_0_), channel_id=1, source_target_pairs={{0,1},{1,2},{2,3},{3,0},{4,5},{5,6},{6,7},{7,4},{8,9},{9,10},{10,1... | collective-permute-start | bytes 2506760 | tf_op jit(solution)/shard_map/ppermute | solution.py:371
  31.6 25.0 %collective-permute-start.9 = (bf16[272,1536]{1,0:T(8,128)(2,1)S(1)}, bf16[272,1536]{1,0:T(8,128)(2,1)}, u32[]{:S(2)}, u32[]{:S(2)}) collective-permute-start(bf16[272,1536]{1,0:T(8,128)(2,1)S(1)} %shard_map.94.refs_0_), channel_id=1, source_target_pairs={{0,3},{1,0},{2,1},{3,2},{4,7},{5,4},{6,5},{7,6},{8,11},{9,8},{10,9... | collective-permute-start | bytes 2506760 | tf_op jit(solution)/shard_map/ppermute | solution.py:371
  33.9 19.8 %collective-permute-start.7 = (bf16[4,5,48,384]{3,2,1,0:T(8,128)(2,1)S(1)}, bf16[4,5,48,384]{3,2,1,0:T(8,128)(2,1)}, u32[]{:S(2)}, u32[]{:S(2)}) collective-permute-start(bf16[4,5,48,384]{3,2,1,0:T(8,128)(2,1)S(1)} %pad_maximum_fusion.refs_5_), channel_id=1, source_target_pairs={{0,4},{4,64},{64,68},{68,0},{1,5},{5,65},{65,69},{69,1},{2,6},{6,6... | collective-permute-start | bytes 2211848 | tf_op jit(solution)/shard_map/ppermute | solution.py:370
  35.2 19.5 %collective-permute-start.11 = (bf16[4,5,48,384]{3,2,1,0:T(8,128)(2,1)S(1)}, bf16[4,5,48,384]{3,2,1,0:T(8,128)(2,1)}, u32[]{:S(2)}, u32[]{:S(2)}) collective-permute-start(bf16[4,5,48,384]{3,2,1,0:T(8,128)(2,1)S(1)} %pad_maximum_fusion.refs_5_), channel_id=1, source_target_pairs={{0,68},{4,0},{64,4},{68,64},{1,69},{5,1},{65,5},{69,65},{2,70},{6,... | collective-permute-start | bytes 2211848 | tf_op jit(solution)/shard_map/ppermute | solution.py:370
  37.8 25.1 %collective-permute-start.17 = (bf16[176,1536]{1,0:T(8,128)(2,1)S(1)}, bf16[176,1536]{1,0:T(8,128)(2,1)S(1)}, u32[]{:S(2)}, u32[]{:S(2)}) collective-permute-start(bf16[176,1536]{1,0:T(8,128)(2,1)S(1)} %pad_maximum_fusion.1), channel_id=1, source_target_pairs={{0,0},{4,8},{8,4},{12,12},{1,1},{5,9},{9,5},{13,13},{2,2},{6,10},{... | collective-permute-start | bytes 1622024 | tf_op jit(solution)/shard_map/ppermute | solution.py:336
  53.7 23.9 %collective-permute-start.12 = (bf16[4,5,48,384]{3,2,1,0:T(8,128)(2,1)S(1)}, bf16[4,5,48,384]{3,2,1,0:T(8,128)(2,1)}, u32[]{:S(2)}, u32[]{:S(2)}) collective-permute-start(bf16[4,5,48,384]{3,2,1,0:T(8,128)(2,1)S(1)} %pad_maximum_fusion.refs_5_), channel_id=1, source_target_pairs={{0,64},{4,68},{64,0},{68,4},{1,65},{5,69},{65,1},{69,5},{2,66},{6,... | collective-permute-start | bytes 2211848 | tf_op jit(solution)/shard_map/ppermute | solution.py:370
  54.8 22.9 %collective-permute-start.16 = (bf16[4,5,48,384]{3,2,1,0:T(8,128)(2,1)}, bf16[4,5,48,384]{3,2,1,0:T(8,128)(2,1)}, u32[]{:S(2)}, u32[]{:S(2)}) collective-permute-start(bf16[4,5,48,384]{3,2,1,0:T(8,128)(2,1)} %collective-permute-done.11.refs_7_), channel_id=1, source_target_pairs={{0,8},{8,0},{1,9},{9,1},{2,10},{10,2},{3,11},{11,3},{4,12},{12,4},... | collective-permute-start | bytes 2211848 | tf_op jit(solution)/shard_map/ppermute | solution.py:340
  56.6 21.0 %collective-permute-start.15 = (bf16[4,5,48,384]{3,2,1,0:T(8,128)(2,1)}, bf16[4,5,48,384]{3,2,1,0:T(8,128)(2,1)S(1)}, u32[]{:S(2)}, u32[]{:S(2)}) collective-permute-start(bf16[4,5,48,384]{3,2,1,0:T(8,128)(2,1)} %collective-permute-done.7.refs_6_), channel_id=1, source_target_pairs={{0,8},{8,0},{1,9},{9,1},{2,10},{10,2},{3,11},{11,3},{4,12},{12,4},... | collective-permute-start | bytes 2211848 | tf_op jit(solution)/shard_map/ppermute | solution.py:340
  58.5 19.1 %collective-permute-start.14 = (bf16[144,1536]{1,0:T(8,128)(2,1)}, bf16[144,1536]{1,0:T(8,128)(2,1)S(1)}, u32[]{:S(2)}, u32[]{:S(2)}) collective-permute-start(bf16[144,1536]{1,0:T(8,128)(2,1)} %slice.39), channel_id=1, source_target_pairs={{0,3},{1,0},{2,1},{3,2},{4,7},{5,4},{6,5},{7,6},{8,11},{9,8},{10,9... | collective-permute-start | bytes 1327112 | tf_op jit(solution)/shard_map/ppermute | solution.py:33
  62.9 0.8 copy-start.6
  62.9 14.7 %collective-permute-start.13 = (bf16[128,1536]{1,0:T(8,128)(2,1)}, bf16[128,1536]{1,0:T(8,128)(2,1)}, u32[]{:S(2)}, u32[]{:S(2)}) collective-permute-start(bf16[128,1536]{1,0:T(8,128)(2,1)} %slice.38), channel_id=1, source_target_pairs={{0,1},{1,2},{2,3},{3,0},{4,5},{5,6},{6,7},{7,4},{8,9},{9,10},{10,1... | collective-permute-start | bytes 1179656 | tf_op jit(solution)/shard_map/ppermute | solution.py:32
  77.7 115.2 %reduce-scatter.2.cloned.1.call-start = ((), (), s32[]{:S(2)}) async-start(), calls=%async_computation.4 | async-start | bytes 3538944 | tf_op jit(solution)/shard_map/reduce_scatter | solution.py:388
  77.7 6.2 %collective-permute-start.18 = (bf16[4,5,48,384]{3,2,1,0:T(8,128)(2,1)}, bf16[4,5,48,384]{3,2,1,0:T(8,128)(2,1)}, u32[]{:S(2)}, u32[]{:S(2)}) collective-permute-start(bf16[4,5,48,384]{3,2,1,0:T(8,128)(2,1)} %collective-permute-done.12.refs_8_), channel_id=1, source_target_pairs={{0,8},{8,0},{1,9},{9,1},{2,10},{10,2},{3,11},{11,3},{4,12},{12,4},... | collective-permute-start | bytes 2211848 | tf_op jit(solution)/shard_map/ppermute | solution.py:340
  79.2 41.8 %copy-start.1 = (s32[4]{0:T(128)}, s32[4]{0:T(128)S(1)}, u32[]{:S(2)}) copy-start(s32[4]{0:T(128)S(1)} %pad_add_fusion.pos_ref) | copy-start | bytes 52
  79.2 28.0 %collective-permute-start.29 = (bf16[4,96,768]{2,1,0:T(8,128)(2,1)S(1)}, bf16[4,96,768]{2,1,0:T(8,128)(2,1)S(1)}, u32[]{:S(2)}, u32[]{:S(2)}) collective-permute-start(bf16[4,96,768]{2,1,0:T(8,128)(2,1)S(1)} %all_gather.6.refs_11_), channel_id=1, source_target_pairs={{0,4},{4,64},{64,68},{68,0},{1,5},{5,65},{65,69},{69,1},{2,6},{6,6... | collective-permute-start | bytes 1769480 | tf_op jit(solution)/shard_map/ppermute | solution.py:38
  80.3 27.1 %collective-permute-start.30 = (bf16[4,96,768]{2,1,0:T(8,128)(2,1)S(1)}, bf16[4,96,768]{2,1,0:T(8,128)(2,1)S(1)}, u32[]{:S(2)}, u32[]{:S(2)}) collective-permute-start(bf16[4,96,768]{2,1,0:T(8,128)(2,1)S(1)} %all_gather.6.refs_11_), channel_id=1, source_target_pairs={{0,68},{4,0},{64,4},{68,64},{1,69},{5,1},{65,5},{69,65},{2,70},{6,... | collective-permute-start | bytes 1769480 | tf_op jit(solution)/shard_map/ppermute | solution.py:39
  95.1 24.7 %copy-start.12 = (f32[1536]{0:T(1024)S(1)}, f32[1536]{0:T(1024)}, u32[]{:S(2)}) copy-start(f32[1536]{0:T(1024)} %param.10) | copy-start | bytes 18436
  95.1 9.5 %collective-permute-start.19 = (bf16[512,384]{1,0:T(8,128)(2,1)S(1)}, bf16[512,384]{1,0:T(8,128)(2,1)S(1)}, u32[]{:S(2)}, u32[]{:S(2)}) collective-permute-start(bf16[512,384]{1,0:T(8,128)(2,1)S(1)} %shard_map.95), channel_id=1, source_target_pairs={{0,0},{4,8},{8,4},{12,12},{1,1},{5,9},{9,5},{13,13},{2,2},{6,10},{... | collective-permute-start | bytes 1179656 | tf_op jit(solution)/shard_map/ppermute | solution.py:336
  104.6 8.8 %collective-permute-start.20 = (bf16[512,384]{1,0:T(8,128)(2,1)S(1)}, bf16[512,384]{1,0:T(8,128)(2,1)S(1)}, u32[]{:S(2)}, u32[]{:S(2)}) collective-permute-start(bf16[512,384]{1,0:T(8,128)(2,1)S(1)} %collective-permute-done.19.refs_0_), channel_id=1, source_target_pairs={{0,1},{1,2},{2,3},{3,0},{4,5},{5,6},{6,7},{7,4},{8,9},{9,10},{10,1... | collective-permute-start | bytes 1179656 | tf_op jit(solution)/shard_map/ppermute | solution.py:38
  104.6 9.1 %collective-permute-start.21 = (bf16[512,384]{1,0:T(8,128)(2,1)S(1)}, bf16[512,384]{1,0:T(8,128)(2,1)S(1)}, u32[]{:S(2)}, u32[]{:S(2)}) collective-permute-start(bf16[512,384]{1,0:T(8,128)(2,1)S(1)} %collective-permute-done.19.refs_0_), channel_id=1, source_target_pairs={{0,3},{1,0},{2,1},{3,2},{4,7},{5,4},{6,5},{7,6},{8,11},{9,8},{10,9... | collective-permute-start | bytes 1179656 | tf_op jit(solution)/shard_map/ppermute | solution.py:39
  107.3 9.8 %collective-permute-start.31 = (bf16[2,96,768]{2,1,0:T(8,128)(2,1)S(1)}, bf16[2,96,768]{2,1,0:T(8,128)(2,1)S(1)}, u32[]{:S(2)}, u32[]{:S(2)}) collective-permute-start(bf16[2,96,768]{2,1,0:T(8,128)(2,1)S(1)} %slice.52), channel_id=1, source_target_pairs={{0,4},{4,64},{64,68},{68,0},{1,5},{5,65},{65,69},{69,1},{2,6},{6,6... | collective-permute-start | bytes 884744 | tf_op jit(solution)/shard_map/ppermute | solution.py:32
  107.4 13.6 %copy-start.9 = (bf16[4,96,768]{2,1,0:T(8,128)(2,1)}, bf16[4,96,768]{2,1,0:T(8,128)(2,1)S(1)}, u32[]{:S(2)}) copy-start(bf16[4,96,768]{2,1,0:T(8,128)(2,1)S(1)} %collective-permute-done.30.refs_13_) | copy-start | bytes 1769476
  107.4 9.6 %collective-permute-start.32 = (bf16[2,96,768]{2,1,0:T(8,128)(2,1)S(1)}, bf16[2,96,768]{2,1,0:T(8,128)(2,1)S(1)}, u32[]{:S(2)}, u32[]{:S(2)}) collective-permute-start(bf16[2,96,768]{2,1,0:T(8,128)(2,1)S(1)} %slice.53), channel_id=1, source_target_pairs={{0,68},{4,0},{64,4},{68,64},{1,69},{5,1},{65,5},{69,65},{2,70},{6,... | collective-permute-start | bytes 884744 | tf_op jit(solution)/shard_map/ppermute | solution.py:33
  110.1 9.6 %collective-permute-start.24 = (bf16[512,384]{1,0:T(8,128)(2,1)S(1)}, bf16[512,384]{1,0:T(8,128)(2,1)S(1)}, u32[]{:S(2)}, u32[]{:S(2)}) collective-permute-start(bf16[512,384]{1,0:T(8,128)(2,1)S(1)} %collective-permute-done.19.refs_0_), channel_id=1, source_target_pairs={{0,8},{8,0},{1,9},{9,1},{2,10},{10,2},{3,11},{11,3},{4,12},{12,4},... | collective-permute-start | bytes 1179656 | tf_op jit(solution)/shard_map/ppermute | solution.py:340
  113.4 5.8 %collective-permute-start.22 = (bf16[256,384]{1,0:T(8,128)(2,1)S(1)}, bf16[256,384]{1,0:T(8,128)(2,1)S(1)}, u32[]{:S(2)}, u32[]{:S(2)}) collective-permute-start(bf16[256,384]{1,0:T(8,128)(2,1)S(1)} %slice.50), channel_id=1, source_target_pairs={{0,1},{1,2},{2,3},{3,0},{4,5},{5,6},{6,7},{7,4},{8,9},{9,10},{10,1... | collective-permute-start | bytes 589832 | tf_op jit(solution)/shard_map/ppermute | solution.py:32
  113.7 5.6 %collective-permute-start.23 = (bf16[256,384]{1,0:T(8,128)(2,1)S(1)}, bf16[256,384]{1,0:T(8,128)(2,1)S(1)}, u32[]{:S(2)}, u32[]{:S(2)}) collective-permute-start(bf16[256,384]{1,0:T(8,128)(2,1)S(1)} %slice.51), channel_id=1, source_target_pairs={{0,3},{1,0},{2,1},{3,2},{4,7},{5,4},{6,5},{7,6},{8,11},{9,8},{10,9... | collective-permute-start | bytes 589832 | tf_op jit(solution)/shard_map/ppermute | solution.py:33
  117.0 3.9 %collective-permute-start.25 = (bf16[512,384]{1,0:T(8,128)(2,1)S(1)}, bf16[512,384]{1,0:T(8,128)(2,1)S(1)}, u32[]{:S(2)}, u32[]{:S(2)}) collective-permute-start(bf16[512,384]{1,0:T(8,128)(2,1)S(1)} %collective-permute-done.20.refs_1_), channel_id=1, source_target_pairs={{0,8},{8,0},{1,9},{9,1},{2,10},{10,2},{3,11},{11,3},{4,12},{12,4},... | collective-permute-start | bytes 1179656 | tf_op jit(solution)/shard_map/ppermute | solution.py:340
  117.1 3.9 %collective-permute-start.26 = (bf16[512,384]{1,0:T(8,128)(2,1)S(1)}, bf16[512,384]{1,0:T(8,128)(2,1)S(1)}, u32[]{:S(2)}, u32[]{:S(2)}) collective-permute-start(bf16[512,384]{1,0:T(8,128)(2,1)S(1)} %collective-permute-done.21.refs_2_), channel_id=1, source_target_pairs={{0,8},{8,0},{1,9},{9,1},{2,10},{10,2},{3,11},{11,3},{4,12},{12,4},... | collective-permute-start | bytes 1179656 | tf_op jit(solution)/shard_map/ppermute | solution.py:340
  119.2 1.4 collective-permute-start.27
  119.3 1.7 collective-permute-start.28
  132.5 0.8 copy-start.3
  188.4 9.2 %collective-permute-start.33 = (bf16[96,768]{1,0:T(8,128)(2,1)}, bf16[96,768]{1,0:T(8,128)(2,1)S(1)}, u32[]{:S(2)}, u32[]{:S(2)}) collective-permute-start(bf16[96,768]{1,0:T(8,128)(2,1)} %get-tuple-element.56), channel_id=1, source_target_pairs={{0,0},{4,8},{8,4},{12,12},{1,1},{5,9},{9,5},{13,13},{2,2},{6,10},{... | collective-permute-start | bytes 442376 | tf_op jit(solution)/shard_map/ppermute | solution.py:336
  192.2 5.3 %collective-permute-start.34 = (bf16[96,192]{1,0:T(8,128)(2,1)}, bf16[96,192]{1,0:T(8,128)(2,1)S(1)}, u32[]{:S(2)}, u32[]{:S(2)}) collective-permute-start(bf16[96,192]{1,0:T(8,128)(2,1)} %get-tuple-element.57), channel_id=1, source_target_pairs={{0,64},{4,72},{8,68},{12,76},{64,0},{68,8},{72,4},{76,12},{1,65},{... | collective-permute-start | bytes 110600 | tf_op jit(solution)/shard_map/ppermute | solution.py:392
  198.6 19.1 %all-to-all-start.1 = ((bf16[8,96,576]{2,1,0:T(8,128)(2,1)}), bf16[8,96,576]{2,1,0:T(8,128)(2,1)S(1)}, u32[]{:S(2)}, u32[]{:S(2)}) async-start(bf16[8,96,576]{2,1,0:T(8,128)(2,1)} %broadcast_in_dim.55), calls=%async_computation.2 | async-start | bytes 1966080 | tf_op jit(solution)/shard_map/all_to_all | solution.py:397
  202.7 8.0 %collective-permute-start.36 = (bf16[2,96,192]{2,1,0:T(8,128)(2,1)S(1)}, bf16[2,96,192]{2,1,0:T(8,128)(2,1)S(1)}, u32[]{:S(2)}, u32[]{:S(2)}) collective-permute-start(bf16[2,96,192]{2,1,0:T(8,128)(2,1)S(1)} %get-tuple-element.70), channel_id=1, source_target_pairs={{0,16},{16,32},{32,48},{48,0},{1,17},{17,33},{33,49},{49,1},{2,18}... | collective-permute-start | bytes 221192 | tf_op jit(solution)/shard_map/ppermute | solution.py:396
  202.8 8.0 %collective-permute-start.37 = (bf16[2,96,192]{2,1,0:T(8,128)(2,1)S(1)}, bf16[2,96,192]{2,1,0:T(8,128)(2,1)S(1)}, u32[]{:S(2)}, u32[]{:S(2)}) collective-permute-start(bf16[2,96,192]{2,1,0:T(8,128)(2,1)S(1)} %get-tuple-element.70), channel_id=1, source_target_pairs={{0,32},{16,48},{32,0},{48,16},{1,33},{17,49},{33,1},{49,17},{2,34}... | collective-permute-start | bytes 221192 | tf_op jit(solution)/shard_map/ppermute | solution.py:396
  204.6 6.1 %collective-permute-start.38 = (bf16[2,96,192]{2,1,0:T(8,128)(2,1)S(1)}, bf16[2,96,192]{2,1,0:T(8,128)(2,1)S(1)}, u32[]{:S(2)}, u32[]{:S(2)}) collective-permute-start(bf16[2,96,192]{2,1,0:T(8,128)(2,1)S(1)} %get-tuple-element.70), channel_id=1, source_target_pairs={{0,48},{16,0},{32,16},{48,32},{1,49},{17,1},{33,17},{49,33},{2,50}... | collective-permute-start | bytes 221192 | tf_op jit(solution)/shard_map/ppermute | solution.py:396
  205.6 15.8 %collective-permute-start.35 = (bf16[128,1536]{1,0:T(8,128)(2,1)S(1)}, bf16[128,1536]{1,0:T(8,128)(2,1)S(1)}, u32[]{:S(2)}, u32[]{:S(2)}) collective-permute-start(bf16[128,1536]{1,0:T(8,128)(2,1)S(1)} %add_convert_fusion), channel_id=1, source_target_pairs={{0,0},{4,8},{8,4},{12,12},{1,1},{5,9},{9,5},{13,13},{2,2},{6,10},{... | collective-permute-start | bytes 1179656 | tf_op jit(solution)/shard_map/ppermute | solution.py:336
  210.8 2.6 %copy-start.5 = (bf16[4,2,96,192]{3,2,1,0:T(8,128)(2,1)}, bf16[4,2,96,192]{3,2,1,0:T(8,128)(2,1)S(1)}, u32[]{:S(2)}) copy-start(bf16[4,2,96,192]{3,2,1,0:T(8,128)(2,1)S(1)} %pad_maximum_fusion.2.own_ref) | copy-start | bytes 884740
  210.9 2.6 %collective-permute-start.39 = (bf16[4,2,96,192]{3,2,1,0:T(8,128)(2,1)S(1)}, bf16[4,2,96,192]{3,2,1,0:T(8,128)(2,1)S(1)}, u32[]{:S(2)}, u32[]{:S(2)}) collective-permute-start(bf16[4,2,96,192]{3,2,1,0:T(8,128)(2,1)S(1)} %pad_maximum_fusion.2.own_ref), channel_id=1, source_target_pairs={{0,8},{8,0},{1,9},{9,1},{2,10},{10,2},{3,11},{11,3},{4,12},{12,4},... | collective-permute-start | bytes 884744 | tf_op jit(solution)/shard_map/ppermute | solution.py:398
  213.4 0.8 copy-start.8
  217.7 1.0 copy-start.4
Sparse Core Ops, SparseCore 0:
  77.8 31.2 all-gather.1
  133.5 44.4 reduce-scatter.1
